TPU v7x, 128 devices: a whole 4x4x4 slice. The times are simulated.
128 devices in a mesh: mem: 16 (over y, x_lo, core), space: 8 (over z, x_hi).
Axes of the slice: x: 4 (x_hi: 2, x_lo: 2; x = x_hi * 2 + x_lo), y: 4, z: 4, core: 2. Of those that a mesh axis runs over, the one named last changes fastest.
Arguments:
- members: bfloat16 [16, 137, 128, 1024], P('mem', None, 'space'), may hold values from -6 to 6
- increment: bfloat16 [137, 128, 1024], P(None, 'space'), may hold values from -6 to 6
- vertical: bfloat16 [137, 137], replicated, may hold values from -1 to 2
- spectral_weights: float32 [128, 1024], P(None, 'space'), may hold values from 0.05 to 1
- tile_rows: int32 [128], replicated, may hold values from 0 to 127, each once
Outputs:
- covariance_product: bfloat16 [137, 128, 1024], P(None, 'space')
All inputs are finite; a program needn't handle non-finite values.
Results may differ from a plain program's by a relative error of at most 0.02.
Values may be sent and summed in bfloat16 or wider, within the bound.
No kernel may reach another device: no remote copies, remote signals or barrier semaphores. Data moves between devices by JAX's collectives and lax.ppermute only.
A program may use at most 128 MiB of HBM per device.

v0:
```python
import math

import jax
import jax.numpy as jnp
from jax import lax
from jax.sharding import PartitionSpec as P


def wave_table(length, positions):
    ranks = lax.broadcasted_iota(jnp.int32, (length, positions.shape[0]), 0)
    middle = length // 2
    wavenumber = jnp.where(ranks <= middle, ranks, ranks - middle)
    phases = wavenumber * positions[None, :] % length
    angles = phases.astype(jnp.float32) * (2.0 * math.pi / length)
    edge = 1.0 / math.sqrt(length)
    inner = math.sqrt(2.0 / length)
    values = jnp.where(
        ranks == 0,
        edge,
        jnp.where(
            ranks < middle,
            inner * jnp.cos(angles),
            jnp.where(ranks == middle, edge * jnp.cos(angles), inner * jnp.sin(angles)),
        ),
    )
    return values.astype(jnp.bfloat16)


def shards(members, increment, vertical, spectral_weights, tile_rows):
    levels, stored_rows, columns = increment.shape
    member = members[0]
    product = (member.astype(jnp.float32) * increment.astype(jnp.float32)).astype(jnp.bfloat16)
    localized = jnp.dot(
        vertical, product.reshape(levels, -1), preferred_element_type=jnp.float32
    ).astype(jnp.bfloat16)
    basis_x = wave_table(columns, jnp.arange(columns, dtype=jnp.int32))
    coeffs = jnp.dot(localized.reshape(-1, columns), basis_x.T, preferred_element_type=jnp.float32)
    coeffs = coeffs.astype(jnp.bfloat16).reshape(levels, stored_rows, columns)
    basis_y = wave_table(tile_rows.shape[0], tile_rows)
    spectral = jnp.einsum(
        "kp,lpq->lkq",
        basis_y,
        lax.all_to_all(coeffs, "space", split_axis=2, concat_axis=1, tiled=True),
        preferred_element_type=jnp.float32,
    )
    damped = (spectral * spectral_weights[None]).astype(jnp.bfloat16)
    returned = jnp.einsum(
        "kp,lkq->lpq", basis_y, damped, preferred_element_type=jnp.float32
    ).astype(jnp.bfloat16)
    returned = lax.all_to_all(returned, "space", split_axis=1, concat_axis=2, tiled=True)
    gridded = jnp.dot(returned.reshape(-1, columns), basis_x, preferred_element_type=jnp.float32)
    contribution = member.astype(jnp.float32) * gridded.reshape(levels, stored_rows, columns)
    summed = lax.psum(contribution.astype(jnp.bfloat16), "mem")
    return summed


def solution(mesh):
    return jax.shard_map(
        shards,
        mesh=mesh,
        in_specs=(
            P("mem", None, "space", None),
            P(None, "space", None),
            P(),
            P(None, "space"),
            P(),
        ),
        out_specs=P(None, "space", None),
        check_vma=False,
    )
```

profile of v0, /device:TPU:1, one launch (start us, length us, event | category | flops | bytes accessed | tf_op | source)
XLA Modules:
  0.0 432.8 jit_solution(3536717331158586347)
XLA Ops:
  6.5 0.0 copy-start
  6.6 6.0 %fusion.1 = bf16[137,16,1024]{2,1,0:T(8,128)(2,1)S(1)} fusion(bf16[137,16,1024]{2,1,0:T(8,128)(2,1)} %param.6, bf16[1,137,16,1024]{3,2,1,0:T(8,128)(2,1)} %param.5), kind=kLoop, calls=%fused_computation.4 | loop fusion | flops 8978432 | bytes 13467648 | tf_op jit(solution)/shard_map/convert_element_type | solution.py:32
  12.6 0.9 pad
  13.5 3.4 copy.36
  16.9 0.0 copy-done
  16.9 3.5 fusion
  20.5 8.2 %reshape.19 = bf16[2192,1024]{1,0:T(8,128)(2,1)} reshape(bf16[137,16384]{1,0:T(8,128)(2,1)} %fusion) | data formatting | bytes 8978432 | tf_op jit(solution)/shard_map/reshape | solution.py:37
  28.6 19.8 %select_convert_fusion.6 = bf16[1024,1024]{1,0:T(8,128)(2,1)S(1)} fusion(s32[1024]{0:T(1024)S(1)} %iota_add_fusion, pred[1024]{0:T(1024)(128)(4,1)S(1)} %get-tuple-element.5, pred[1024]{0:T(1024)(128)(4,1)S(1)} %get-tuple-element.6, pred[1024]{0:T(1024)(128)(4,1)S(1)} %get-tuple-element.7, pred[1024]{0:T(1024)(128)(4,1)S(1)} %get-tuple-element.8), kind=kLoop, calls=%fused_computation.18.clone.1.clone.1 | loop fusion | flops 23068672 | bytes 2105344 | tf_op jit(solution)/shard_map/dot_general | solution.py:37
  48.5 8.8 %convolution_convert_fusion.1 = bf16[2192,1024]{1,0:T(8,128)(2,1)} fusion(bf16[2192,1024]{1,0:T(8,128)(2,1)} %reshape.19, bf16[1024,1024]{1,0:T(8,128)(2,1)S(1)} %select_convert_fusion.6), kind=kOutput, calls=%fused_computation.11 | convolution fusion | flops 4599201792 | bytes 11075584 | tf_op jit(solution)/shard_map/dot_general | solution.py:37
  57.2 13.2 %copy.24 = bf16[137,16,1024]{0,1,2:T(8,128)(2,1)} copy(bf16[137,16,1024]{2,1,0:T(8,128)(2,1)} %bitcast.52) | data formatting | bytes 8978432 | tf_op jit(solution)/shard_map/reshape | solution.py:38
  70.4 0.0 copy-start.2
  70.4 8.5 %all-to-all-start = ((bf16[137,16,1024]{0,1,2:T(8,128)(2,1)}), bf16[137,16,1024]{0,1,2:T(8,128)(2,1)}, u32[]{:S(2)}, u32[]{:S(2)}) async-start(bf16[137,16,1024]{0,1,2:T(8,128)(2,1)} %copy.24), calls=%async_computation | async-start | bytes 16777216 | tf_op jit(solution)/shard_map/all_to_all | solution.py:43
  78.9 0.0 copy-done.2
  78.9 0.1 copy.28
  79.0 94.9 %all-to-all-done = bf16[137,16,1024]{0,1,2:T(8,128)(2,1)} async-done(((bf16[137,16,1024]{0,1,2:T(8,128)(2,1)}), bf16[137,16,1024]{0,1,2:T(8,128)(2,1)}, u32[]{:S(2)}, u32[]{:S(2)}) %all-to-all-start) | async-done | bytes 4489248 | tf_op jit(solution)/shard_map/all_to_all | solution.py:43
  173.9 0.0 copy-start.3
  173.9 12.4 %copy.26 = bf16[137,8,16,128]{3,2,1,0:T(8,128)(2,1)} copy(bf16[137,8,16,128]{0,2,3,1:T(8,128)(2,1)} %bitcast.6) | data formatting | bytes 8978432 | tf_op jit(solution)/shard_map/all_to_all | solution.py:43
  186.4 0.0 copy-done.3
  186.4 7.5 %convert_bitcast_fusion = bf16[137,128,128]{1,2,0:T(8,128)(2,1)} fusion(f32[128,128]{0,1:T(8,128)S(1)} %copy.28, bf16[137,128,128]{2,1,0:T(8,128)(2,1)} %bitcast.51, s32[128]{0:T(128)S(1)} %copy-done.3, s32[128]{0:T(128)S(1)} %iota_add_fusion.1, pred[128]{0:T(512)(128)(4,1)S(1)} %get-tuple-element.10, pred[128]{0:T(512)(128)(4,1)S(1)} %get-tuple-element.9, ...), kind=kOutput, calls=%fused_computation.13 | convolution fusion | flops 1156694016 | bytes 9045504 | tf_op jit(solution)/shard_map/kp,lkq->lpq/dot_general | solution.py:47
  193.9 6.9 %copy.29 = bf16[137,128,128]{2,0,1:T(8,128)(2,1)} copy(bf16[137,128,128]{1,2,0:T(8,128)(2,1)} %convert_bitcast_fusion) | data formatting | bytes 8978432 | tf_op jit(solution)/shard_map/convert_element_type | solution.py:49
  200.7 4.6 %all-to-all-start.1 = ((bf16[137,128,128]{2,0,1:T(8,128)(2,1)}), bf16[137,128,128]{2,0,1:T(8,128)(2,1)}, u32[]{:S(2)}, u32[]{:S(2)}) async-start(bf16[137,128,128]{2,0,1:T(8,128)(2,1)} %copy.29), calls=%async_computation.1 | async-start | bytes 9437184 | tf_op jit(solution)/shard_map/all_to_all | solution.py:50
  205.4 0.0 all-reduce.2.cloned.1.call-start
  205.4 20.1 %fusion.78 = bf16[1024,1024,1]{1,0,2:T(8,128)(2,1)S(1)} fusion(pred[1024]{0:T(1024)(128)(4,1)S(1)} %get-tuple-element.5, s32[1024]{0:T(1024)S(1)} %iota_add_fusion, pred[1024]{0:T(1024)(128)(4,1)S(1)} %get-tuple-element.6, pred[1024]{0:T(1024)(128)(4,1)S(1)} %get-tuple-element.7, pred[1024]{0:T(1024)(128)(4,1)S(1)} %get-tuple-element.8), kind=kLoop, calls=%fused_computation.20.clone.1 | loop fusion | flops 23068672 | bytes 2105344 | tf_op jit(solution)/shard_map/dot_general | solution.py:51
  225.6 34.5 %all-to-all-done.1 = bf16[137,128,128]{2,0,1:T(8,128)(2,1)} async-done(((bf16[137,128,128]{2,0,1:T(8,128)(2,1)}), bf16[137,128,128]{2,0,1:T(8,128)(2,1)}, u32[]{:S(2)}, u32[]{:S(2)}) %all-to-all-start.1) | async-done | bytes 4489248 | tf_op jit(solution)/shard_map/all_to_all | solution.py:50
  260.0 7.4 %copy.31 = bf16[137,16,8,128]{3,2,1,0:T(8,128)(2,1)} copy(bf16[137,16,8,128]{3,0,1,2:T(8,128)(2,1)} %bitcast.13) | data formatting | bytes 8978432 | tf_op jit(solution)/shard_map/all_to_all | solution.py:50
  267.4 8.0 %dot_general.21 = bf16[137,16,1024]{2,1,0:T(8,128)(2,1)} reshape(bf16[137,16,8,128]{3,2,1,0:T(8,128)(2,1)} %copy.31) | data formatting | bytes 8978432 | tf_op jit(solution)/shard_map/dot_general | solution.py:51
  275.4 9.4 %fusion.2 = bf16[137,16,1024]{2,1,0:T(8,128)(2,1)} fusion(bf16[1,137,16,1024]{3,2,1,0:T(8,128)(2,1)} %param.5, bf16[137,16,1024]{2,1,0:T(8,128)(2,1)} %dot_general.21, bf16[1024,1024,1]{1,0,2:T(8,128)(2,1)S(1)} %fusion.78), kind=kOutput, calls=%fused_computation.5 | convolution fusion | flops 4603691008 | bytes 15564800 | tf_op jit(solution)/shard_map/dot_general | solution.py:51
  284.7 0.0 all-reduce.2.cloned.1.call-update
  284.8 0.0 copy-start.1
  284.8 135.9 %all-reduce.2.cloned.1.call-done = bf16[137,16,1024]{2,1,0:T(8,128)(2,1)} async-done(((bf16[137,16,1024]{2,1,0:T(8,128)(2,1)}), bf16[137,16,1024]{2,1,0:T(8,128)(2,1)}) %all-reduce.2.cloned.1.call-update) | async-done | bytes 4489232 | tf_op jit(solution)/shard_map/psum | solution.py:53
  420.7 5.3 %copy.38 = bf16[137,16,1024]{2,1,0:T(8,128)(2,1)} copy(bf16[137,16,1024]{2,1,0:T(8,128)(2,1)} %all-reduce.2.cloned.1.call-done) | data formatting | bytes 8978432
  425.9 0.0 copy-done.1
  (6 shorter events, 0.0 us)
Async XLA Ops:
  6.5 10.4 %copy-start = (bf16[137,137]{1,0:T(8,128)(2,1)S(1)}, bf16[137,137]{1,0:T(8,128)(2,1)}, u32[]{:S(2)}) copy-start(bf16[137,137]{1,0:T(8,128)(2,1)} %param.7) | copy-start | bytes 112618
  70.4 8.5 %copy-start.2 = (f32[128,128]{1,0:T(8,128)S(1)}, f32[128,128]{1,0:T(8,128)}, u32[]{:S(2)}) copy-start(f32[128,128]{1,0:T(8,128)} %param.8) | copy-start | bytes 196612
  70.4 103.5 %all-to-all-start = ((bf16[137,16,1024]{0,1,2:T(8,128)(2,1)}), bf16[137,16,1024]{0,1,2:T(8,128)(2,1)}, u32[]{:S(2)}, u32[]{:S(2)}) async-start(bf16[137,16,1024]{0,1,2:T(8,128)(2,1)} %copy.24), calls=%async_computation | async-start | bytes 16777216 | tf_op jit(solution)/shard_map/all_to_all | solution.py:43
  173.9 12.4 %copy-start.3 = (s32[128]{0:T(128)S(1)}, s32[128]{0:T(128)}, u32[]{:S(2)}) copy-start(s32[128]{0:T(128)} %param.9) | copy-start | bytes 1540
  200.7 59.3 %all-to-all-start.1 = ((bf16[137,128,128]{2,0,1:T(8,128)(2,1)}), bf16[137,128,128]{2,0,1:T(8,128)(2,1)}, u32[]{:S(2)}, u32[]{:S(2)}) async-start(bf16[137,128,128]{2,0,1:T(8,128)(2,1)} %copy.29), calls=%async_computation.1 | async-start | bytes 9437184 | tf_op jit(solution)/shard_map/all_to_all | solution.py:50
  205.4 215.3 %all-reduce.2.cloned.1.call-start = ((), (), s32[]{:S(2)}) async-start(), calls=%async_computation.2 | async-start | bytes 8978432 | tf_op jit(solution)/shard_map/psum | solution.py:53
  284.8 141.2 %copy-start.1 = (bf16[137,137]{1,0:T(8,128)(2,1)S(1)}, bf16[137,137]{1,0:T(8,128)(2,1)}, u32[]{:S(2)}) copy-start(bf16[137,137]{1,0:T(8,128)(2,1)} %param.7) | copy-start | bytes 112618
Sparse Core Ops, SparseCore 0:
  284.9 135.7 all-reduce.1
where the time goes:
time: 435 us; the launch traced here: 433 us
  waiting for transfers between devices  265 us (61%)
  local copies, waits for them, and re-layouts  65.7 us (15%)
  other arithmetic  46 us (11%)
  matrix products  29.1 us (7%)
  between operations  13.5 us (3%)
  starting transfers between devices  13.1 us (3%)
    psum x1, waiting for transfers between devices, shards(): summed = lax.psum(contribution.astype(jnp.bfloat16), 'mem')  136 us
    all_to_all x1, waiting for transfers between devices, shards(): lax.all_to_all(coeffs, 'space', split_axis=2, concat_axis=1, tiled=True)  94.9 us
    all_to_all x1, waiting for transfers between devices, shards(): lax.all_to_all(returned, 'space', split_axis=1, concat_axis=2, tiled=True)  34.5 us
    dot_general x1, other arithmetic, shards(): jnp.dot(returned.reshape(-1, columns), basis_x, preferred_element_type=jn...  20.1 us
    dot_general x1, other arithmetic, shards(): jnp.dot(localized.reshape(-1, columns), basis_x.T, preferred_element_type...  19.8 us
    reshape x1, local copies, waits for them, and re-layouts, shards(): coeffs = coeffs.astype(jnp.bfloat16).reshape(levels, stored_rows, columns)  13.2 us
    all_to_all x1, local copies, waits for them, and re-layouts, shards(): lax.all_to_all(coeffs, 'space', split_axis=2, concat_axis=1, tiled=True)  12.4 us
    unnamed x12, local copies, waits for them, and re-layouts  9.72 us
  transfers between devices with their start and end apart: 3, of which 3 were waited for; matrix products, arithmetic and copies ran while one was open for 5% of the time, Pallas kernels for 0%

commit v1 on v0

v1 whole, which is shorter than its diff:
```python
import functools
import math

import jax
import jax.numpy as jnp
import numpy as np
from jax import lax
from jax.experimental import pallas as pl
from jax.experimental.pallas import tpu as pltpu
from jax.sharding import PartitionSpec as P

BF16, F32 = jnp.bfloat16, jnp.float32
LANES = 128
VMEM_LIMIT = 48 * 1024 * 1024
CHUNKS = (32, 32, 32, 32, 9)
STEP = 8


def wave_table(length):
    ranks = np.arange(length)[:, None]
    middle = length // 2
    wavenumber = np.where(ranks <= middle, ranks, ranks - middle)
    angles = wavenumber * np.arange(length)[None, :] % length * (2.0 * math.pi / length)
    edge, inner = 1.0 / math.sqrt(length), math.sqrt(2.0 / length)
    values = np.where(
        ranks == 0,
        edge,
        np.where(
            ranks < middle,
            inner * np.cos(angles),
            np.where(ranks == middle, edge * np.cos(angles), inner * np.sin(angles)),
        ),
    )
    return values.astype(jnp.bfloat16)


def params():
    return pltpu.CompilerParams(vmem_limit_bytes=VMEM_LIMIT)


def mix_kernel(vertical_ref, member_ref, increment_ref, *refs):
    *out_refs, rows, mixed = refs
    levels, stored, _ = member_ref.shape
    tiles = rows.shape[0]
    product = member_ref[...].astype(F32) * increment_ref[...].astype(F32)
    product = product.reshape(levels * stored, tiles * LANES)
    for t in range(tiles):
        rows[t] = product[:, t * LANES : (t + 1) * LANES]
    vertical = vertical_ref[...]
    for p in range(stored):
        at = pl.ds(p, levels, stride=stored)
        block = jnp.concatenate([rows[t, at, :] for t in range(tiles)], axis=1).astype(BF16)
        block = jnp.dot(vertical, block, preferred_element_type=F32)
        for t in range(tiles):
            mixed[t, at, :] = block[:, t * LANES : (t + 1) * LANES]
    start = 0
    for out_ref in out_refs:
        size = out_ref.shape[0]
        for t in range(tiles):
            part = mixed[t, start * stored : (start + size) * stored, :].astype(BF16)
            out_ref[:, :, t * LANES : (t + 1) * LANES] = part.reshape(size, stored, LANES)
        start += size


def mix(vertical, member, increment, chunks, width=256):
    levels, stored, columns = member.shape
    wide = lambda size: pl.BlockSpec((size, stored, width), lambda i: (0, 0, i))
    return pl.pallas_call(
        mix_kernel,
        grid=(columns // width,),
        in_specs=[pl.BlockSpec((levels, levels), lambda i: (0, 0)), wide(levels), wide(levels)],
        out_specs=[wide(size) for size in chunks],
        out_shape=[jax.ShapeDtypeStruct((size, stored, columns), BF16) for size in chunks],
        scratch_shapes=[pltpu.VMEM((width // LANES, levels * stored, LANES), F32)] * 2,
        compiler_params=params(),
        name="mix",
    )(vertical, member, increment)


def forward_kernel(basis_ref, x_ref, out_ref):
    size, stored, columns = x_ref.shape
    parts, _, _, width = out_ref.shape
    coeffs = jnp.dot(
        x_ref[...].reshape(size * stored, columns), basis_ref[...], preferred_element_type=F32
    ).astype(BF16)
    for s in range(parts):
        out_ref[s] = coeffs[:, s * width : (s + 1) * width].reshape(size, stored, width)


def forward(basis, x, parts):
    size, stored, columns = x.shape
    width = columns // parts
    step = min(STEP, size)
    return pl.pallas_call(
        forward_kernel,
        grid=(pl.cdiv(size, step),),
        in_specs=[
            pl.BlockSpec((columns, columns), lambda i: (0, 0)),
            pl.BlockSpec((step, stored, columns), lambda i: (i, 0, 0)),
        ],
        out_specs=pl.BlockSpec((parts, step, stored, width), lambda i: (0, i, 0, 0)),
        out_shape=jax.ShapeDtypeStruct((parts, size, stored, width), BF16),
        compiler_params=params(),
        cost_estimate=pl.CostEstimate(
            flops=2 * size * stored * columns * columns,
            bytes_accessed=2 * (2 * x.size + basis.size),
            transcendentals=0,
        ),
        name="forward",
    )(basis, x)


def filter_kernel(basis_ref, basis_t_ref, weights_ref, x_ref, out_ref):
    parts, step, stored, width = x_ref.shape
    rows = parts * stored
    x = jnp.concatenate([x_ref[:, l].reshape(rows, width) for l in range(step)], axis=1)
    spectral = jnp.dot(basis_ref[...], x, preferred_element_type=F32)
    weights = jnp.concatenate([weights_ref[...]] * step, axis=1)
    damped = (spectral * weights).astype(BF16)
    back = jnp.dot(basis_t_ref[...], damped, preferred_element_type=F32).astype(BF16)
    for l in range(step):
        out_ref[:, l] = back[:, l * width : (l + 1) * width].reshape(parts, stored, width)


def filter_rows(basis, basis_t, weights, x):
    parts, size, stored, width = x.shape
    rows = parts * stored
    step = min(STEP, size)
    whole = lambda a: pl.BlockSpec(a.shape, lambda i: (0, 0))
    block = pl.BlockSpec((parts, step, stored, width), lambda i: (0, i, 0, 0))
    return pl.pallas_call(
        filter_kernel,
        grid=(pl.cdiv(size, step),),
        in_specs=[whole(basis), whole(basis_t), whole(weights), block],
        out_specs=block,
        out_shape=jax.ShapeDtypeStruct(x.shape, BF16),
        compiler_params=params(),
        cost_estimate=pl.CostEstimate(
            flops=4 * rows * x.size, bytes_accessed=4 * x.size, transcendentals=0
        ),
        name="filter",
    )(basis, basis_t, weights, x)


def backward_kernel(basis_ref, member_ref, x_ref, out_ref):
    parts, step, stored, width = x_ref.shape
    x = jnp.concatenate([x_ref[s].reshape(step * stored, width) for s in range(parts)], axis=1)
    gridded = jnp.dot(x, basis_ref[...], preferred_element_type=F32)
    member = member_ref[...].astype(F32).reshape(gridded.shape)
    out_ref[...] = (member * gridded).astype(BF16).reshape(out_ref.shape)


def backward(basis, member, x, start):
    parts, size, stored, width = x.shape
    columns = parts * width
    step = min(STEP, size)
    first = start // step
    assert first * step == start
    return pl.pallas_call(
        backward_kernel,
        grid=(pl.cdiv(size, step),),
        in_specs=[
            pl.BlockSpec((columns, columns), lambda i: (0, 0)),
            pl.BlockSpec((step, stored, columns), lambda i: (first + i, 0, 0)),
            pl.BlockSpec((parts, step, stored, width), lambda i: (0, i, 0, 0)),
        ],
        out_specs=pl.BlockSpec((step, stored, columns), lambda i: (i, 0, 0)),
        out_shape=jax.ShapeDtypeStruct((size, stored, columns), BF16),
        compiler_params=params(),
        cost_estimate=pl.CostEstimate(
            flops=2 * x.size * columns,
            bytes_accessed=2 * (3 * x.size + basis.size),
            transcendentals=0,
        ),
        name="backward",
    )(basis, member, x)


def shards(spaces, mems, members, increment, vertical, spectral_weights, tile_rows):
    levels, stored, columns = increment.shape
    member = members[0]
    table = wave_table(columns)
    basis_x, basis_xt = jnp.asarray(table), jnp.asarray(np.ascontiguousarray(table.T))
    rows = tile_rows.shape[0]
    chosen = (lax.broadcasted_iota(jnp.int32, (rows, rows), 0) == tile_rows[None, :]).astype(BF16)
    basis_y = jnp.dot(jnp.asarray(wave_table(rows)), chosen, preferred_element_type=F32).astype(BF16)
    basis_yt = basis_y.T
    localized = mix(vertical, member, increment, CHUNKS)
    out = jnp.zeros((levels, stored, columns), BF16)
    start = 0
    for chunk in localized:
        size = chunk.shape[0]
        coeffs = forward(basis_xt, chunk, spaces)
        coeffs = lax.all_to_all(coeffs, "space", 0, 0, tiled=True)
        returned = filter_rows(basis_y, basis_yt, spectral_weights, coeffs)
        returned = lax.all_to_all(returned, "space", 0, 0, tiled=True)
        part = backward(basis_x, member, returned, start)
        full = -(-size // 16) * 16
        part = jnp.pad(part, ((0, full - size), (0, 0), (0, 0)))
        part = lax.psum_scatter(
            part.reshape(full * stored, columns), "mem", scatter_dimension=0, tiled=True
        )
        part = lax.all_gather(part, "mem", axis=0, tiled=True)
        part = part[: size * stored].reshape(size, stored, columns)
        out = lax.dynamic_update_slice(out, part, (start, 0, 0))
        start += size
    return out


def solution(mesh):
    return jax.shard_map(
        functools.partial(shards, mesh.shape["space"], mesh.shape["mem"]),
        mesh=mesh,
        in_specs=(
            P("mem", None, "space", None),
            P(None, "space", None),
            P(),
            P(None, "space"),
            P(),
        ),
        out_specs=P(None, "space", None),
        check_vma=False,
    )
```

time: 435 us -> 536 us (1.23)
  blocking collectives: 0 us -> 178 us
  local copies, waits for them, and re-layouts: 65.7 us -> 18.2 us
  other arithmetic: 46 us -> 0 us
  Pallas kernels: 0 us -> 45.2 us
  matrix products: 29.1 us -> 0.19 us
  waiting for transfers between devices: 265 us -> 271 us
    all_to_all x0 -> x9, blocking collectives: none -> 155 us  [the longest x5 86.4 us: shards(): returned = lax.all_to_all(returned, 'space', 0, 0, tiled=True)]
    reduce_scatter x0 -> x5, waiting for transfers between devices: none -> 146 us  [shards(): lax.psum_scatter(part.reshape(full * stored, columns), 'mem', scatter_dim...]
    psum x1 -> x0, waiting for transfers between devices: 136 us -> none  [shards(): summed = lax.psum(contribution.astype(jnp.bfloat16), 'mem')]
    all_to_all x2 -> x1, waiting for transfers between devices: 129 us -> 15.6 us  [shards(): coeffs = lax.all_to_all(coeffs, 'space', 0, 0, tiled=True)]
    all_gather x0 -> x4, waiting for transfers between devices: none -> 108 us  [shards(): part = lax.all_gather(part, 'mem', axis=0, tiled=True)]
    pallas_call x0 -> x16, Pallas kernels: none -> 45.2 us  [the longest x5 19.2 us: backward(): pl.pallas_call(backward_kernel, grid=(pl.cdiv(size, step),), in_specs=[pl...]
    dot_general x2 -> x0, other arithmetic: 40 us -> none  [the longest x1 20.1 us: shards(): jnp.dot(returned.reshape(-1, columns), basis_x, preferred_element_type=jn...]
    dot_general x4 -> x1, matrix products: 29.1 us -> 0.19 us  [shards(): jnp.dot(jnp.asarray(wave_table(rows)), chosen, preferred_element_type=F32)]
  transfers between devices with their start and end apart: 3 -> 10, of which waited for: 3 -> 8; matrix products, arithmetic and copies ran while one was open for 5% -> 2% of each run, Pallas kernels for 0% -> 5%
where the time goes in v1:
time: 536 us; the launch traced here: 535 us
  waiting for transfers between devices  271 us (51%)
  blocking collectives  178 us (33%)
  Pallas kernels  45.2 us (8%)
  local copies, waits for them, and re-layouts  18.2 us (3%)
  between operations  13.5 us (3%)
  starting transfers between devices  8.69 us (2%)
    reduce_scatter x5, waiting for transfers between devices, shards(): lax.psum_scatter(part.reshape(full * stored, columns), 'mem', scatter_dim...  146 us
    all_gather x4, waiting for transfers between devices, shards(): part = lax.all_gather(part, 'mem', axis=0, tiled=True)  108 us
    all_to_all x5, blocking collectives, shards(): returned = lax.all_to_all(returned, 'space', 0, 0, tiled=True)  86.4 us
    all_to_all x4, blocking collectives, shards(): coeffs = lax.all_to_all(coeffs, 'space', 0, 0, tiled=True)  68.9 us
    all_gather x1, blocking collectives, shards(): part = lax.all_gather(part, 'mem', axis=0, tiled=True)  23.1 us
    pallas_call x5, Pallas kernels, backward(): pl.pallas_call(backward_kernel, grid=(pl.cdiv(size, step),), in_specs=[pl...  19.2 us
    all_to_all x1, waiting for transfers between devices, shards(): coeffs = lax.all_to_all(coeffs, 'space', 0, 0, tiled=True)  15.6 us
    dynamic_update_slice x5, local copies, waits for them, and re-layouts, shards(): out = lax.dynamic_update_slice(out, part, (start, 0, 0))  11.6 us
  transfers between devices with their start and end apart: 10, of which 8 were waited for; matrix products, arithmetic and copies ran while one was open for 2% of the time, Pallas kernels for 5%

profile of v1, /device:TPU:1, one launch (start us, length us, event | category | flops | bytes accessed | tf_op | source)
XLA Modules:
  0.0 535.2 jit_solution(7868512600821161606)
XLA Ops:
  6.5 0.9 copy-done.16
  7.4 9.7 %mix.1 = (bf16[32,16,1024]{2,1,0:T(8,128)(2,1)S(1)}, bf16[32,16,1024]{2,1,0:T(8,128)(2,1)S(1)}, bf16[32,16,1024]{2,1,0:T(8,128)(2,1)S(1)}, bf16[32,16,1024]{2,1,0:T(8,128)(2,1)S(1)}, bf16[9,16,1024]{2,1,0:T(8,128)(2,1)S(1)}) custom-call(bf16[137,137]{1,0:T(8,128)(2,1)S(1)} %copy-done.16, bf16[137,16,1024]{2,1,0:T(8,128)(2,1)} %bitcast.14, ...), custom_call_target="tpu_custom_call" | custom-call | tf_op jit(solution)/shard_map/mix/pallas_call | solution.py:68
  17.2 1.0 copy-done.8
  18.2 1.0 copy-done.10
  19.1 1.0 copy-done.12
  20.1 0.7 copy-done.14
  20.9 1.9 forward.5
  22.8 1.0 copy-done.6
  23.7 8.3 %all-to-all-start = ((bf16[8,32,16,128]{3,2,1,0:T(8,128)(2,1)}), bf16[8,32,16,128]{3,2,1,0:T(8,128)(2,1)S(1)}, u32[]{:S(2)}, u32[]{:S(2)}) async-start(bf16[8,32,16,128]{3,2,1,0:T(8,128)(2,1)} %copy-done.6), calls=%async_computation | async-start | bytes 2097152 | tf_op jit(solution)/shard_map/all_to_all | solution.py:194
  32.4 15.6 %all-to-all-done.x_ref = bf16[8,32,16,128]{3,2,1,0:T(8,128)(2,1)S(1)} async-done(((bf16[8,32,16,128]{3,2,1,0:T(8,128)(2,1)}), bf16[8,32,16,128]{3,2,1,0:T(8,128)(2,1)S(1)}, u32[]{:S(2)}, u32[]{:S(2)}) %all-to-all-start) | async-done | bytes 1048608 | tf_op jit(solution)/shard_map/all_to_all | solution.py:194
  48.1 1.7 filter.5
  49.8 20.1 %all_to_all.50.x_ref = bf16[8,32,16,128]{3,2,1,0:T(8,128)(2,1)S(1)} all-to-all(bf16[8,32,16,128]{3,2,1,0:T(8,128)(2,1)S(1)} %filter.5), channel_id=1, replica_groups=mesh['mem'=16,'space'=8] {'space'}, dimensions={0} | all-to-all | bytes 2097152 | tf_op jit(solution)/shard_map/all_to_all | solution.py:196
  69.9 4.3 backward.5
  74.3 1.9 forward.6
  76.2 21.1 %all_to_all.51.x_ref = bf16[8,32,16,128]{3,2,1,0:T(8,128)(2,1)S(1)} all-to-all(bf16[8,32,16,128]{3,2,1,0:T(8,128)(2,1)S(1)} %forward.6), channel_id=1, replica_groups=mesh['mem'=16,'space'=8] {'space'}, dimensions={0} | all-to-all | bytes 2097152 | tf_op jit(solution)/shard_map/all_to_all | solution.py:194
  97.3 1.7 filter.6
  99.0 20.7 %all_to_all.52.x_ref = bf16[8,32,16,128]{3,2,1,0:T(8,128)(2,1)S(1)} all-to-all(bf16[8,32,16,128]{3,2,1,0:T(8,128)(2,1)S(1)} %filter.6), channel_id=1, replica_groups=mesh['mem'=16,'space'=8] {'space'}, dimensions={0} | all-to-all | bytes 2097152 | tf_op jit(solution)/shard_map/all_to_all | solution.py:196
  119.7 4.3 backward.6
  124.1 1.9 forward.7
  126.0 19.1 %all_to_all.53.x_ref = bf16[8,32,16,128]{3,2,1,0:T(8,128)(2,1)S(1)} all-to-all(bf16[8,32,16,128]{3,2,1,0:T(8,128)(2,1)S(1)} %forward.7), channel_id=1, replica_groups=mesh['mem'=16,'space'=8] {'space'}, dimensions={0} | all-to-all | bytes 2097152 | tf_op jit(solution)/shard_map/all_to_all | solution.py:194
  145.1 1.7 filter.7
  146.8 19.7 %all_to_all.54.x_ref = bf16[8,32,16,128]{3,2,1,0:T(8,128)(2,1)S(1)} all-to-all(bf16[8,32,16,128]{3,2,1,0:T(8,128)(2,1)S(1)} %filter.7), channel_id=1, replica_groups=mesh['mem'=16,'space'=8] {'space'}, dimensions={0} | all-to-all | bytes 2097152 | tf_op jit(solution)/shard_map/all_to_all | solution.py:196
  166.5 4.3 backward.7
  170.9 1.9 forward.8
  172.8 18.0 %all_to_all.55.x_ref = bf16[8,32,16,128]{3,2,1,0:T(8,128)(2,1)S(1)} all-to-all(bf16[8,32,16,128]{3,2,1,0:T(8,128)(2,1)S(1)} %forward.8), channel_id=1, replica_groups=mesh['mem'=16,'space'=8] {'space'}, dimensions={0} | all-to-all | bytes 2097152 | tf_op jit(solution)/shard_map/all_to_all | solution.py:194
  190.9 1.7 filter.8
  192.5 15.5 %all_to_all.56.x_ref = bf16[8,32,16,128]{3,2,1,0:T(8,128)(2,1)S(1)} all-to-all(bf16[8,32,16,128]{3,2,1,0:T(8,128)(2,1)S(1)} %filter.8), channel_id=1, replica_groups=mesh['mem'=16,'space'=8] {'space'}, dimensions={0} | all-to-all | bytes 2097152 | tf_op jit(solution)/shard_map/all_to_all | solution.py:196
  208.0 4.3 backward.8
  212.4 1.0 forward.9
  213.4 10.7 %all_to_all.57.x_ref = bf16[8,9,16,128]{3,2,1,0:T(8,128)(2,1)S(1)} all-to-all(bf16[8,9,16,128]{3,2,1,0:T(8,128)(2,1)S(1)} %forward.9), channel_id=1, replica_groups=mesh['mem'=16,'space'=8] {'space'}, dimensions={0} | all-to-all | bytes 589824 | tf_op jit(solution)/shard_map/all_to_all | solution.py:194
  224.1 1.0 filter.9
  225.1 10.4 %all_to_all.58.x_ref = bf16[8,9,16,128]{3,2,1,0:T(8,128)(2,1)S(1)} all-to-all(bf16[8,9,16,128]{3,2,1,0:T(8,128)(2,1)S(1)} %filter.9), channel_id=1, replica_groups=mesh['mem'=16,'space'=8] {'space'}, dimensions={0} | all-to-all | bytes 589824 | tf_op jit(solution)/shard_map/all_to_all | solution.py:196
  235.5 1.9 backward.9
  237.4 0.9 pad.5
  239.0 0.7 all-gather.7.cloned.1.call-update
  239.7 23.1 %reduce-scatter.10.cloned.1.call-done = bf16[32,1024]{1,0:T(8,128)(2,1)} async-done(((bf16[512,1024]{1,0:T(8,128)(2,1)}), bf16[32,1024]{1,0:T(8,128)(2,1)}) %reduce-scatter.10.cloned.1.call-update) | async-done | bytes 65552 | tf_op jit(solution)/shard_map/reduce_scatter | solution.py:200
  262.9 61.6 %reduce-scatter.12.cloned.1.call-done = bf16[32,1024]{1,0:T(8,128)(2,1)} async-done(((bf16[512,1024]{1,0:T(8,128)(2,1)}), bf16[32,1024]{1,0:T(8,128)(2,1)}) %reduce-scatter.12.cloned.1.call-update) | async-done | bytes 65552 | tf_op jit(solution)/shard_map/reduce_scatter | solution.py:200
  324.6 61.2 %reduce-scatter.14.cloned.1.call-done = bf16[16,1024]{1,0:T(8,128)(2,1)} async-done(((bf16[256,1024]{1,0:T(8,128)(2,1)}), bf16[16,1024]{1,0:T(8,128)(2,1)}) %reduce-scatter.14.cloned.1.call-update) | async-done | bytes 32784 | tf_op jit(solution)/shard_map/reduce_scatter | solution.py:200
  385.8 23.1 %all_gather.19 = bf16[256,1024]{1,0:T(8,128)(2,1)S(1)} all-gather(bf16[16,1024]{1,0:T(8,128)(2,1)} %reduce-scatter.14.cloned.1.call-done), channel_id=1, replica_groups=mesh['mem'=16,'space'=8] {'mem'}, dimensions={0}, use_global_device_ids=true | all-gather | bytes 557056 | tf_op jit(solution)/shard_map/all_gather | solution.py:203
  408.9 13.4 %all-gather.5.cloned.1.call-done = bf16[512,1024]{1,0:T(8,128)(2,1)} async-done(((bf16[32,1024]{1,0:T(8,128)(2,1)}), bf16[512,1024]{1,0:T(8,128)(2,1)}) %all-gather.5.cloned.1.call-update) | async-done | bytes 1048592 | tf_op jit(solution)/shard_map/all_gather | solution.py:203
  422.4 3.9 dynamic_update_slice.15
  426.3 30.6 %all-gather.7.cloned.1.call-done = bf16[512,1024]{1,0:T(8,128)(2,1)} async-done(((bf16[32,1024]{1,0:T(8,128)(2,1)}), bf16[512,1024]{1,0:T(8,128)(2,1)}) %all-gather.7.cloned.1.call-update) | async-done | bytes 1048592 | tf_op jit(solution)/shard_map/all_gather | solution.py:203
  456.9 2.3 constant_dynamic-update-slice_fusion.3
  459.2 32.0 %all-gather.9.cloned.1.call-done = bf16[512,1024]{1,0:T(8,128)(2,1)} async-done(((bf16[32,1024]{1,0:T(8,128)(2,1)}), bf16[512,1024]{1,0:T(8,128)(2,1)}) %all-gather.9.cloned.1.call-update) | async-done | bytes 1048592 | tf_op jit(solution)/shard_map/all_gather | solution.py:203
  491.2 2.3 constant_dynamic-update-slice_fusion.2
  493.5 32.0 %all-gather.11.cloned.1.call-done = bf16[512,1024]{1,0:T(8,128)(2,1)} async-done(((bf16[32,1024]{1,0:T(8,128)(2,1)}), bf16[512,1024]{1,0:T(8,128)(2,1)}) %all-gather.11.cloned.1.call-update) | async-done | bytes 1048592 | tf_op jit(solution)/shard_map/all_gather | solution.py:203
  525.6 2.3 constant_dynamic-update-slice_fusion.1
  527.9 0.7 constant_dynamic-update-slice_fusion
  (54 shorter events, 1.4 us)
Async XLA Ops:
  6.5 0.9 copy-start.16
  7.4 13.4 %copy-start = (bf16[1024,1024]{1,0:T(8,128)(2,1)S(1)}, bf16[1024,1024]{1,0:T(8,128)(2,1)}, u32[]{:S(2)}) copy-start(bf16[1024,1024]{1,0:T(8,128)(2,1)} %constant.20.clone.basis_ref) | copy-start | bytes 6291460
  17.2 1.0 copy-start.8
  18.2 1.0 copy-start.10
  19.1 1.0 copy-start.12
  20.1 0.7 copy-start.14
  20.9 11.3 %copy-start.17 = (bf16[128,128]{1,0:T(8,128)(2,1)S(1)}, bf16[128,128]{1,0:T(8,128)(2,1)}, u32[]{:S(2)}) copy-start(bf16[128,128]{1,0:T(8,128)(2,1)} %constant.21.clone) | copy-start | bytes 98308
  20.9 11.3 %copy-start.18 = (s32[128]{0:T(128)S(1)}, s32[128]{0:T(128)}, u32[]{:S(2)}) copy-start(s32[128]{0:T(128)} %param.12) | copy-start | bytes 1540
  20.9 27.2 %copy-start.7 = (f32[128,128]{1,0:T(8,128)S(1)}, f32[128,128]{1,0:T(8,128)}, u32[]{:S(2)}) copy-start(f32[128,128]{1,0:T(8,128)} %weights_ref.9) | copy-start | bytes 196612
  22.8 1.0 copy-start.6
  23.7 24.3 %all-to-all-start = ((bf16[8,32,16,128]{3,2,1,0:T(8,128)(2,1)}), bf16[8,32,16,128]{3,2,1,0:T(8,128)(2,1)S(1)}, u32[]{:S(2)}, u32[]{:S(2)}) async-start(bf16[8,32,16,128]{3,2,1,0:T(8,128)(2,1)} %copy-done.6), calls=%async_computation | async-start | bytes 2097152 | tf_op jit(solution)/shard_map/all_to_all | solution.py:194
  32.1 206.3 %reduce-scatter.6.cloned.1.call-start = ((), (), s32[]{:S(2)}) async-start(), calls=%async_computation.15 | async-start | bytes 1114112 | tf_op jit(solution)/shard_map/reduce_scatter | solution.py:200
  48.1 21.8 %copy-start.1 = (bf16[1024,1024]{1,0:T(8,128)(2,1)S(1)}, bf16[1024,1024]{1,0:T(8,128)(2,1)}, u32[]{:S(2)}) copy-start(bf16[1024,1024]{1,0:T(8,128)(2,1)} %constant.19.clone.basis_ref) | copy-start | bytes 6291460
  69.9 4.4 copy-start.13
  74.3 164.7 %reduce-scatter.8.cloned.1.call-start = ((), (), s32[]{:S(2)}) async-start(), calls=%async_computation.17 | async-start | bytes 1114112 | tf_op jit(solution)/shard_map/reduce_scatter | solution.py:200
  74.3 45.4 %copy-start.2 = (bf16[1024,1024]{1,0:T(8,128)(2,1)S(1)}, bf16[1024,1024]{1,0:T(8,128)(2,1)}, u32[]{:S(2)}) copy-start(bf16[1024,1024]{1,0:T(8,128)(2,1)} %constant.19.clone.basis_ref) | copy-start | bytes 6291460
  119.7 4.4 copy-start.11
  124.1 138.8 %reduce-scatter.10.cloned.1.call-start = ((), (), s32[]{:S(2)}) async-start(), calls=%async_computation.19 | async-start | bytes 1114112 | tf_op jit(solution)/shard_map/reduce_scatter | solution.py:200
  124.1 42.4 %copy-start.3 = (bf16[1024,1024]{1,0:T(8,128)(2,1)S(1)}, bf16[1024,1024]{1,0:T(8,128)(2,1)}, u32[]{:S(2)}) copy-start(bf16[1024,1024]{1,0:T(8,128)(2,1)} %constant.19.clone.basis_ref) | copy-start | bytes 6291460
  166.5 4.4 copy-start.9
  170.8 153.7 %reduce-scatter.12.cloned.1.call-start = ((), (), s32[]{:S(2)}) async-start(), calls=%async_computation.21 | async-start | bytes 1114112 | tf_op jit(solution)/shard_map/reduce_scatter | solution.py:200
  170.9 37.1 %copy-start.4 = (bf16[1024,1024]{1,0:T(8,128)(2,1)S(1)}, bf16[1024,1024]{1,0:T(8,128)(2,1)}, u32[]{:S(2)}) copy-start(bf16[1024,1024]{1,0:T(8,128)(2,1)} %constant.19.clone.basis_ref) | copy-start | bytes 6291460
  208.0 4.4 copy-start.15
  212.3 173.5 %reduce-scatter.14.cloned.1.call-start = ((), (), s32[]{:S(2)}) async-start(), calls=%async_computation.23 | async-start | bytes 557056 | tf_op jit(solution)/shard_map/reduce_scatter | solution.py:200
  212.4 23.1 %copy-start.5 = (bf16[1024,1024]{1,0:T(8,128)(2,1)S(1)}, bf16[1024,1024]{1,0:T(8,128)(2,1)}, u32[]{:S(2)}) copy-start(bf16[1024,1024]{1,0:T(8,128)(2,1)} %constant.19.clone.basis_ref) | copy-start | bytes 6291460
  238.3 184.0 %all-gather.5.cloned.1.call-start = ((), (), s32[]{:S(2)}) async-start(), calls=%async_computation.16 | async-start | bytes 1114112 | tf_op jit(solution)/shard_map/all_gather | solution.py:203
  238.9 218.0 %all-gather.7.cloned.1.call-start = ((), (), s32[]{:S(2)}) async-start(), calls=%async_computation.18 | async-start | bytes 1114112 | tf_op jit(solution)/shard_map/all_gather | solution.py:203
  239.7 251.6 %all-gather.9.cloned.1.call-start = ((), (), s32[]{:S(2)}) async-start(), calls=%async_computation.20 | async-start | bytes 1114112 | tf_op jit(solution)/shard_map/all_gather | solution.py:203
  262.9 262.7 %all-gather.11.cloned.1.call-start = ((), (), s32[]{:S(2)}) async-start(), calls=%async_computation.22 | async-start | bytes 1114112 | tf_op jit(solution)/shard_map/all_gather | solution.py:203
Sparse Core Ops, SparseCore 0:
  74.4 59.4 reduce-scatter.5
  136.4 62.4 reduce-scatter.7
  201.2 61.5 reduce-scatter.9
  265.2 59.3 reduce-scatter.11
  326.8 59.0 reduce-scatter.13
  387.5 34.8 all-gather.4
  424.2 32.6 all-gather.6
  458.7 32.4 all-gather.8
  493.1 32.4 all-gather.10

commit v2 on v1

v2 whole, which is shorter than its diff:
```python
import math

import jax
import jax.numpy as jnp
import numpy as np
from jax import lax
from jax.experimental import pallas as pl
from jax.experimental.pallas import tpu as pltpu
from jax.sharding import PartitionSpec as P

BF16, F32 = jnp.bfloat16, jnp.float32
LANES = 128
VMEM_LIMIT = 48 * 1024 * 1024
CHUNKS = (46, 46, 45)
STEP = 23


def wave_table(length):
    ranks = np.arange(length)[:, None]
    middle = length // 2
    wavenumber = np.where(ranks <= middle, ranks, ranks - middle)
    angles = wavenumber * np.arange(length)[None, :] % length * (2.0 * math.pi / length)
    edge, inner = 1.0 / math.sqrt(length), math.sqrt(2.0 / length)
    values = np.where(
        ranks == 0,
        edge,
        np.where(
            ranks < middle,
            inner * np.cos(angles),
            np.where(ranks == middle, edge * np.cos(angles), inner * np.sin(angles)),
        ),
    )
    return values.astype(jnp.bfloat16)


def params():
    return pltpu.CompilerParams(vmem_limit_bytes=VMEM_LIMIT)


def mix_kernel(vertical_ref, member_ref, increment_ref, *refs):
    *out_refs, rows, mixed = refs
    levels, stored, _ = member_ref.shape
    tiles = rows.shape[0]
    product = member_ref[...].astype(F32) * increment_ref[...].astype(F32)
    product = product.reshape(levels * stored, tiles * LANES)
    for t in range(tiles):
        rows[t] = product[:, t * LANES : (t + 1) * LANES]
    vertical = vertical_ref[...]
    for p in range(stored):
        at = pl.ds(p, levels, stride=stored)
        block = jnp.concatenate([rows[t, at, :] for t in range(tiles)], axis=1).astype(BF16)
        block = jnp.dot(vertical, block, preferred_element_type=F32)
        for t in range(tiles):
            mixed[t, at, :] = block[:, t * LANES : (t + 1) * LANES]
    start = 0
    for out_ref in out_refs:
        size = out_ref.shape[0]
        for t in range(tiles):
            part = mixed[t, start * stored : (start + size) * stored, :].astype(BF16)
            out_ref[:, :, t * LANES : (t + 1) * LANES] = part.reshape(size, stored, LANES)
        start += size


def mix(vertical, member, increment, chunks, width=256):
    levels, stored, columns = member.shape
    wide = lambda size: pl.BlockSpec((size, stored, width), lambda i: (0, 0, i))
    return pl.pallas_call(
        mix_kernel,
        grid=(columns // width,),
        in_specs=[pl.BlockSpec((levels, levels), lambda i: (0, 0)), wide(levels), wide(levels)],
        out_specs=[wide(size) for size in chunks],
        out_shape=[jax.ShapeDtypeStruct((size, stored, columns), BF16) for size in chunks],
        scratch_shapes=[pltpu.VMEM((width // LANES, levels * stored, LANES), F32)] * 2,
        compiler_params=params(),
        name="mix",
    )(vertical, member, increment)


def cost(flops, values):
    return pl.CostEstimate(flops=flops, bytes_accessed=2 * values, transcendentals=0)


def at_tile(tile):
    return pl.ds(pl.multiple_of(tile * LANES, LANES), LANES)


def forward_kernel(order_ref, basis_ref, x_ref, *refs):
    *out_refs, coeffs = refs
    step, stored, columns = x_ref.shape
    coeffs[...] = jnp.dot(
        x_ref[...].reshape(step * stored, columns), basis_ref[...], preferred_element_type=F32
    ).astype(BF16)
    for d, out_ref in enumerate(out_refs):
        out_ref[...] = coeffs[:, at_tile(order_ref[d])].reshape(out_ref.shape)


def forward(order, basis, x):
    size, stored, columns = x.shape
    parts = columns // LANES
    step = min(STEP, size)
    piece = pl.BlockSpec((step, stored, LANES), lambda i, *_: (i, 0, 0))
    return pl.pallas_call(
        forward_kernel,
        grid_spec=pltpu.PrefetchScalarGridSpec(
            num_scalar_prefetch=1,
            grid=(pl.cdiv(size, step),),
            in_specs=[
                pl.BlockSpec((columns, columns), lambda i, *_: (0, 0)),
                pl.BlockSpec((step, stored, columns), lambda i, *_: (i, 0, 0)),
            ],
            out_specs=[piece] * parts,
            scratch_shapes=[pltpu.VMEM((step * stored, columns), BF16)],
        ),
        out_shape=[jax.ShapeDtypeStruct((size, stored, LANES), BF16)] * parts,
        compiler_params=params(),
        cost_estimate=cost(2 * x.size * columns, 2 * x.size + basis.size),
        name="forward",
    )(order, basis, x)


def filter_kernel(basis_ref, basis_t_ref, weights_ref, *refs):
    parts = len(refs) // 2
    x_refs, out_refs = refs[:parts], refs[parts:]
    step, stored, width = x_refs[0].shape
    x = jnp.concatenate(
        [jnp.concatenate([r[l] for r in x_refs], axis=0) for l in range(step)], axis=1
    )
    spectral = jnp.dot(basis_ref[...], x, preferred_element_type=F32)
    weights = jnp.concatenate([weights_ref[...]] * step, axis=1)
    damped = (spectral * weights).astype(BF16)
    back = jnp.dot(basis_t_ref[...], damped, preferred_element_type=F32).astype(BF16)
    for l in range(step):
        for d, out_ref in enumerate(out_refs):
            out_ref[l] = back[d * stored : (d + 1) * stored, l * width : (l + 1) * width]


def filter_rows(basis, basis_t, weights, pieces):
    parts = len(pieces)
    size, stored, width = pieces[0].shape
    step = min(STEP, size)
    whole = lambda a: pl.BlockSpec(a.shape, lambda i: (0, 0))
    block = pl.BlockSpec((step, stored, width), lambda i: (i, 0, 0))
    total = parts * pieces[0].size
    return pl.pallas_call(
        filter_kernel,
        grid=(pl.cdiv(size, step),),
        in_specs=[whole(basis), whole(basis_t), whole(weights)] + [block] * parts,
        out_specs=[block] * parts,
        out_shape=[jax.ShapeDtypeStruct(pieces[0].shape, BF16)] * parts,
        compiler_params=params(),
        cost_estimate=cost(4 * parts * stored * total, 2 * total),
        name="filter",
    )(basis, basis_t, weights, *pieces)


def backward_kernel(order_ref, tiles_ref, basis_ref, member_ref, *refs):
    *x_refs, keep_ref, give_ref, coeffs, held = refs
    step, stored, width = x_refs[0].shape
    for d, x_ref in enumerate(x_refs):
        coeffs[:, at_tile(order_ref[d])] = x_ref[...].reshape(step * stored, width)
    gridded = jnp.dot(coeffs[...], basis_ref[...], preferred_element_type=F32)
    held[...] = (member_ref[...].astype(F32).reshape(gridded.shape) * gridded).astype(BF16)
    half = len(x_refs) // 2
    for q in range(half):
        keep_ref[q] = held[:, at_tile(tiles_ref[q])].reshape(step, stored, width)
        give_ref[q] = held[:, at_tile(tiles_ref[half + q])].reshape(step, stored, width)


def backward(order, tiles, basis, member, pieces, start):
    parts = len(pieces)
    size, stored, width = pieces[0].shape
    columns = parts * width
    step = min(STEP, size)
    first = start // step
    assert first * step == start
    half = pl.BlockSpec((parts // 2, step, stored, width), lambda i, *_: (0, i, 0, 0))
    total = parts * pieces[0].size
    return pl.pallas_call(
        backward_kernel,
        grid_spec=pltpu.PrefetchScalarGridSpec(
            num_scalar_prefetch=2,
            grid=(pl.cdiv(size, step),),
            in_specs=[
                pl.BlockSpec((columns, columns), lambda i, *_: (0, 0)),
                pl.BlockSpec((step, stored, columns), lambda i, *_: (first + i, 0, 0)),
            ]
            + [pl.BlockSpec((step, stored, width), lambda i, *_: (i, 0, 0))] * parts,
            out_specs=[half] * 2,
            scratch_shapes=[pltpu.VMEM((step * stored, columns), BF16)] * 2,
        ),
        out_shape=[jax.ShapeDtypeStruct((parts // 2, size, stored, width), BF16)] * 2,
        compiler_params=params(),
        cost_estimate=cost(2 * total * columns, 3 * total + basis.size),
        name="backward",
    )(order, tiles, basis, member, *pieces)


def pair_kernel(a_ref, b_ref, *out_refs):
    for q, out_ref in enumerate(out_refs):
        out_ref[...] = (a_ref[q].astype(F32) + b_ref[q].astype(F32)).astype(BF16)


def pair_sum(a, b):
    parts, size, stored, width = a.shape
    step = min(STEP, size)
    block = pl.BlockSpec((parts, step, stored, width), lambda i: (0, i, 0, 0))
    return pl.pallas_call(
        pair_kernel,
        grid=(pl.cdiv(size, step),),
        in_specs=[block] * 2,
        out_specs=[pl.BlockSpec((step, stored, width), lambda i: (i, 0, 0))] * parts,
        out_shape=[jax.ShapeDtypeStruct(a.shape[1:], BF16)] * parts,
        compiler_params=params(),
        cost_estimate=cost(a.size, 3 * a.size),
        name="pair_sum",
    )(a, b)


def place_kernel(tiles_ref, mine_ref, theirs_ref, *refs):
    out_ref = refs[-1]
    half = mine_ref.shape[0]
    for q in range(half):
        out_ref[:, :, at_tile(tiles_ref[q])] = mine_ref[q]
        out_ref[:, :, at_tile(tiles_ref[half + q])] = theirs_ref[q]


def place(tiles, mine, theirs, out, start, levels):
    half, size, stored, width = mine.shape
    columns = 2 * half * width
    step = min(STEP, size)
    first = start // step
    block = pl.BlockSpec((half, step, stored, width), lambda i, *_: (0, i, 0, 0))
    held = [] if out is None else [out]
    return pl.pallas_call(
        place_kernel,
        grid_spec=pltpu.PrefetchScalarGridSpec(
            num_scalar_prefetch=1,
            grid=(pl.cdiv(size, step),),
            in_specs=[block] * 2 + [pl.BlockSpec(memory_space=pl.ANY)] * len(held),
            out_specs=pl.BlockSpec((step, stored, columns), lambda i, *_: (first + i, 0, 0)),
        ),
        out_shape=jax.ShapeDtypeStruct((levels, stored, columns), BF16),
        input_output_aliases={3: 0} if held else {},
        compiler_params=params(),
        cost_estimate=cost(0, 4 * mine.size),
        name="place",
    )(tiles, mine, theirs, *held)


Y, XLO, CORE, Z, XHI = 4, 2, 2, 4, 2


def space_to(dz, dx):
    return [(z * XHI + x, (z + dz) % Z * XHI + (x ^ dx)) for z in range(Z) for x in range(XHI)]


def mem_to(dy, dx, dc):
    return [
        ((y * XLO + x) * CORE + c, ((y + dy) % Y * XLO + (x ^ dx)) * CORE + (c ^ dc))
        for y in range(Y)
        for x in range(XLO)
        for c in range(CORE)
    ]


HOPS = [(dz, dx) for dz in range(Z) for dx in range(XHI)]


def exchange(pieces):
    out = [None] * len(HOPS)
    for d, (dz, dx) in enumerate(HOPS):
        source = HOPS.index((-dz % Z, dx))
        out[source] = pieces[d] if d == 0 else lax.ppermute(pieces[d], "space", space_to(dz, dx))
    return out


def add(*terms):
    return sum(t.astype(F32) for t in terms).astype(BF16)


def shards(members, increment, vertical, spectral_weights, tile_rows):
    levels, stored, columns = increment.shape
    member = members[0]
    table = wave_table(columns)
    basis_x, basis_xt = jnp.asarray(table), jnp.asarray(np.ascontiguousarray(table.T))
    space, mem = lax.axis_index("space"), lax.axis_index("mem")
    z, x, y, core = space // XHI, space % XHI, mem // (XLO * CORE), mem % CORE
    order = jnp.stack([(z + dz) % Z * XHI + (x ^ dx) for dz, dx in HOPS]).astype(jnp.int32)
    tiles = jnp.stack(
        [(core ^ dc) * Y + (y + dy) % Y for dc in range(CORE) for dy in range(Y)]
    ).astype(jnp.int32)
    rows = tile_rows.shape[0]
    held = jnp.take(tile_rows.reshape(len(HOPS), stored), order, axis=0).reshape(1, rows)
    chosen = (lax.broadcasted_iota(jnp.int32, (rows, rows), 0) == held).astype(BF16)
    basis_y = jnp.dot(jnp.asarray(wave_table(rows)), chosen, preferred_element_type=F32).astype(BF16)
    basis_yt = basis_y.T
    localized = mix(vertical, member, increment, CHUNKS)
    out = None
    start = 0
    for chunk in localized:
        size = chunk.shape[0]
        pieces = exchange(forward(order, basis_xt, chunk))
        pieces = exchange(filter_rows(basis_y, basis_yt, spectral_weights, pieces))
        keep, give = backward(order, tiles, basis_x, member, pieces, start)
        keep = pair_sum(keep, lax.ppermute(give, "mem", mem_to(0, 0, 1)))
        part = add(
            keep[0], *[lax.ppermute(keep[dy], "mem", mem_to(dy, 0, 0)) for dy in range(1, Y)]
        )
        part = add(part, lax.ppermute(part, "mem", mem_to(0, 1, 0)))
        mine = jnp.stack(
            [part] + [lax.ppermute(part, "mem", mem_to(-dy, 0, 0)) for dy in range(1, Y)]
        )
        theirs = lax.ppermute(mine, "mem", mem_to(0, 0, 1))
        out = place(tiles, mine, theirs, out, start, levels)
        start += size
    return out


def solution(mesh):
    return jax.shard_map(
        shards,
        mesh=mesh,
        in_specs=(
            P("mem", None, "space", None),
            P(None, "space", None),
            P(),
            P(None, "space"),
            P(),
        ),
        out_specs=P(None, "space", None),
        check_vma=False,
    )
```

time: 536 us -> 253 us (0.47)
  waiting for transfers between devices: 271 us -> 34.2 us
  blocking collectives: 178 us -> 0 us
  starting transfers between devices: 8.69 us -> 121 us
  local copies, waits for them, and re-layouts: 18.2 us -> 41.7 us
  between operations: 13.5 us -> 0.41 us
  Pallas kernels: 45.2 us -> 53.5 us
    all_to_all x9 -> x0, blocking collectives: 155 us -> none  [the longest x5 86.4 us: shards(): returned = lax.all_to_all(returned, 'space', 0, 0, tiled=True)]
    reduce_scatter x5 -> x0, waiting for transfers between devices: 146 us -> none  [shards(): lax.psum_scatter(part.reshape(full * stored, columns), 'mem', scatter_dim...]
    ppermute x0 -> x69, starting transfers between devices: none -> 121 us  [the longest x42 74 us: exchange(): lax.ppermute(pieces[d], 'space', space_to(dz, dx))]
    all_gather x4 -> x0, waiting for transfers between devices: 108 us -> none  [shards(): part = lax.all_gather(part, 'mem', axis=0, tiled=True)]
    unnamed x38 -> x110, local copies, waits for them, and re-layouts: 5.58 us -> 40.6 us
    ppermute x0 -> x69, waiting for transfers between devices: none -> 34.2 us  [the longest x9 16.7 us: shards(): lax.ppermute(keep[dy], 'mem', mem_to(dy, 0, 0))]
    all_gather x1 -> x0, blocking collectives: 23.1 us -> none  [shards(): part = lax.all_gather(part, 'mem', axis=0, tiled=True)]
    all_to_all x1 -> x0, waiting for transfers between devices: 15.6 us -> none  [shards(): coeffs = lax.all_to_all(coeffs, 'space', 0, 0, tiled=True)]
  transfers between devices with their start and end apart: 10 -> 69, of which waited for: 8 -> 16; matrix products, arithmetic and copies ran while one was open for 2% -> 1% of each run, Pallas kernels for 5% -> 14%
where the time goes in v2:
time: 253 us; the launch traced here: 252 us
  starting transfers between devices  121 us (48%)
  Pallas kernels  53.5 us (21%)
  local copies, waits for them, and re-layouts  41.7 us (16%)
  waiting for transfers between devices  34.2 us (14%)
    ppermute x42, starting transfers between devices, exchange(): lax.ppermute(pieces[d], 'space', space_to(dz, dx))  74 us
    unnamed x110, local copies, waits for them, and re-layouts  40.6 us
    ppermute x3, starting transfers between devices, shards(): keep = pair_sum(keep, lax.ppermute(give, 'mem', mem_to(0, 0, 1)))  18.7 us
    ppermute x9, waiting for transfers between devices, shards(): lax.ppermute(keep[dy], 'mem', mem_to(dy, 0, 0))  16.7 us
    pallas_call x3, Pallas kernels, backward(): pl.pallas_call(backward_kernel, grid_spec=pltpu.PrefetchScalarGridSpec(nu...  14.2 us
    pallas_call x3, Pallas kernels, forward(): pl.pallas_call(forward_kernel, grid_spec=pltpu.PrefetchScalarGridSpec(num...  12.1 us
    ppermute x9, waiting for transfers between devices, shards(): lax.ppermute(part, 'mem', mem_to(-dy, 0, 0))  11.1 us
    ppermute x9, starting transfers between devices, shards(): lax.ppermute(keep[dy], 'mem', mem_to(dy, 0, 0))  9.79 us
  transfers between devices with their start and end apart: 69, of which 16 were waited for; matrix products, arithmetic and copies ran while one was open for 1% of the time, Pallas kernels for 14%

profile of v2, /device:TPU:1, one launch (start us, length us, event | category | flops | bytes accessed | tf_op | source)
XLA Modules:
  0.0 251.9 jit_solution(1597806117406190406)
XLA Ops:
  0.9 9.6 %mix.1 = (bf16[46,16,1024]{2,1,0:T(8,128)(2,1)S(1)}, bf16[46,16,1024]{2,1,0:T(8,128)(2,1)S(1)}, bf16[45,16,1024]{2,1,0:T(8,128)(2,1)S(1)}) custom-call(bf16[137,137]{1,0:T(8,128)(2,1)S(1)} %copy-done.38, bf16[137,16,1024]{2,1,0:T(8,128)(2,1)} %bitcast.42, bf16[137,16,1024]{2,1,0:T(8,128)(2,1)} %increment_ref.1), custom_call_target="tpu_custom_call" | custom-call | tf_op jit(solution)/shard_map/mix/pallas_call | solution.py:67
  14.4 5.0 %forward.3 = (bf16[45,16,128]{2,1,0:T(8,128)(2,1)S(1)}, bf16[45,16,128]{2,1,0:T(8,128)(2,1)}, bf16[45,16,128]{2,1,0:T(8,128)(2,1)S(1)}, bf16[45,16,128]{2,1,0:T(...) custom-call(s32[8]{0:T(128)S(1)} %stack.134.order_ref, ...), custom_call_target="tpu_custom_call" | custom-call | flops 1509949440 | bytes 5046272 | tf_op jit(solution)/shard_map/forward/pallas_call | solution.py:102
  20.0 3.6 %collective-permute-start = (bf16[45,16,128]{2,1,0:T(8,128)(2,1)}, bf16[45,16,128]{2,1,0:T(8,128)(2,1)S(1)}, u32[]{:S(2)}, u32[]{:S(2)}) collective-permute-start(bf16[45,16,128]{2,1,0:T(8,128)(2,1)} %get-tuple-element.76), channel_id=1, source_target_pairs={{0,1},{1,0},{2,3},{3,2},{4,5},{5,4},{6,7},{7,6},{8,9},{9,8},{10,11... | collective-permute-start | bytes 552968 | tf_op jit(solution)/shard_map/ppermute | solution.py:273
  23.6 3.8 %collective-permute-start.1 = (bf16[45,16,128]{2,1,0:T(8,128)(2,1)S(1)}, bf16[45,16,128]{2,1,0:T(8,128)(2,1)S(1)}, u32[]{:S(2)}, u32[]{:S(2)}) collective-permute-start(bf16[45,16,128]{2,1,0:T(8,128)(2,1)S(1)} %get-tuple-element.77), channel_id=1, source_target_pairs={{0,6},{1,7},{2,0},{3,1},{4,2},{5,3},{6,4},{7,5},{8,14},{9,15},{10,... | collective-permute-start | bytes 552968 | tf_op jit(solution)/shard_map/ppermute | solution.py:273
  27.4 5.4 %collective-permute-start.4 = (bf16[45,16,128]{2,1,0:T(8,128)(2,1)S(1)}, bf16[45,16,128]{2,1,0:T(8,128)(2,1)S(1)}, u32[]{:S(2)}, u32[]{:S(2)}) collective-permute-start(bf16[45,16,128]{2,1,0:T(8,128)(2,1)S(1)} %get-tuple-element.80), channel_id=1, source_target_pairs={{0,5},{1,4},{2,7},{3,6},{4,1},{5,0},{6,3},{7,2},{8,13},{9,12},{10,... | collective-permute-start | bytes 552968 | tf_op jit(solution)/shard_map/ppermute | solution.py:273
  36.6 3.6 %forward.5 = (bf16[46,16,128]{2,1,0:T(8,128)(2,1)S(1)}, bf16[46,16,128]{2,1,0:T(8,128)(2,1)S(1)}, bf16[46,16,128]{2,1,0:T(8,128)(2,1)}, bf16[46,16,128]{2,1,0:T(...) custom-call(s32[8]{0:T(128)S(1)} %stack.134.order_ref, ...), custom_call_target="tpu_custom_call" | custom-call | flops 1543503872 | bytes 5111808 | tf_op jit(solution)/shard_map/forward/pallas_call | solution.py:102
  43.6 2.7 %collective-permute-start.46 = (bf16[46,16,128]{2,1,0:T(8,128)(2,1)S(1)}, bf16[46,16,128]{2,1,0:T(8,128)(2,1)S(1)}, u32[]{:S(2)}, u32[]{:S(2)}) collective-permute-start(bf16[46,16,128]{2,1,0:T(8,128)(2,1)S(1)} %get-tuple-element.122), channel_id=1, source_target_pairs={{0,1},{1,0},{2,3},{3,2},{4,5},{5,4},{6,7},{7,6},{8,9},{9,8},{10,11... | collective-permute-start | bytes 565256 | tf_op jit(solution)/shard_map/ppermute | solution.py:273
  47.0 2.7 %collective-permute-start.47 = (bf16[46,16,128]{2,1,0:T(8,128)(2,1)}, bf16[46,16,128]{2,1,0:T(8,128)(2,1)S(1)}, u32[]{:S(2)}, u32[]{:S(2)}) collective-permute-start(bf16[46,16,128]{2,1,0:T(8,128)(2,1)} %get-tuple-element.123), channel_id=1, source_target_pairs={{0,6},{1,7},{2,0},{3,1},{4,2},{5,3},{6,4},{7,5},{8,14},{9,15},{10,... | collective-permute-start | bytes 565256 | tf_op jit(solution)/shard_map/ppermute | solution.py:273
  50.3 2.0 collective-permute-start.48
  53.7 5.6 %collective-permute-start.50 = (bf16[46,16,128]{2,1,0:T(8,128)(2,1)}, bf16[46,16,128]{2,1,0:T(8,128)(2,1)S(1)}, u32[]{:S(2)}, u32[]{:S(2)}) collective-permute-start(bf16[46,16,128]{2,1,0:T(8,128)(2,1)} %get-tuple-element.126), channel_id=1, source_target_pairs={{0,5},{1,4},{2,7},{3,6},{4,1},{5,0},{6,3},{7,2},{8,13},{9,12},{10,... | collective-permute-start | bytes 565256 | tf_op jit(solution)/shard_map/ppermute | solution.py:273
  62.5 3.6 %forward.4 = (bf16[46,16,128]{2,1,0:T(8,128)(2,1)S(1)}, bf16[46,16,128]{2,1,0:T(8,128)(2,1)}, bf16[46,16,128]{2,1,0:T(8,128)(2,1)S(1)}, bf16[46,16,128]{2,1,0:T(...) custom-call(s32[8]{0:T(128)S(1)} %stack.134.order_ref, ...), custom_call_target="tpu_custom_call" | custom-call | flops 1543503872 | bytes 5111808 | tf_op jit(solution)/shard_map/forward/pallas_call | solution.py:102
  68.7 2.4 collective-permute-start.23
  71.1 3.0 %collective-permute-start.24 = (bf16[46,16,128]{2,1,0:T(8,128)(2,1)}, bf16[46,16,128]{2,1,0:T(8,128)(2,1)}, u32[]{:S(2)}, u32[]{:S(2)}) collective-permute-start(bf16[46,16,128]{2,1,0:T(8,128)(2,1)} %get-tuple-element.100), channel_id=1, source_target_pairs={{0,6},{1,7},{2,0},{3,1},{4,2},{5,3},{6,4},{7,5},{8,14},{9,15},{10,... | collective-permute-start | bytes 565256 | tf_op jit(solution)/shard_map/ppermute | solution.py:273
  77.1 4.3 %collective-permute-start.27 = (bf16[46,16,128]{2,1,0:T(8,128)(2,1)}, bf16[46,16,128]{2,1,0:T(8,128)(2,1)S(1)}, u32[]{:S(2)}, u32[]{:S(2)}) collective-permute-start(bf16[46,16,128]{2,1,0:T(8,128)(2,1)} %copy-done.49), channel_id=1, source_target_pairs={{0,5},{1,4},{2,7},{3,6},{4,1},{5,0},{6,3},{7,2},{8,13},{9,12},{10,... | collective-permute-start | bytes 565256 | tf_op jit(solution)/shard_map/ppermute | solution.py:273
  89.5 3.5 %filter.3 = (bf16[45,16,128]{2,1,0:T(8,128)(2,1)S(1)}, bf16[45,16,128]{2,1,0:T(8,128)(2,1)S(1)}, bf16[45,16,128]{2,1,0:T(8,128)(2,1)S(1)}, bf16[45,16,128]{2,1,0...) custom-call(bf16[128,128]{1,0:T(8,128)(2,1)S(1)} %copy.11.basis_ref,, ...), custom_call_target="tpu_custom_call" | custom-call | flops 377487360 | bytes 2949120 | tf_op jit(solution)/shard_map/filter/pallas_call | solution.py:144
  93.7 2.1 collective-permute-start.7
  95.8 2.7 %collective-permute-start.8 = (bf16[45,16,128]{2,1,0:T(8,128)(2,1)S(1)}, bf16[45,16,128]{2,1,0:T(8,128)(2,1)S(1)}, u32[]{:S(2)}, u32[]{:S(2)}) collective-permute-start(bf16[45,16,128]{2,1,0:T(8,128)(2,1)S(1)} %get-tuple-element.85), channel_id=1, source_target_pairs={{0,6},{1,7},{2,0},{3,1},{4,2},{5,3},{6,4},{7,5},{8,14},{9,15},{10,... | collective-permute-start | bytes 552968 | tf_op jit(solution)/shard_map/ppermute | solution.py:273
  99.6 5.5 %collective-permute-start.11 = (bf16[45,16,128]{2,1,0:T(8,128)(2,1)S(1)}, bf16[45,16,128]{2,1,0:T(8,128)(2,1)S(1)}, u32[]{:S(2)}, u32[]{:S(2)}) collective-permute-start(bf16[45,16,128]{2,1,0:T(8,128)(2,1)S(1)} %get-tuple-element.88), channel_id=1, source_target_pairs={{0,5},{1,4},{2,7},{3,6},{4,1},{5,0},{6,3},{7,2},{8,13},{9,12},{10,... | collective-permute-start | bytes 552968 | tf_op jit(solution)/shard_map/ppermute | solution.py:273
  106.1 2.0 filter.5
  111.2 2.9 %filter.4 = (bf16[46,16,128]{2,1,0:T(8,128)(2,1)S(1)}, bf16[46,16,128]{2,1,0:T(8,128)(2,1)S(1)}, bf16[46,16,128]{2,1,0:T(8,128)(2,1)}, bf16[46,16,128]{2,1,0:T(8...) custom-call(bf16[128,128]{1,0:T(8,128)(2,1)S(1)} %copy.11.basis_ref,, ...), custom_call_target="tpu_custom_call" | custom-call | flops 385875968 | bytes 3014656 | tf_op jit(solution)/shard_map/filter/pallas_call | solution.py:144
  114.8 2.1 collective-permute-start.53
  117.6 2.6 %collective-permute-start.54 = (bf16[46,16,128]{2,1,0:T(8,128)(2,1)S(1)}, bf16[46,16,128]{2,1,0:T(8,128)(2,1)S(1)}, u32[]{:S(2)}, u32[]{:S(2)}) collective-permute-start(bf16[46,16,128]{2,1,0:T(8,128)(2,1)S(1)} %get-tuple-element.131), channel_id=1, source_target_pairs={{0,6},{1,7},{2,0},{3,1},{4,2},{5,3},{6,4},{7,5},{8,14},{9,15},{10,... | collective-permute-start | bytes 565256 | tf_op jit(solution)/shard_map/ppermute | solution.py:273
  122.7 3.0 %collective-permute-start.30 = (bf16[46,16,128]{2,1,0:T(8,128)(2,1)S(1)}, bf16[46,16,128]{2,1,0:T(8,128)(2,1)S(1)}, u32[]{:S(2)}, u32[]{:S(2)}) collective-permute-start(bf16[46,16,128]{2,1,0:T(8,128)(2,1)S(1)} %get-tuple-element.107), channel_id=1, source_target_pairs={{0,1},{1,0},{2,3},{3,2},{4,5},{5,4},{6,7},{7,6},{8,9},{9,8},{10,11... | collective-permute-start | bytes 565256 | tf_op jit(solution)/shard_map/ppermute | solution.py:273
  126.4 2.9 %collective-permute-start.33 = (bf16[46,16,128]{2,1,0:T(8,128)(2,1)}, bf16[46,16,128]{2,1,0:T(8,128)(2,1)}, u32[]{:S(2)}, u32[]{:S(2)}) collective-permute-start(bf16[46,16,128]{2,1,0:T(8,128)(2,1)} %get-tuple-element.110), channel_id=1, source_target_pairs={{0,4},{1,5},{2,6},{3,7},{4,0},{5,1},{6,2},{7,3},{8,12},{9,13},{10,... | collective-permute-start | bytes 565256 | tf_op jit(solution)/shard_map/ppermute | solution.py:273
  129.3 2.8 %collective-permute-start.34 = (bf16[46,16,128]{2,1,0:T(8,128)(2,1)}, bf16[46,16,128]{2,1,0:T(8,128)(2,1)}, u32[]{:S(2)}, u32[]{:S(2)}) collective-permute-start(bf16[46,16,128]{2,1,0:T(8,128)(2,1)} %get-tuple-element.111), channel_id=1, source_target_pairs={{0,5},{1,4},{2,7},{3,6},{4,1},{5,0},{6,3},{7,2},{8,13},{9,12},{10,... | collective-permute-start | bytes 565256 | tf_op jit(solution)/shard_map/ppermute | solution.py:273
  134.6 2.1 collective-permute-start.56
  136.7 3.6 %collective-permute-start.57 = (bf16[46,16,128]{2,1,0:T(8,128)(2,1)}, bf16[46,16,128]{2,1,0:T(8,128)(2,1)S(1)}, u32[]{:S(2)}, u32[]{:S(2)}) collective-permute-start(bf16[46,16,128]{2,1,0:T(8,128)(2,1)} %copy-done.45), channel_id=1, source_target_pairs={{0,5},{1,4},{2,7},{3,6},{4,1},{5,0},{6,3},{7,2},{8,13},{9,12},{10,... | collective-permute-start | bytes 565256 | tf_op jit(solution)/shard_map/ppermute | solution.py:273
  140.3 3.5 %collective-permute-done.35.refs_6_ = bf16[46,16,128]{2,1,0:T(8,128)(2,1)} collective-permute-done((bf16[46,16,128]{2,1,0:T(8,128)(2,1)}, bf16[46,16,128]{2,1,0:T(8,128)(2,1)}, u32[]{:S(2)}, u32[]{:S(2)}) %collective-permute-start.35) | collective-permute-done | bytes 188448 | tf_op jit(solution)/shard_map/ppermute | solution.py:273
  151.2 5.1 %backward.3 = (bf16[4,45,16,128]{3,2,1,0:T(8,128)(2,1)S(1)}, bf16[4,45,16,128]{3,2,1,0:T(8,128)(2,1)S(1)}) custom-call(s32[8]{0:T(128)S(1)} %stack.134.order_ref, s32[8]{0:T(128)S(1)} %stack.125.tiles_ref, bf16[1024,1024]{1,0:T(8,128)(2,1)S(1)} %copy-done, bf16[137,16,1024]{2,1,0:T(8,128)(2,1)} %bitcast.43, bf16[45,16,128]{2,1,0:T(8,128)(2,1)S(1)} %copy-done.23, ...), custom_call_target="tpu_custom_call" | custom-call | flops 1509949440 | bytes 6520832 | tf_op jit(solution)/shard_map/backward/pallas_call | solution.py:178
  156.3 17.8 %collective-permute-start.14 = (bf16[4,45,16,128]{3,2,1,0:T(8,128)(2,1)S(1)}, bf16[4,45,16,128]{3,2,1,0:T(8,128)(2,1)S(1)}, u32[]{:S(2)}, u32[]{:S(2)}) collective-permute-start(bf16[4,45,16,128]{3,2,1,0:T(8,128)(2,1)S(1)} %get-tuple-element.92), channel_id=1, source_target_pairs={{0,8},{8,0},{16,24},{24,16},{32,40},{40,32},{48,56},{56,48},{64,72... | collective-permute-start | bytes 2211848 | tf_op jit(solution)/shard_map/ppermute | solution.py:305
  174.1 4.6 %backward.4 = (bf16[4,46,16,128]{3,2,1,0:T(8,128)(2,1)S(1)}, bf16[4,46,16,128]{3,2,1,0:T(8,128)(2,1)S(1)}) custom-call(s32[8]{0:T(128)S(1)} %stack.134.order_ref, s32[8]{0:T(128)S(1)} %stack.125.tiles_ref, bf16[1024,1024]{1,0:T(8,128)(2,1)S(1)} %copy-done, bf16[137,16,1024]{2,1,0:T(8,128)(2,1)} %bitcast.44, ...), custom_call_target="tpu_custom_call" | custom-call | flops 1543503872 | bytes 6619136 | tf_op jit(solution)/shard_map/backward/pallas_call | solution.py:178
  179.1 4.5 %backward.5 = (bf16[4,46,16,128]{3,2,1,0:T(8,128)(2,1)S(1)}, bf16[4,46,16,128]{3,2,1,0:T(8,128)(2,1)S(1)}) custom-call(s32[8]{0:T(128)S(1)} %stack.134.order_ref, s32[8]{0:T(128)S(1)} %stack.125.tiles_ref, bf16[1024,1024]{1,0:T(8,128)(2,1)S(1)} %copy-done, bf16[137,16,1024]{2,1,0:T(8,128)(2,1)} %bitcast.45, bf16[46,16,128]{2,1,0:T(8,128)(2,1)S(1)} %copy-done.5, ...), custom_call_target="tpu_custom_call" | custom-call | flops 1543503872 | bytes 6619136 | tf_op jit(solution)/shard_map/backward/pallas_call | solution.py:178
  184.2 2.0 pair_sum.3
  187.6 2.6 %collective-permute-start.16 = (bf16[45,16,128]{2,1,0:T(8,128)(2,1)S(1)}, bf16[45,16,128]{2,1,0:T(8,128)(2,1)S(1)}, u32[]{:S(2)}, u32[]{:S(2)}) collective-permute-start(bf16[45,16,128]{2,1,0:T(8,128)(2,1)S(1)} %get-tuple-element.95), channel_id=1, source_target_pairs={{0,64},{8,72},{16,80},{24,88},{32,96},{40,104},{48,112},{56,120},{... | collective-permute-start | bytes 552968 | tf_op jit(solution)/shard_map/ppermute | solution.py:307
  195.2 3.7 %collective-permute-done.16 = bf16[45,16,128]{2,1,0:T(8,128)(2,1)S(1)} collective-permute-done((bf16[45,16,128]{2,1,0:T(8,128)(2,1)S(1)}, bf16[45,16,128]{2,1,0:T(8,128)(2,1)S(1)}, u32[]{:S(2)}, u32[]{:S(2)}) %collective-permute-start.16) | collective-permute-done | bytes 184352 | tf_op jit(solution)/shard_map/ppermute | solution.py:307
  199.0 1.9 collective-permute-start.62
  201.0 2.1 collective-permute-done.38
  203.3 3.8 %collective-permute-done.39 = bf16[46,16,128]{2,1,0:T(8,128)(2,1)S(1)} collective-permute-done((bf16[46,16,128]{2,1,0:T(8,128)(2,1)S(1)}, bf16[46,16,128]{2,1,0:T(8,128)(2,1)S(1)}, u32[]{:S(2)}, u32[]{:S(2)}) %collective-permute-start.39) | collective-permute-done | bytes 188448 | tf_op jit(solution)/shard_map/ppermute | solution.py:307
  208.7 2.3 collective-permute-done.61
  211.0 4.1 %collective-permute-done.62 = bf16[46,16,128]{2,1,0:T(8,128)(2,1)S(1)} collective-permute-done((bf16[46,16,128]{2,1,0:T(8,128)(2,1)S(1)}, bf16[46,16,128]{2,1,0:T(8,128)(2,1)S(1)}, u32[]{:S(2)}, u32[]{:S(2)}) %collective-permute-start.62) | collective-permute-done | bytes 188448 | tf_op jit(solution)/shard_map/ppermute | solution.py:307
  216.2 2.8 %collective-permute-start.43 = (bf16[46,16,128]{2,1,0:T(8,128)(2,1)S(1)}, bf16[46,16,128]{2,1,0:T(8,128)(2,1)S(1)}, u32[]{:S(2)}, u32[]{:S(2)}) collective-permute-start(bf16[46,16,128]{2,1,0:T(8,128)(2,1)S(1)} %add_convert_fusion.2), channel_id=1, source_target_pairs={{0,64},{8,72},{16,80},{24,88},{32,96},{40,104},{48,112},{56,120},{... | collective-permute-start | bytes 565256 | tf_op jit(solution)/shard_map/ppermute | solution.py:311
  221.0 3.6 %collective-permute-start.66 = (bf16[46,16,128]{2,1,0:T(8,128)(2,1)S(1)}, bf16[46,16,128]{2,1,0:T(8,128)(2,1)S(1)}, u32[]{:S(2)}, u32[]{:S(2)}) collective-permute-start(bf16[46,16,128]{2,1,0:T(8,128)(2,1)S(1)} %add_convert_fusion), channel_id=1, source_target_pairs={{0,64},{8,72},{16,80},{24,88},{32,96},{40,104},{48,112},{56,120},{... | collective-permute-start | bytes 565256 | tf_op jit(solution)/shard_map/ppermute | solution.py:311
  228.9 4.1 %collective-permute-done.67 = bf16[46,16,128]{2,1,0:T(8,128)(2,1)S(1)} collective-permute-done((bf16[46,16,128]{2,1,0:T(8,128)(2,1)S(1)}, bf16[46,16,128]{2,1,0:T(8,128)(2,1)S(1)}, u32[]{:S(2)}, u32[]{:S(2)}) %collective-permute-start.67) | collective-permute-done | bytes 188448 | tf_op jit(solution)/shard_map/ppermute | solution.py:311
  234.6 3.8 %collective-permute-start.45 = (bf16[4,46,16,128]{3,2,1,0:T(8,128)(2,1)S(1)}, bf16[4,46,16,128]{3,2,1,0:T(8,128)(2,1)S(1)}, u32[]{:S(2)}, u32[]{:S(2)}) collective-permute-start(bf16[4,46,16,128]{3,2,1,0:T(8,128)(2,1)S(1)} %pad_maximum_fusion.mine_ref), channel_id=1, source_target_pairs={{0,8},{8,0},{16,24},{24,16},{32,40},{40,32},{48,56},{56,48},{64,72... | collective-permute-start | bytes 2261000 | tf_op jit(solution)/shard_map/ppermute | solution.py:313
  242.6 2.7 %collective-permute-start.22 = (bf16[4,45,16,128]{3,2,1,0:T(8,128)(2,1)S(1)}, bf16[4,45,16,128]{3,2,1,0:T(8,128)(2,1)S(1)}, u32[]{:S(2)}, u32[]{:S(2)}) collective-permute-start(bf16[4,45,16,128]{3,2,1,0:T(8,128)(2,1)S(1)} %pad_maximum_fusion.2.mine_ref), channel_id=1, source_target_pairs={{0,8},{8,0},{16,24},{24,16},{32,40},{40,32},{48,56},{56,48},{64,72... | collective-permute-start | bytes 2211848 | tf_op jit(solution)/shard_map/ppermute | solution.py:313
  245.3 2.0 place.3.refs_0_
  247.3 2.0 place.4.refs_0_
  249.3 2.5 %place.5 = bf16[137,16,1024]{2,1,0:T(8,128)(2,1)} custom-call(s32[8]{0:T(128)S(1)} %stack.125.tiles_ref, bf16[4,45,16,128]{3,2,1,0:T(8,128)(2,1)S(1)} %pad_maximum_fusion.2.mine_ref, bf16[4,45,16,128]{3,2,1,0:T(8,128)(2,1)S(1)} %collective-permute-done.22.theirs_ref, bf16[137,16,1024]{2,1,0:T(8,128)(2,1)} %place.4.refs_0_), custom_call_target="tpu_custom_call", output_to_operand_aliasing={{}: (3, {})} | custom-call | bytes 2949120 | tf_op jit(solution)/shard_map/place/pallas_call | solution.py:234
  (237 shorter events, 75.0 us)
Async XLA Ops:
  20.0 20.2 %collective-permute-start = (bf16[45,16,128]{2,1,0:T(8,128)(2,1)}, bf16[45,16,128]{2,1,0:T(8,128)(2,1)S(1)}, u32[]{:S(2)}, u32[]{:S(2)}) collective-permute-start(bf16[45,16,128]{2,1,0:T(8,128)(2,1)} %get-tuple-element.76), channel_id=1, source_target_pairs={{0,1},{1,0},{2,3},{3,2},{4,5},{5,4},{6,7},{7,6},{8,9},{9,8},{10,11... | collective-permute-start | bytes 552968 | tf_op jit(solution)/shard_map/ppermute | solution.py:273
  23.6 18.6 %collective-permute-start.1 = (bf16[45,16,128]{2,1,0:T(8,128)(2,1)S(1)}, bf16[45,16,128]{2,1,0:T(8,128)(2,1)S(1)}, u32[]{:S(2)}, u32[]{:S(2)}) collective-permute-start(bf16[45,16,128]{2,1,0:T(8,128)(2,1)S(1)} %get-tuple-element.77), channel_id=1, source_target_pairs={{0,6},{1,7},{2,0},{3,1},{4,2},{5,3},{6,4},{7,5},{8,14},{9,15},{10,... | collective-permute-start | bytes 552968 | tf_op jit(solution)/shard_map/ppermute | solution.py:273
  27.3 15.6 %collective-permute-start.2 = (bf16[45,16,128]{2,1,0:T(8,128)(2,1)S(1)}, bf16[45,16,128]{2,1,0:T(8,128)(2,1)S(1)}, u32[]{:S(2)}, u32[]{:S(2)}) collective-permute-start(bf16[45,16,128]{2,1,0:T(8,128)(2,1)S(1)} %get-tuple-element.78), channel_id=1, source_target_pairs={{0,7},{1,6},{2,1},{3,0},{4,3},{5,2},{6,5},{7,4},{8,15},{9,14},{10,... | collective-permute-start | bytes 552968 | tf_op jit(solution)/shard_map/ppermute | solution.py:273
  27.4 18.9 %collective-permute-start.3 = (bf16[45,16,128]{2,1,0:T(8,128)(2,1)S(1)}, bf16[45,16,128]{2,1,0:T(8,128)(2,1)S(1)}, u32[]{:S(2)}, u32[]{:S(2)}) collective-permute-start(bf16[45,16,128]{2,1,0:T(8,128)(2,1)S(1)} %get-tuple-element.79), channel_id=1, source_target_pairs={{0,4},{1,5},{2,6},{3,7},{4,0},{5,1},{6,2},{7,3},{8,12},{9,13},{10,... | collective-permute-start | bytes 552968 | tf_op jit(solution)/shard_map/ppermute | solution.py:273
  27.4 22.2 %collective-permute-start.4 = (bf16[45,16,128]{2,1,0:T(8,128)(2,1)S(1)}, bf16[45,16,128]{2,1,0:T(8,128)(2,1)S(1)}, u32[]{:S(2)}, u32[]{:S(2)}) collective-permute-start(bf16[45,16,128]{2,1,0:T(8,128)(2,1)S(1)} %get-tuple-element.80), channel_id=1, source_target_pairs={{0,5},{1,4},{2,7},{3,6},{4,1},{5,0},{6,3},{7,2},{8,13},{9,12},{10,... | collective-permute-start | bytes 552968 | tf_op jit(solution)/shard_map/ppermute | solution.py:273
  40.9 11.4 %collective-permute-start.5 = (bf16[45,16,128]{2,1,0:T(8,128)(2,1)S(1)}, bf16[45,16,128]{2,1,0:T(8,128)(2,1)S(1)}, u32[]{:S(2)}, u32[]{:S(2)}) collective-permute-start(bf16[45,16,128]{2,1,0:T(8,128)(2,1)S(1)} %get-tuple-element.81), channel_id=1, source_target_pairs={{0,2},{1,3},{2,4},{3,5},{4,6},{5,7},{6,0},{7,1},{8,10},{9,11},{10,... | collective-permute-start | bytes 552968 | tf_op jit(solution)/shard_map/ppermute | solution.py:273
  43.6 15.7 %collective-permute-start.46 = (bf16[46,16,128]{2,1,0:T(8,128)(2,1)S(1)}, bf16[46,16,128]{2,1,0:T(8,128)(2,1)S(1)}, u32[]{:S(2)}, u32[]{:S(2)}) collective-permute-start(bf16[46,16,128]{2,1,0:T(8,128)(2,1)S(1)} %get-tuple-element.122), channel_id=1, source_target_pairs={{0,1},{1,0},{2,3},{3,2},{4,5},{5,4},{6,7},{7,6},{8,9},{9,8},{10,11... | collective-permute-start | bytes 565256 | tf_op jit(solution)/shard_map/ppermute | solution.py:273
  47.0 21.8 %collective-permute-start.47 = (bf16[46,16,128]{2,1,0:T(8,128)(2,1)}, bf16[46,16,128]{2,1,0:T(8,128)(2,1)S(1)}, u32[]{:S(2)}, u32[]{:S(2)}) collective-permute-start(bf16[46,16,128]{2,1,0:T(8,128)(2,1)} %get-tuple-element.123), channel_id=1, source_target_pairs={{0,6},{1,7},{2,0},{3,1},{4,2},{5,3},{6,4},{7,5},{8,14},{9,15},{10,... | collective-permute-start | bytes 565256 | tf_op jit(solution)/shard_map/ppermute | solution.py:273
  50.3 18.4 %collective-permute-start.48 = (bf16[46,16,128]{2,1,0:T(8,128)(2,1)}, bf16[46,16,128]{2,1,0:T(8,128)(2,1)S(1)}, u32[]{:S(2)}, u32[]{:S(2)}) collective-permute-start(bf16[46,16,128]{2,1,0:T(8,128)(2,1)} %get-tuple-element.124), channel_id=1, source_target_pairs={{0,7},{1,6},{2,1},{3,0},{4,3},{5,2},{6,5},{7,4},{8,15},{9,14},{10,... | collective-permute-start | bytes 565256 | tf_op jit(solution)/shard_map/ppermute | solution.py:273
  53.0 18.1 %collective-permute-start.49 = (bf16[46,16,128]{2,1,0:T(8,128)(2,1)}, bf16[46,16,128]{2,1,0:T(8,128)(2,1)S(1)}, u32[]{:S(2)}, u32[]{:S(2)}) collective-permute-start(bf16[46,16,128]{2,1,0:T(8,128)(2,1)} %get-tuple-element.125), channel_id=1, source_target_pairs={{0,4},{1,5},{2,6},{3,7},{4,0},{5,1},{6,2},{7,3},{8,12},{9,13},{10,... | collective-permute-start | bytes 565256 | tf_op jit(solution)/shard_map/ppermute | solution.py:273
  53.7 20.4 %collective-permute-start.50 = (bf16[46,16,128]{2,1,0:T(8,128)(2,1)}, bf16[46,16,128]{2,1,0:T(8,128)(2,1)S(1)}, u32[]{:S(2)}, u32[]{:S(2)}) collective-permute-start(bf16[46,16,128]{2,1,0:T(8,128)(2,1)} %get-tuple-element.126), channel_id=1, source_target_pairs={{0,5},{1,4},{2,7},{3,6},{4,1},{5,0},{6,3},{7,2},{8,13},{9,12},{10,... | collective-permute-start | bytes 565256 | tf_op jit(solution)/shard_map/ppermute | solution.py:273
  59.3 16.0 %collective-permute-start.51 = (bf16[46,16,128]{2,1,0:T(8,128)(2,1)}, bf16[46,16,128]{2,1,0:T(8,128)(2,1)S(1)}, u32[]{:S(2)}, u32[]{:S(2)}) collective-permute-start(bf16[46,16,128]{2,1,0:T(8,128)(2,1)} %get-tuple-element.127), channel_id=1, source_target_pairs={{0,2},{1,3},{2,4},{3,5},{4,6},{5,7},{6,0},{7,1},{8,10},{9,11},{10,... | collective-permute-start | bytes 565256 | tf_op jit(solution)/shard_map/ppermute | solution.py:273
  68.7 12.6 %collective-permute-start.23 = (bf16[46,16,128]{2,1,0:T(8,128)(2,1)}, bf16[46,16,128]{2,1,0:T(8,128)(2,1)}, u32[]{:S(2)}, u32[]{:S(2)}) collective-permute-start(bf16[46,16,128]{2,1,0:T(8,128)(2,1)} %get-tuple-element.99), channel_id=1, source_target_pairs={{0,1},{1,0},{2,3},{3,2},{4,5},{5,4},{6,7},{7,6},{8,9},{9,8},{10,11... | collective-permute-start | bytes 565256 | tf_op jit(solution)/shard_map/ppermute | solution.py:273
  74.1 19.6 %collective-permute-start.25 = (bf16[46,16,128]{2,1,0:T(8,128)(2,1)}, bf16[46,16,128]{2,1,0:T(8,128)(2,1)}, u32[]{:S(2)}, u32[]{:S(2)}) collective-permute-start(bf16[46,16,128]{2,1,0:T(8,128)(2,1)} %get-tuple-element.101), channel_id=1, source_target_pairs={{0,7},{1,6},{2,1},{3,0},{4,3},{5,2},{6,5},{7,4},{8,15},{9,14},{10,... | collective-permute-start | bytes 565256 | tf_op jit(solution)/shard_map/ppermute | solution.py:273
  75.4 20.5 %collective-permute-start.26 = (bf16[46,16,128]{2,1,0:T(8,128)(2,1)}, bf16[46,16,128]{2,1,0:T(8,128)(2,1)}, u32[]{:S(2)}, u32[]{:S(2)}) collective-permute-start(bf16[46,16,128]{2,1,0:T(8,128)(2,1)} %get-tuple-element.102), channel_id=1, source_target_pairs={{0,4},{1,5},{2,6},{3,7},{4,0},{5,1},{6,2},{7,3},{8,12},{9,13},{10,... | collective-permute-start | bytes 565256 | tf_op jit(solution)/shard_map/ppermute | solution.py:273
  77.1 21.4 %collective-permute-start.27 = (bf16[46,16,128]{2,1,0:T(8,128)(2,1)}, bf16[46,16,128]{2,1,0:T(8,128)(2,1)S(1)}, u32[]{:S(2)}, u32[]{:S(2)}) collective-permute-start(bf16[46,16,128]{2,1,0:T(8,128)(2,1)} %copy-done.49), channel_id=1, source_target_pairs={{0,5},{1,4},{2,7},{3,6},{4,1},{5,0},{6,3},{7,2},{8,13},{9,12},{10,... | collective-permute-start | bytes 565256 | tf_op jit(solution)/shard_map/ppermute | solution.py:273
  81.3 18.2 %collective-permute-start.28 = (bf16[46,16,128]{2,1,0:T(8,128)(2,1)}, bf16[46,16,128]{2,1,0:T(8,128)(2,1)S(1)}, u32[]{:S(2)}, u32[]{:S(2)}) collective-permute-start(bf16[46,16,128]{2,1,0:T(8,128)(2,1)} %copy-done.48), channel_id=1, source_target_pairs={{0,2},{1,3},{2,4},{3,5},{4,6},{5,7},{6,0},{7,1},{8,10},{9,11},{10,... | collective-permute-start | bytes 565256 | tf_op jit(solution)/shard_map/ppermute | solution.py:273
  81.4 18.3 %collective-permute-start.29 = (bf16[46,16,128]{2,1,0:T(8,128)(2,1)}, bf16[46,16,128]{2,1,0:T(8,128)(2,1)S(1)}, u32[]{:S(2)}, u32[]{:S(2)}) collective-permute-start(bf16[46,16,128]{2,1,0:T(8,128)(2,1)} %copy-done.47), channel_id=1, source_target_pairs={{0,3},{1,2},{2,5},{3,4},{4,7},{5,6},{6,1},{7,0},{8,11},{9,10},{10,... | collective-permute-start | bytes 565256 | tf_op jit(solution)/shard_map/ppermute | solution.py:273
  93.7 11.4 %collective-permute-start.7 = (bf16[45,16,128]{2,1,0:T(8,128)(2,1)S(1)}, bf16[45,16,128]{2,1,0:T(8,128)(2,1)S(1)}, u32[]{:S(2)}, u32[]{:S(2)}) collective-permute-start(bf16[45,16,128]{2,1,0:T(8,128)(2,1)S(1)} %get-tuple-element.84), channel_id=1, source_target_pairs={{0,1},{1,0},{2,3},{3,2},{4,5},{5,4},{6,7},{7,6},{8,9},{9,8},{10,11... | collective-permute-start | bytes 552968 | tf_op jit(solution)/shard_map/ppermute | solution.py:273
  98.5 15.6 %collective-permute-start.9 = (bf16[45,16,128]{2,1,0:T(8,128)(2,1)S(1)}, bf16[45,16,128]{2,1,0:T(8,128)(2,1)S(1)}, u32[]{:S(2)}, u32[]{:S(2)}) collective-permute-start(bf16[45,16,128]{2,1,0:T(8,128)(2,1)S(1)} %get-tuple-element.86), channel_id=1, source_target_pairs={{0,7},{1,6},{2,1},{3,0},{4,3},{5,2},{6,5},{7,4},{8,15},{9,14},{10,... | collective-permute-start | bytes 552968 | tf_op jit(solution)/shard_map/ppermute | solution.py:273
  99.5 17.4 %collective-permute-start.10 = (bf16[45,16,128]{2,1,0:T(8,128)(2,1)S(1)}, bf16[45,16,128]{2,1,0:T(8,128)(2,1)S(1)}, u32[]{:S(2)}, u32[]{:S(2)}) collective-permute-start(bf16[45,16,128]{2,1,0:T(8,128)(2,1)S(1)} %get-tuple-element.87), channel_id=1, source_target_pairs={{0,4},{1,5},{2,6},{3,7},{4,0},{5,1},{6,2},{7,3},{8,12},{9,13},{10,... | collective-permute-start | bytes 552968 | tf_op jit(solution)/shard_map/ppermute | solution.py:273
  99.6 20.5 %collective-permute-start.11 = (bf16[45,16,128]{2,1,0:T(8,128)(2,1)S(1)}, bf16[45,16,128]{2,1,0:T(8,128)(2,1)S(1)}, u32[]{:S(2)}, u32[]{:S(2)}) collective-permute-start(bf16[45,16,128]{2,1,0:T(8,128)(2,1)S(1)} %get-tuple-element.88), channel_id=1, source_target_pairs={{0,5},{1,4},{2,7},{3,6},{4,1},{5,0},{6,3},{7,2},{8,13},{9,12},{10,... | collective-permute-start | bytes 552968 | tf_op jit(solution)/shard_map/ppermute | solution.py:273
  105.1 16.9 %collective-permute-start.12 = (bf16[45,16,128]{2,1,0:T(8,128)(2,1)S(1)}, bf16[45,16,128]{2,1,0:T(8,128)(2,1)S(1)}, u32[]{:S(2)}, u32[]{:S(2)}) collective-permute-start(bf16[45,16,128]{2,1,0:T(8,128)(2,1)S(1)} %get-tuple-element.89), channel_id=1, source_target_pairs={{0,2},{1,3},{2,4},{3,5},{4,6},{5,7},{6,0},{7,1},{8,10},{9,11},{10,... | collective-permute-start | bytes 552968 | tf_op jit(solution)/shard_map/ppermute | solution.py:273
  105.4 20.3 %collective-permute-start.13 = (bf16[45,16,128]{2,1,0:T(8,128)(2,1)S(1)}, bf16[45,16,128]{2,1,0:T(8,128)(2,1)S(1)}, u32[]{:S(2)}, u32[]{:S(2)}) collective-permute-start(bf16[45,16,128]{2,1,0:T(8,128)(2,1)S(1)} %get-tuple-element.90), channel_id=1, source_target_pairs={{0,3},{1,2},{2,5},{3,4},{4,7},{5,6},{6,1},{7,0},{8,11},{9,10},{10,... | collective-permute-start | bytes 552968 | tf_op jit(solution)/shard_map/ppermute | solution.py:273
  114.8 11.6 %collective-permute-start.53 = (bf16[46,16,128]{2,1,0:T(8,128)(2,1)S(1)}, bf16[46,16,128]{2,1,0:T(8,128)(2,1)S(1)}, u32[]{:S(2)}, u32[]{:S(2)}) collective-permute-start(bf16[46,16,128]{2,1,0:T(8,128)(2,1)S(1)} %get-tuple-element.130), channel_id=1, source_target_pairs={{0,1},{1,0},{2,3},{3,2},{4,5},{5,4},{6,7},{7,6},{8,9},{9,8},{10,11... | collective-permute-start | bytes 565256 | tf_op jit(solution)/shard_map/ppermute | solution.py:273
  129.3 11.0 %collective-permute-start.34 = (bf16[46,16,128]{2,1,0:T(8,128)(2,1)}, bf16[46,16,128]{2,1,0:T(8,128)(2,1)}, u32[]{:S(2)}, u32[]{:S(2)}) collective-permute-start(bf16[46,16,128]{2,1,0:T(8,128)(2,1)} %get-tuple-element.111), channel_id=1, source_target_pairs={{0,5},{1,4},{2,7},{3,6},{4,1},{5,0},{6,3},{7,2},{8,13},{9,12},{10,... | collective-permute-start | bytes 565256 | tf_op jit(solution)/shard_map/ppermute | solution.py:273
  132.1 11.7 %collective-permute-start.35 = (bf16[46,16,128]{2,1,0:T(8,128)(2,1)}, bf16[46,16,128]{2,1,0:T(8,128)(2,1)}, u32[]{:S(2)}, u32[]{:S(2)}) collective-permute-start(bf16[46,16,128]{2,1,0:T(8,128)(2,1)} %get-tuple-element.112), channel_id=1, source_target_pairs={{0,2},{1,3},{2,4},{3,5},{4,6},{5,7},{6,0},{7,1},{8,10},{9,11},{10,... | collective-permute-start | bytes 565256 | tf_op jit(solution)/shard_map/ppermute | solution.py:273
  133.2 23.1 %collective-permute-start.36 = (bf16[46,16,128]{2,1,0:T(8,128)(2,1)}, bf16[46,16,128]{2,1,0:T(8,128)(2,1)}, u32[]{:S(2)}, u32[]{:S(2)}) collective-permute-start(bf16[46,16,128]{2,1,0:T(8,128)(2,1)} %get-tuple-element.113), channel_id=1, source_target_pairs={{0,3},{1,2},{2,5},{3,4},{4,7},{5,6},{6,1},{7,0},{8,11},{9,10},{10,... | collective-permute-start | bytes 565256 | tf_op jit(solution)/shard_map/ppermute | solution.py:273
  134.6 44.2 %collective-permute-start.56 = (bf16[46,16,128]{2,1,0:T(8,128)(2,1)}, bf16[46,16,128]{2,1,0:T(8,128)(2,1)S(1)}, u32[]{:S(2)}, u32[]{:S(2)}) collective-permute-start(bf16[46,16,128]{2,1,0:T(8,128)(2,1)} %copy-done.46), channel_id=1, source_target_pairs={{0,4},{1,5},{2,6},{3,7},{4,0},{5,1},{6,2},{7,3},{8,12},{9,13},{10,... | collective-permute-start | bytes 565256 | tf_op jit(solution)/shard_map/ppermute | solution.py:273
  136.7 42.4 %collective-permute-start.57 = (bf16[46,16,128]{2,1,0:T(8,128)(2,1)}, bf16[46,16,128]{2,1,0:T(8,128)(2,1)S(1)}, u32[]{:S(2)}, u32[]{:S(2)}) collective-permute-start(bf16[46,16,128]{2,1,0:T(8,128)(2,1)} %copy-done.45), channel_id=1, source_target_pairs={{0,5},{1,4},{2,7},{3,6},{4,1},{5,0},{6,3},{7,2},{8,13},{9,12},{10,... | collective-permute-start | bytes 565256 | tf_op jit(solution)/shard_map/ppermute | solution.py:273
  140.3 38.8 %collective-permute-start.58 = (bf16[46,16,128]{2,1,0:T(8,128)(2,1)}, bf16[46,16,128]{2,1,0:T(8,128)(2,1)S(1)}, u32[]{:S(2)}, u32[]{:S(2)}) collective-permute-start(bf16[46,16,128]{2,1,0:T(8,128)(2,1)} %copy-done.44), channel_id=1, source_target_pairs={{0,2},{1,3},{2,4},{3,5},{4,6},{5,7},{6,0},{7,1},{8,10},{9,11},{10,... | collective-permute-start | bytes 565256 | tf_op jit(solution)/shard_map/ppermute | solution.py:273
  143.8 35.3 %collective-permute-start.59 = (bf16[46,16,128]{2,1,0:T(8,128)(2,1)}, bf16[46,16,128]{2,1,0:T(8,128)(2,1)S(1)}, u32[]{:S(2)}, u32[]{:S(2)}) collective-permute-start(bf16[46,16,128]{2,1,0:T(8,128)(2,1)} %copy-done.43), channel_id=1, source_target_pairs={{0,3},{1,2},{2,5},{3,4},{4,7},{5,6},{6,1},{7,0},{8,11},{9,10},{10,... | collective-permute-start | bytes 565256 | tf_op jit(solution)/shard_map/ppermute | solution.py:273
  156.3 27.9 %collective-permute-start.14 = (bf16[4,45,16,128]{3,2,1,0:T(8,128)(2,1)S(1)}, bf16[4,45,16,128]{3,2,1,0:T(8,128)(2,1)S(1)}, u32[]{:S(2)}, u32[]{:S(2)}) collective-permute-start(bf16[4,45,16,128]{3,2,1,0:T(8,128)(2,1)S(1)} %get-tuple-element.92), channel_id=1, source_target_pairs={{0,8},{8,0},{16,24},{24,16},{32,40},{40,32},{48,56},{56,48},{64,72... | collective-permute-start | bytes 2211848 | tf_op jit(solution)/shard_map/ppermute | solution.py:305
  178.8 12.5 %collective-permute-start.37 = (bf16[4,46,16,128]{3,2,1,0:T(8,128)(2,1)S(1)}, bf16[4,46,16,128]{3,2,1,0:T(8,128)(2,1)S(1)}, u32[]{:S(2)}, u32[]{:S(2)}) collective-permute-start(bf16[4,46,16,128]{3,2,1,0:T(8,128)(2,1)S(1)} %get-tuple-element.115), channel_id=1, source_target_pairs={{0,8},{8,0},{16,24},{24,16},{32,40},{40,32},{48,56},{56,48},{64,72... | collective-permute-start | bytes 2261000 | tf_op jit(solution)/shard_map/ppermute | solution.py:305
  187.6 11.4 %collective-permute-start.16 = (bf16[45,16,128]{2,1,0:T(8,128)(2,1)S(1)}, bf16[45,16,128]{2,1,0:T(8,128)(2,1)S(1)}, u32[]{:S(2)}, u32[]{:S(2)}) collective-permute-start(bf16[45,16,128]{2,1,0:T(8,128)(2,1)S(1)} %get-tuple-element.95), channel_id=1, source_target_pairs={{0,64},{8,72},{16,80},{24,88},{32,96},{40,104},{48,112},{56,120},{... | collective-permute-start | bytes 552968 | tf_op jit(solution)/shard_map/ppermute | solution.py:307
  191.6 11.5 %collective-permute-start.38 = (bf16[46,16,128]{2,1,0:T(8,128)(2,1)S(1)}, bf16[46,16,128]{2,1,0:T(8,128)(2,1)S(1)}, u32[]{:S(2)}, u32[]{:S(2)}) collective-permute-start(bf16[46,16,128]{2,1,0:T(8,128)(2,1)S(1)} %get-tuple-element.117), channel_id=1, source_target_pairs={{0,32},{8,40},{16,48},{24,56},{32,64},{40,72},{48,80},{56,88},{64,... | collective-permute-start | bytes 565256 | tf_op jit(solution)/shard_map/ppermute | solution.py:307
  192.1 15.0 %collective-permute-start.39 = (bf16[46,16,128]{2,1,0:T(8,128)(2,1)S(1)}, bf16[46,16,128]{2,1,0:T(8,128)(2,1)S(1)}, u32[]{:S(2)}, u32[]{:S(2)}) collective-permute-start(bf16[46,16,128]{2,1,0:T(8,128)(2,1)S(1)} %get-tuple-element.118), channel_id=1, source_target_pairs={{0,64},{8,72},{16,80},{24,88},{32,96},{40,104},{48,112},{56,120},{... | collective-permute-start | bytes 565256 | tf_op jit(solution)/shard_map/ppermute | solution.py:307
  193.8 13.4 %collective-permute-start.40 = (bf16[46,16,128]{2,1,0:T(8,128)(2,1)S(1)}, bf16[46,16,128]{2,1,0:T(8,128)(2,1)S(1)}, u32[]{:S(2)}, u32[]{:S(2)}) collective-permute-start(bf16[46,16,128]{2,1,0:T(8,128)(2,1)S(1)} %get-tuple-element.119), channel_id=1, source_target_pairs={{0,96},{8,104},{16,112},{24,120},{32,0},{40,8},{48,16},{56,24},{64... | collective-permute-start | bytes 565256 | tf_op jit(solution)/shard_map/ppermute | solution.py:307
  198.9 12.1 %collective-permute-start.61 = (bf16[46,16,128]{2,1,0:T(8,128)(2,1)S(1)}, bf16[46,16,128]{2,1,0:T(8,128)(2,1)S(1)}, u32[]{:S(2)}, u32[]{:S(2)}) collective-permute-start(bf16[46,16,128]{2,1,0:T(8,128)(2,1)S(1)} %get-tuple-element.140), channel_id=1, source_target_pairs={{0,32},{8,40},{16,48},{24,56},{32,64},{40,72},{48,80},{56,88},{64,... | collective-permute-start | bytes 565256 | tf_op jit(solution)/shard_map/ppermute | solution.py:307
  199.0 16.2 %collective-permute-start.62 = (bf16[46,16,128]{2,1,0:T(8,128)(2,1)S(1)}, bf16[46,16,128]{2,1,0:T(8,128)(2,1)S(1)}, u32[]{:S(2)}, u32[]{:S(2)}) collective-permute-start(bf16[46,16,128]{2,1,0:T(8,128)(2,1)S(1)} %get-tuple-element.141), channel_id=1, source_target_pairs={{0,64},{8,72},{16,80},{24,88},{32,96},{40,104},{48,112},{56,120},{... | collective-permute-start | bytes 565256 | tf_op jit(solution)/shard_map/ppermute | solution.py:307
  203.1 12.0 %collective-permute-start.63 = (bf16[46,16,128]{2,1,0:T(8,128)(2,1)S(1)}, bf16[46,16,128]{2,1,0:T(8,128)(2,1)S(1)}, u32[]{:S(2)}, u32[]{:S(2)}) collective-permute-start(bf16[46,16,128]{2,1,0:T(8,128)(2,1)S(1)} %get-tuple-element.142), channel_id=1, source_target_pairs={{0,96},{8,104},{16,112},{24,120},{32,0},{40,8},{48,16},{56,24},{64... | collective-permute-start | bytes 565256 | tf_op jit(solution)/shard_map/ppermute | solution.py:307
  207.1 13.9 %collective-permute-start.18 = (bf16[45,16,128]{2,1,0:T(8,128)(2,1)S(1)}, bf16[45,16,128]{2,1,0:T(8,128)(2,1)S(1)}, u32[]{:S(2)}, u32[]{:S(2)}) collective-permute-start(bf16[45,16,128]{2,1,0:T(8,128)(2,1)S(1)} %add_convert_fusion.5), channel_id=1, source_target_pairs={{0,16},{8,24},{16,0},{24,8},{32,48},{40,56},{48,32},{56,40},{64,80... | collective-permute-start | bytes 552968 | tf_op jit(solution)/shard_map/ppermute | solution.py:309
  220.8 12.2 %collective-permute-start.67 = (bf16[46,16,128]{2,1,0:T(8,128)(2,1)S(1)}, bf16[46,16,128]{2,1,0:T(8,128)(2,1)S(1)}, u32[]{:S(2)}, u32[]{:S(2)}) collective-permute-start(bf16[46,16,128]{2,1,0:T(8,128)(2,1)S(1)} %add_convert_fusion), channel_id=1, source_target_pairs={{0,32},{8,40},{16,48},{24,56},{32,64},{40,72},{48,80},{56,88},{64,... | collective-permute-start | bytes 565256 | tf_op jit(solution)/shard_map/ppermute | solution.py:311
  221.0 13.7 %collective-permute-start.66 = (bf16[46,16,128]{2,1,0:T(8,128)(2,1)S(1)}, bf16[46,16,128]{2,1,0:T(8,128)(2,1)S(1)}, u32[]{:S(2)}, u32[]{:S(2)}) collective-permute-start(bf16[46,16,128]{2,1,0:T(8,128)(2,1)S(1)} %add_convert_fusion), channel_id=1, source_target_pairs={{0,64},{8,72},{16,80},{24,88},{32,96},{40,104},{48,112},{56,120},{... | collective-permute-start | bytes 565256 | tf_op jit(solution)/shard_map/ppermute | solution.py:311
  224.6 13.9 %collective-permute-start.65 = (bf16[46,16,128]{2,1,0:T(8,128)(2,1)S(1)}, bf16[46,16,128]{2,1,0:T(8,128)(2,1)S(1)}, u32[]{:S(2)}, u32[]{:S(2)}) collective-permute-start(bf16[46,16,128]{2,1,0:T(8,128)(2,1)S(1)} %add_convert_fusion), channel_id=1, source_target_pairs={{0,96},{8,104},{16,112},{24,120},{32,0},{40,8},{48,16},{56,24},{64... | collective-permute-start | bytes 565256 | tf_op jit(solution)/shard_map/ppermute | solution.py:311
  226.6 14.4 %collective-permute-start.21 = (bf16[45,16,128]{2,1,0:T(8,128)(2,1)S(1)}, bf16[45,16,128]{2,1,0:T(8,128)(2,1)S(1)}, u32[]{:S(2)}, u32[]{:S(2)}) collective-permute-start(bf16[45,16,128]{2,1,0:T(8,128)(2,1)S(1)} %add_convert_fusion.4), channel_id=1, source_target_pairs={{0,32},{8,40},{16,48},{24,56},{32,64},{40,72},{48,80},{56,88},{64,... | collective-permute-start | bytes 552968 | tf_op jit(solution)/shard_map/ppermute | solution.py:311
  228.0 14.6 %collective-permute-start.20 = (bf16[45,16,128]{2,1,0:T(8,128)(2,1)S(1)}, bf16[45,16,128]{2,1,0:T(8,128)(2,1)S(1)}, u32[]{:S(2)}, u32[]{:S(2)}) collective-permute-start(bf16[45,16,128]{2,1,0:T(8,128)(2,1)S(1)} %add_convert_fusion.4), channel_id=1, source_target_pairs={{0,64},{8,72},{16,80},{24,88},{32,96},{40,104},{48,112},{56,120},{... | collective-permute-start | bytes 552968 | tf_op jit(solution)/shard_map/ppermute | solution.py:311
  234.6 12.7 %collective-permute-start.45 = (bf16[4,46,16,128]{3,2,1,0:T(8,128)(2,1)S(1)}, bf16[4,46,16,128]{3,2,1,0:T(8,128)(2,1)S(1)}, u32[]{:S(2)}, u32[]{:S(2)}) collective-permute-start(bf16[4,46,16,128]{3,2,1,0:T(8,128)(2,1)S(1)} %pad_maximum_fusion.mine_ref), channel_id=1, source_target_pairs={{0,8},{8,0},{16,24},{24,16},{32,40},{40,32},{48,56},{56,48},{64,72... | collective-permute-start | bytes 2261000 | tf_op jit(solution)/shard_map/ppermute | solution.py:313
  (76 other events, 531.9 us)

commit v3 on v2

v3 whole, which is shorter than its diff:
```python
import math

import jax
import jax.numpy as jnp
import numpy as np
from jax import lax
from jax.experimental import pallas as pl
from jax.experimental.pallas import tpu as pltpu
from jax.sharding import PartitionSpec as P

BF16, F32 = jnp.bfloat16, jnp.float32
LANES = 128
VMEM_LIMIT = 20 * 1024 * 1024
CHUNKS = (46, 46, 45)
STEP = 23


def wave_table(length):
    ranks = np.arange(length)[:, None]
    middle = length // 2
    wavenumber = np.where(ranks <= middle, ranks, ranks - middle)
    angles = wavenumber * np.arange(length)[None, :] % length * (2.0 * math.pi / length)
    edge, inner = 1.0 / math.sqrt(length), math.sqrt(2.0 / length)
    values = np.where(
        ranks == 0,
        edge,
        np.where(
            ranks < middle,
            inner * np.cos(angles),
            np.where(ranks == middle, edge * np.cos(angles), inner * np.sin(angles)),
        ),
    )
    return values.astype(jnp.bfloat16)


def params():
    return pltpu.CompilerParams(vmem_limit_bytes=VMEM_LIMIT)


def mix_kernel(vertical_ref, member_ref, increment_ref, *refs):
    *out_refs, rows, mixed = refs
    levels, stored, _ = member_ref.shape
    tiles = rows.shape[0]
    product = member_ref[...].astype(F32) * increment_ref[...].astype(F32)
    product = product.reshape(levels * stored, tiles * LANES)
    for t in range(tiles):
        rows[t] = product[:, t * LANES : (t + 1) * LANES]
    vertical = vertical_ref[...]
    for p in range(stored):
        at = pl.ds(p, levels, stride=stored)
        block = jnp.concatenate([rows[t, at, :] for t in range(tiles)], axis=1).astype(BF16)
        block = jnp.dot(vertical, block, preferred_element_type=F32)
        for t in range(tiles):
            mixed[t, at, :] = block[:, t * LANES : (t + 1) * LANES]
    start = 0
    for out_ref in out_refs:
        size = out_ref.shape[0]
        for t in range(tiles):
            part = mixed[t, start * stored : (start + size) * stored, :].astype(BF16)
            out_ref[:, :, t * LANES : (t + 1) * LANES] = part.reshape(size, stored, LANES)
        start += size


def mix(vertical, member, increment, chunks, width=256):
    levels, stored, columns = member.shape
    wide = lambda size: pl.BlockSpec((size, stored, width), lambda i: (0, 0, i))
    return pl.pallas_call(
        mix_kernel,
        grid=(columns // width,),
        in_specs=[pl.BlockSpec((levels, levels), lambda i: (0, 0)), wide(levels), wide(levels)],
        out_specs=[wide(size) for size in chunks],
        out_shape=[jax.ShapeDtypeStruct((size, stored, columns), BF16) for size in chunks],
        scratch_shapes=[pltpu.VMEM((width // LANES, levels * stored, LANES), F32)] * 2,
        compiler_params=params(),
        name="mix",
    )(vertical, *[pltpu.with_memory_space_constraint(a, pltpu.HBM) for a in (member, increment)])


def cost(flops, values):
    return pl.CostEstimate(flops=flops, bytes_accessed=2 * values, transcendentals=0)


def at_tile(tile):
    return pl.ds(pl.multiple_of(tile * LANES, LANES), LANES)


def forward_kernel(basis_ref, x_ref, out_ref):
    step, stored, columns = x_ref.shape
    coeffs = jnp.dot(
        x_ref[...].reshape(step * stored, columns), basis_ref[...], preferred_element_type=F32
    ).astype(BF16)
    for d in range(out_ref.shape[0]):
        out_ref[d] = coeffs[:, d * LANES : (d + 1) * LANES].reshape(step, stored, LANES)


def forward(basis, x):
    size, stored, columns = x.shape
    parts = columns // LANES
    step = min(STEP, size)
    return pl.pallas_call(
        forward_kernel,
        grid=(pl.cdiv(size, step),),
        in_specs=[
            pl.BlockSpec((columns, columns), lambda i: (0, 0)),
            pl.BlockSpec((step, stored, columns), lambda i: (i, 0, 0)),
        ],
        out_specs=pl.BlockSpec((parts, step, stored, LANES), lambda i: (0, i, 0, 0)),
        out_shape=jax.ShapeDtypeStruct((parts, size, stored, LANES), BF16),
        compiler_params=params(),
        cost_estimate=cost(2 * x.size * columns, 2 * x.size + basis.size),
        name="forward",
    )(basis, x)


def filter_kernel(basis_ref, basis_t_ref, weights_ref, x_ref, out_ref):
    parts, step, stored, width = x_ref.shape
    x = jnp.concatenate([x_ref[:, l].reshape(parts * stored, width) for l in range(step)], axis=1)
    spectral = jnp.dot(basis_ref[...], x, preferred_element_type=F32)
    weights = jnp.concatenate([weights_ref[...]] * step, axis=1)
    damped = (spectral * weights).astype(BF16)
    back = jnp.dot(basis_t_ref[...], damped, preferred_element_type=F32).astype(BF16)
    for l in range(step):
        out_ref[:, l] = back[:, l * width : (l + 1) * width].reshape(parts, stored, width)


def filter_rows(basis, basis_t, weights, x):
    parts, size, stored, width = x.shape
    step = min(STEP, size)
    whole = lambda a: pl.BlockSpec(a.shape, lambda i: (0, 0))
    block = pl.BlockSpec((parts, step, stored, width), lambda i: (0, i, 0, 0))
    return pl.pallas_call(
        filter_kernel,
        grid=(pl.cdiv(size, step),),
        in_specs=[whole(basis), whole(basis_t), whole(weights), block],
        out_specs=block,
        out_shape=jax.ShapeDtypeStruct(x.shape, BF16),
        compiler_params=params(),
        cost_estimate=cost(4 * parts * stored * x.size, 2 * x.size),
        name="filter",
    )(basis, basis_t, weights, x)


def backward_kernel(tiles_ref, basis_ref, member_ref, x_ref, keep_ref, give_ref, held):
    parts, step, stored, width = x_ref.shape
    x = jnp.concatenate([x_ref[d].reshape(step * stored, width) for d in range(parts)], axis=1)
    gridded = jnp.dot(x, basis_ref[...], preferred_element_type=F32)
    held[...] = (member_ref[...].astype(F32).reshape(gridded.shape) * gridded).astype(BF16)
    half = parts // 2
    for q in range(half):
        keep_ref[q] = held[:, at_tile(tiles_ref[q])].reshape(step, stored, width)
        give_ref[q] = held[:, at_tile(tiles_ref[half + q])].reshape(step, stored, width)


def backward(tiles, basis, member, x, start):
    parts, size, stored, width = x.shape
    columns = parts * width
    step = min(STEP, size)
    first = start // step
    assert first * step == start
    half = pl.BlockSpec((parts // 2, step, stored, width), lambda i, *_: (0, i, 0, 0))
    total = x.size
    return pl.pallas_call(
        backward_kernel,
        grid_spec=pltpu.PrefetchScalarGridSpec(
            num_scalar_prefetch=1,
            grid=(pl.cdiv(size, step),),
            in_specs=[
                pl.BlockSpec((columns, columns), lambda i, *_: (0, 0)),
                pl.BlockSpec((step, stored, columns), lambda i, *_: (first + i, 0, 0)),
                pl.BlockSpec((parts, step, stored, width), lambda i, *_: (0, i, 0, 0)),
            ],
            out_specs=[half] * 2,
            scratch_shapes=[pltpu.VMEM((step * stored, columns), BF16)],
        ),
        out_shape=[jax.ShapeDtypeStruct((parts // 2, size, stored, width), BF16)] * 2,
        compiler_params=params(),
        cost_estimate=cost(2 * total * columns, 3 * total + basis.size),
        name="backward",
    )(tiles, basis, pltpu.with_memory_space_constraint(member, pltpu.HBM), x)


def pair_kernel(a_ref, b_ref, *out_refs):
    for q, out_ref in enumerate(out_refs):
        out_ref[...] = (a_ref[q].astype(F32) + b_ref[q].astype(F32)).astype(BF16)


def pair_sum(a, b):
    parts, size, stored, width = a.shape
    step = min(STEP, size)
    block = pl.BlockSpec((parts, step, stored, width), lambda i: (0, i, 0, 0))
    return pl.pallas_call(
        pair_kernel,
        grid=(pl.cdiv(size, step),),
        in_specs=[block] * 2,
        out_specs=[pl.BlockSpec((step, stored, width), lambda i: (i, 0, 0))] * parts,
        out_shape=[jax.ShapeDtypeStruct(a.shape[1:], BF16)] * parts,
        compiler_params=params(),
        cost_estimate=cost(a.size, 3 * a.size),
        name="pair_sum",
    )(a, b)


def place_kernel(tiles_ref, mine_ref, theirs_ref, *refs):
    out_ref = refs[-1]
    half = mine_ref.shape[0]
    for q in range(half):
        out_ref[:, :, at_tile(tiles_ref[q])] = mine_ref[q]
        out_ref[:, :, at_tile(tiles_ref[half + q])] = theirs_ref[q]


def place(tiles, mine, theirs, out, start, levels):
    half, size, stored, width = mine.shape
    columns = 2 * half * width
    step = min(STEP, size)
    first = start // step
    block = pl.BlockSpec((half, step, stored, width), lambda i, *_: (0, i, 0, 0))
    held = [] if out is None else [out]
    return pl.pallas_call(
        place_kernel,
        grid_spec=pltpu.PrefetchScalarGridSpec(
            num_scalar_prefetch=1,
            grid=(pl.cdiv(size, step),),
            in_specs=[block] * 2 + [pl.BlockSpec(memory_space=pl.ANY)] * len(held),
            out_specs=pl.BlockSpec((step, stored, columns), lambda i, *_: (first + i, 0, 0)),
        ),
        out_shape=jax.ShapeDtypeStruct((levels, stored, columns), BF16),
        input_output_aliases={3: 0} if held else {},
        compiler_params=params(),
        cost_estimate=cost(0, 4 * mine.size),
        name="place",
    )(tiles, mine, theirs, *held)


Y, XLO, CORE, Z, XHI = 4, 2, 2, 4, 2


def space_to(dz, dx):
    return [(z * XHI + x, (z + dz) % Z * XHI + (x ^ dx)) for z in range(Z) for x in range(XHI)]


def mem_to(dy, dx, dc):
    return [
        ((y * XLO + x) * CORE + c, ((y + dy) % Y * XLO + (x ^ dx)) * CORE + (c ^ dc))
        for y in range(Y)
        for x in range(XLO)
        for c in range(CORE)
    ]


def swap(pieces):
    return lax.all_to_all(pieces, "space", 0, 0, tiled=True)


tie = lax.optimization_barrier


def add(*terms):
    return sum(t.astype(F32) for t in terms).astype(BF16)


def shards(members, increment, vertical, spectral_weights, tile_rows):
    levels, stored, columns = increment.shape
    member = members[0]
    table = wave_table(columns)
    basis_x, basis_xt = jnp.asarray(table), jnp.asarray(np.ascontiguousarray(table.T))
    space, mem = lax.axis_index("space"), lax.axis_index("mem")
    z, x, y, core = space // XHI, space % XHI, mem // (XLO * CORE), mem % CORE
    tiles = jnp.stack(
        [(core ^ dc) * Y + (y + dy) % Y for dc in range(CORE) for dy in range(Y)]
    ).astype(jnp.int32)
    rows = tile_rows.shape[0]
    held = tile_rows[None, :]
    chosen = (lax.broadcasted_iota(jnp.int32, (rows, rows), 0) == held).astype(BF16)
    basis_y = jnp.dot(jnp.asarray(wave_table(rows)), chosen, preferred_element_type=F32).astype(BF16)
    basis_yt = basis_y.T
    localized = mix(vertical, member, increment, CHUNKS)
    starts = [sum(CHUNKS[:i]) for i in range(len(CHUNKS))]

    def spread(i):
        return forward(basis_xt, localized[i])

    def damp(pieces):
        return filter_rows(basis_y, basis_yt, spectral_weights, pieces)

    def fold(keep, give):
        return keep, pair_sum(keep, lax.ppermute(give, "mem", mem_to(0, 0, 1)))

    def along_y(keep):
        part = add(
            keep[0], *[lax.ppermute(keep[dy], "mem", mem_to(dy, 0, 0)) for dy in range(1, Y)]
        )
        return add(part, lax.ppermute(part, "mem", mem_to(0, 1, 0)))

    def spread_y(part):
        mine = jnp.stack(
            [part] + [lax.ppermute(part, "mem", mem_to(-dy, 0, 0)) for dy in range(1, Y)]
        )
        return mine, lax.ppermute(mine, "mem", mem_to(0, 0, 1))

    c0 = spread(0)
    r0 = swap(c0)
    c1 = spread(1)
    r1 = swap(c1)
    c2 = spread(2)
    r0, c2 = tie((r0, c2))
    g0 = damp(r0)
    s0 = swap(g0)
    r1, g0, c2 = tie((r1, g0, c2))
    g1 = damp(r1)
    r2 = swap(c2)
    s0, g1 = tie((s0, g1))
    s1 = swap(g1)
    keep0, give0 = backward(tiles, basis_x, member, s0, starts[0])
    keep0, half0 = fold(keep0, give0)
    r2, half0 = tie((r2, half0))
    g2 = damp(r2)
    s2 = swap(g2)
    sum0 = along_y(half0)
    s1, sum0 = tie((s1, sum0))
    keep1, give1 = backward(tiles, basis_x, member, s1, starts[1])
    keep1, half1 = fold(keep1, give1)
    done0 = spread_y(sum0)
    s2, half1, done0 = tie((s2, half1, done0))
    keep2, give2 = backward(tiles, basis_x, member, s2, starts[2])
    keep2, half2 = fold(keep2, give2)
    done1 = spread_y(along_y(half1))
    done2 = spread_y(along_y(half2))
    out = None
    for i, (mine, theirs) in enumerate((done0, done1, done2)):
        out = place(tiles, mine, theirs, out, starts[i], levels)
    return out


def solution(mesh):
    return jax.shard_map(
        shards,
        mesh=mesh,
        in_specs=(
            P("mem", None, "space", None),
            P(None, "space", None),
            P(),
            P(None, "space"),
            P(),
        ),
        out_specs=P(None, "space", None),
        check_vma=False,
    )
```

time: 253 us -> 225 us (0.89)
  waiting for transfers between devices: 34.2 us -> 83 us
  starting transfers between devices: 121 us -> 76 us
  local copies, waits for them, and re-layouts: 41.7 us -> 16.9 us
  Pallas kernels: 53.5 us -> 47 us
    ppermute x69 -> x27, starting transfers between devices: 121 us -> 45.2 us  [the longest x9 13 us: along_y(): lax.ppermute(keep[dy], 'mem', mem_to(dy, 0, 0))]
    all_to_all x0 -> x6, waiting for transfers between devices: none -> 58.7 us  [swap(): return lax.all_to_all(pieces, 'space', 0, 0, tiled=True)]
    all_to_all x0 -> x6, starting transfers between devices: none -> 30.7 us  [swap(): return lax.all_to_all(pieces, 'space', 0, 0, tiled=True)]
    unnamed x110 -> x42, local copies, waits for them, and re-layouts: 40.6 us -> 16.7 us
    ppermute x69 -> x27, waiting for transfers between devices: 34.2 us -> 24.4 us  [the longest x9 15 us: along_y(): lax.ppermute(keep[dy], 'mem', mem_to(dy, 0, 0))]
    pallas_call x3, Pallas kernels: 12.1 us -> 7.06 us  [forward(): pl.pallas_call(forward_kernel, grid=(pl.cdiv(size, step),), in_specs=[pl....]
    pallas_call x3, Pallas kernels: 8.42 us -> 5.22 us  [filter_rows(): pl.pallas_call(filter_kernel, grid=(pl.cdiv(size, step),), in_specs=[whol...]
  transfers between devices with their start and end apart: 69 -> 33, of which waited for: 16 -> 16; matrix products, arithmetic and copies ran while one was open for 1% -> 1% of each run, Pallas kernels for 14% -> 12%
where the time goes in v3:
time: 225 us; the launch traced here: 224 us
  waiting for transfers between devices  83 us (37%)
  starting transfers between devices  76 us (34%)
  Pallas kernels  47 us (21%)
  local copies, waits for them, and re-layouts  16.9 us (8%)
    all_to_all x6, waiting for transfers between devices, swap(): return lax.all_to_all(pieces, 'space', 0, 0, tiled=True)  58.7 us
    all_to_all x6, starting transfers between devices, swap(): return lax.all_to_all(pieces, 'space', 0, 0, tiled=True)  30.7 us
    unnamed x42, local copies, waits for them, and re-layouts  16.7 us
    ppermute x9, waiting for transfers between devices, along_y(): lax.ppermute(keep[dy], 'mem', mem_to(dy, 0, 0))  15 us
    pallas_call x3, Pallas kernels, backward(): pl.pallas_call(backward_kernel, grid_spec=pltpu.PrefetchScalarGridSpec(nu...  14 us
    ppermute x9, starting transfers between devices, along_y(): lax.ppermute(keep[dy], 'mem', mem_to(dy, 0, 0))  13 us
    ppermute x9, starting transfers between devices, spread_y(): lax.ppermute(part, 'mem', mem_to(-dy, 0, 0))  13 us
    ppermute x3, starting transfers between devices, fold(): return (keep, pair_sum(keep, lax.ppermute(give, 'mem', mem_to(0, 0, 1))))  12.7 us
  transfers between devices with their start and end apart: 33, of which 16 were waited for; matrix products, arithmetic and copies ran while one was open for 1% of the time, Pallas kernels for 12%

profile of v3, /device:TPU:1, one launch (start us, length us, event | category | flops | bytes accessed | tf_op | source)
XLA Modules:
  0.0 224.3 jit_solution(10131474730449894303)
XLA Ops:
  0.9 9.7 %mix.1 = (bf16[46,16,1024]{2,1,0:T(8,128)(2,1)S(1)}, bf16[46,16,1024]{2,1,0:T(8,128)(2,1)S(1)}, bf16[45,16,1024]{2,1,0:T(8,128)(2,1)S(1)}) custom-call(bf16[137,137]{1,0:T(8,128)(2,1)S(1)} %copy-done.11, bf16[137,16,1024]{2,1,0:T(8,128)(2,1)} %bitcast.24, bf16[137,16,1024]{2,1,0:T(8,128)(2,1)} %increment_ref.1), custom_call_target="tpu_custom_call" | custom-call | tf_op jit(solution)/shard_map/mix/pallas_call | solution.py:67
  11.8 2.8 %forward.4 = bf16[8,46,16,128]{3,2,1,0:T(8,128)(2,1)} custom-call(bf16[1024,1024]{1,0:T(8,128)(2,1)S(1)} %copy-done.16, bf16[46,16,1024]{2,1,0:T(8,128)(2,1)S(1)} %get-tuple-element.47.x_ref), custom_call_target="tpu_custom_call" | custom-call | flops 1543503872 | bytes 5111808 | tf_op jit(solution)/shard_map/forward/pallas_call | solution.py:100
  14.6 8.3 %all-to-all-start.1 = ((bf16[8,46,16,128]{3,2,1,0:T(8,128)(2,1)}), bf16[8,46,16,128]{3,2,1,0:T(8,128)(2,1)S(1)}, u32[]{:S(2)}, u32[]{:S(2)}) async-start(bf16[8,46,16,128]{3,2,1,0:T(8,128)(2,1)} %forward.4), calls=%async_computation.1 | async-start | bytes 3014656 | tf_op jit(solution)/shard_map/all_to_all | solution.py:251
  22.9 1.6 copy-done.17
  24.5 2.0 forward.3
  27.6 16.5 %all-to-all-done.1.x_ref = bf16[8,46,16,128]{3,2,1,0:T(8,128)(2,1)S(1)} async-done(((bf16[8,46,16,128]{3,2,1,0:T(8,128)(2,1)}), bf16[8,46,16,128]{3,2,1,0:T(8,128)(2,1)S(1)}, u32[]{:S(2)}, u32[]{:S(2)}) %all-to-all-start.1) | async-done | bytes 1507360 | tf_op jit(solution)/shard_map/all_to_all | solution.py:251
  44.1 3.8 %all-to-all-start = ((bf16[8,46,16,128]{3,2,1,0:T(8,128)(2,1)}), bf16[8,46,16,128]{3,2,1,0:T(8,128)(2,1)S(1)}, u32[]{:S(2)}, u32[]{:S(2)}) async-start(bf16[8,46,16,128]{3,2,1,0:T(8,128)(2,1)} %copy-done.8), calls=%async_computation | async-start | bytes 3014656 | tf_op jit(solution)/shard_map/all_to_all | solution.py:251
  48.3 1.4 copy-done.13
  49.6 1.6 copy-done.18
  51.2 2.3 %forward.5 = bf16[8,45,16,128]{3,2,1,0:T(8,128)(2,1)S(1)} custom-call(bf16[1024,1024]{1,0:T(8,128)(2,1)S(1)} %copy-done.18, bf16[45,16,1024]{2,1,0:T(8,128)(2,1)S(1)} %copy-done.13), custom_call_target="tpu_custom_call" | custom-call | flops 1509949440 | bytes 5046272 | tf_op jit(solution)/shard_map/forward/pallas_call | solution.py:100
  57.1 11.1 %all-to-all-done.x_ref = bf16[8,46,16,128]{3,2,1,0:T(8,128)(2,1)S(1)} async-done(((bf16[8,46,16,128]{3,2,1,0:T(8,128)(2,1)}), bf16[8,46,16,128]{3,2,1,0:T(8,128)(2,1)S(1)}, u32[]{:S(2)}, u32[]{:S(2)}) %all-to-all-start) | async-done | bytes 1507360 | tf_op jit(solution)/shard_map/all_to_all | solution.py:251
  69.3 4.8 %all-to-all-start.3 = ((bf16[8,46,16,128]{3,2,1,0:T(8,128)(2,1)}), bf16[8,46,16,128]{3,2,1,0:T(8,128)(2,1)S(1)}, u32[]{:S(2)}, u32[]{:S(2)}) async-start(bf16[8,46,16,128]{3,2,1,0:T(8,128)(2,1)} %copy-done.6), calls=%async_computation.3 | async-start | bytes 3014656 | tf_op jit(solution)/shard_map/all_to_all | solution.py:251
  74.1 20.3 %all-to-all-done.3.x_ref = bf16[8,46,16,128]{3,2,1,0:T(8,128)(2,1)S(1)} async-done(((bf16[8,46,16,128]{3,2,1,0:T(8,128)(2,1)}), bf16[8,46,16,128]{3,2,1,0:T(8,128)(2,1)S(1)}, u32[]{:S(2)}, u32[]{:S(2)}) %all-to-all-start.3) | async-done | bytes 1507360 | tf_op jit(solution)/shard_map/all_to_all | solution.py:251
  94.4 4.7 %all-to-all-start.2 = ((bf16[8,45,16,128]{3,2,1,0:T(8,128)(2,1)}), bf16[8,45,16,128]{3,2,1,0:T(8,128)(2,1)}, u32[]{:S(2)}, u32[]{:S(2)}) async-start(bf16[8,45,16,128]{3,2,1,0:T(8,128)(2,1)} %copy-done.9), calls=%async_computation.2 | async-start | bytes 2949120 | tf_op jit(solution)/shard_map/all_to_all | solution.py:251
  99.3 1.4 copy-done.2
  103.1 1.4 copy-done.4
  104.5 4.8 %backward.3 = (bf16[4,46,16,128]{3,2,1,0:T(8,128)(2,1)S(1)}, bf16[4,46,16,128]{3,2,1,0:T(8,128)(2,1)}) custom-call(s32[8]{0:T(128)S(1)} %stack.80.tiles_ref, bf16[1024,1024]{1,0:T(8,128)(2,1)S(1)} %copy-done, bf16[137,16,1024]{2,1,0:T(8,128)(2,1)} %bitcast.25, bf16[8,46,16,128]{3,2,1,0:T(8,128)(2,1)S(1)} %copy-done.4), custom_call_target="tpu_custom_call" | custom-call | flops 1543503872 | bytes 6619136 | tf_op jit(solution)/shard_map/backward/pallas_call | solution.py:162
  109.3 2.4 %collective-permute-start = (bf16[4,46,16,128]{3,2,1,0:T(8,128)(2,1)}, bf16[4,46,16,128]{3,2,1,0:T(8,128)(2,1)}, u32[]{:S(2)}, u32[]{:S(2)}) collective-permute-start(bf16[4,46,16,128]{3,2,1,0:T(8,128)(2,1)} %get-tuple-element.55), channel_id=1, source_target_pairs={{0,8},{8,0},{16,24},{24,16},{32,40},{40,32},{48,56},{56,48},{64,72... | collective-permute-start | bytes 2261000 | tf_op jit(solution)/shard_map/ppermute | solution.py:286
  111.7 6.8 %all-to-all-done.2.x_ref = bf16[8,45,16,128]{3,2,1,0:T(8,128)(2,1)} async-done(((bf16[8,45,16,128]{3,2,1,0:T(8,128)(2,1)}), bf16[8,45,16,128]{3,2,1,0:T(8,128)(2,1)}, u32[]{:S(2)}, u32[]{:S(2)}) %all-to-all-start.2) | async-done | bytes 1474592 | tf_op jit(solution)/shard_map/all_to_all | solution.py:251
  118.5 4.7 %all-to-all-start.5 = ((bf16[8,46,16,128]{3,2,1,0:T(8,128)(2,1)}), bf16[8,46,16,128]{3,2,1,0:T(8,128)(2,1)}, u32[]{:S(2)}, u32[]{:S(2)}) async-start(bf16[8,46,16,128]{3,2,1,0:T(8,128)(2,1)} %copy-done.5), calls=%async_computation.5 | async-start | bytes 3014656 | tf_op jit(solution)/shard_map/all_to_all | solution.py:251
  124.5 1.4 collective-permute-start.1
  125.9 2.6 %collective-permute-start.2 = (bf16[46,16,128]{2,1,0:T(8,128)(2,1)S(1)}, bf16[46,16,128]{2,1,0:T(8,128)(2,1)S(1)}, u32[]{:S(2)}, u32[]{:S(2)}) collective-permute-start(bf16[46,16,128]{2,1,0:T(8,128)(2,1)S(1)} %get-tuple-element.64), channel_id=1, source_target_pairs={{0,64},{8,72},{16,80},{24,88},{32,96},{40,104},{48,112},{56,120},{... | collective-permute-start | bytes 565256 | tf_op jit(solution)/shard_map/ppermute | solution.py:290
  130.3 4.1 %collective-permute-done.2 = bf16[46,16,128]{2,1,0:T(8,128)(2,1)S(1)} collective-permute-done((bf16[46,16,128]{2,1,0:T(8,128)(2,1)S(1)}, bf16[46,16,128]{2,1,0:T(8,128)(2,1)S(1)}, u32[]{:S(2)}, u32[]{:S(2)}) %collective-permute-start.2) | collective-permute-done | bytes 188448 | tf_op jit(solution)/shard_map/ppermute | solution.py:290
  134.6 2.6 %filter.5 = bf16[8,45,16,128]{3,2,1,0:T(8,128)(2,1)S(1)} custom-call(bf16[128,128]{1,0:T(8,128)(2,1)S(1)} %copy.13.basis_ref, bf16[128,128]{1,0:T(8,128)(2,1)S(1)} %convolution_convert_fusion.basis_t_ref, f32[128,128]{1,0:T(8,128)S(1)} %copy-done.10, bf16[8,45,16,128]{3,2,1,0:T(8,128)(2,1)} %all-to-all-done.2.x_ref), custom_call_target="tpu_custom_call" | custom-call | flops 377487360 | bytes 2949120 | tf_op jit(solution)/shard_map/filter/pallas_call | solution.py:131
  138.3 3.9 %all-to-all-done.5.x_ref = bf16[8,46,16,128]{3,2,1,0:T(8,128)(2,1)} async-done(((bf16[8,46,16,128]{3,2,1,0:T(8,128)(2,1)}), bf16[8,46,16,128]{3,2,1,0:T(8,128)(2,1)}, u32[]{:S(2)}, u32[]{:S(2)}) %all-to-all-start.5) | async-done | bytes 1507360 | tf_op jit(solution)/shard_map/all_to_all | solution.py:251
  142.3 4.3 %all-to-all-start.4 = ((bf16[8,45,16,128]{3,2,1,0:T(8,128)(2,1)}), bf16[8,45,16,128]{3,2,1,0:T(8,128)(2,1)}, u32[]{:S(2)}, u32[]{:S(2)}) async-start(bf16[8,45,16,128]{3,2,1,0:T(8,128)(2,1)} %copy-done.7), calls=%async_computation.4 | async-start | bytes 2949120 | tf_op jit(solution)/shard_map/all_to_all | solution.py:251
  146.6 1.4 collective-permute-start.8
  148.0 2.6 %collective-permute-start.7 = (bf16[46,16,128]{2,1,0:T(8,128)(2,1)S(1)}, bf16[46,16,128]{2,1,0:T(8,128)(2,1)S(1)}, u32[]{:S(2)}, u32[]{:S(2)}) collective-permute-start(bf16[46,16,128]{2,1,0:T(8,128)(2,1)S(1)} %add_convert_fusion.2), channel_id=1, source_target_pairs={{0,64},{8,72},{16,80},{24,88},{32,96},{40,104},{48,112},{56,120},{... | collective-permute-start | bytes 565256 | tf_op jit(solution)/shard_map/ppermute | solution.py:296
  151.7 4.3 %backward.4 = (bf16[4,46,16,128]{3,2,1,0:T(8,128)(2,1)S(1)}, bf16[4,46,16,128]{3,2,1,0:T(8,128)(2,1)S(1)}) custom-call(s32[8]{0:T(128)S(1)} %stack.80.tiles_ref, bf16[1024,1024]{1,0:T(8,128)(2,1)S(1)} %copy-done, bf16[137,16,1024]{2,1,0:T(8,128)(2,1)} %bitcast.26, bf16[8,46,16,128]{3,2,1,0:T(8,128)(2,1)} %all-to-all-done.5.x_ref), custom_call_target="tpu_custom_call" | custom-call | flops 1543503872 | bytes 6619136 | tf_op jit(solution)/shard_map/backward/pallas_call | solution.py:162
  156.1 7.3 %collective-permute-start.5 = (bf16[4,46,16,128]{3,2,1,0:T(8,128)(2,1)S(1)}, bf16[4,46,16,128]{3,2,1,0:T(8,128)(2,1)S(1)}, u32[]{:S(2)}, u32[]{:S(2)}) collective-permute-start(bf16[4,46,16,128]{3,2,1,0:T(8,128)(2,1)S(1)} %get-tuple-element.68), channel_id=1, source_target_pairs={{0,8},{8,0},{16,24},{24,16},{32,40},{40,32},{48,56},{56,48},{64,72... | collective-permute-start | bytes 2261000 | tf_op jit(solution)/shard_map/ppermute | solution.py:286
  163.5 1.6 collective-permute-done.5.b_ref
  166.4 4.9 %backward.5 = (bf16[4,45,16,128]{3,2,1,0:T(8,128)(2,1)S(1)}, bf16[4,45,16,128]{3,2,1,0:T(8,128)(2,1)S(1)}) custom-call(s32[8]{0:T(128)S(1)} %stack.80.tiles_ref, bf16[1024,1024]{1,0:T(8,128)(2,1)S(1)} %copy-done, bf16[137,16,1024]{2,1,0:T(8,128)(2,1)} %bitcast.27, bf16[8,45,16,128]{3,2,1,0:T(8,128)(2,1)} %all-to-all-done.4.x_ref), custom_call_target="tpu_custom_call" | custom-call | flops 1509949440 | bytes 6520832 | tf_op jit(solution)/shard_map/backward/pallas_call | solution.py:162
  171.3 3.0 %collective-permute-start.10 = (bf16[4,45,16,128]{3,2,1,0:T(8,128)(2,1)S(1)}, bf16[4,45,16,128]{3,2,1,0:T(8,128)(2,1)S(1)}, u32[]{:S(2)}, u32[]{:S(2)}) collective-permute-start(bf16[4,45,16,128]{3,2,1,0:T(8,128)(2,1)S(1)} %get-tuple-element.76), channel_id=1, source_target_pairs={{0,8},{8,0},{16,24},{24,16},{32,40},{40,32},{48,56},{56,48},{64,72... | collective-permute-start | bytes 2211848 | tf_op jit(solution)/shard_map/ppermute | solution.py:286
  175.6 2.6 %collective-permute-start.20 = (bf16[46,16,128]{2,1,0:T(8,128)(2,1)S(1)}, bf16[46,16,128]{2,1,0:T(8,128)(2,1)S(1)}, u32[]{:S(2)}, u32[]{:S(2)}) collective-permute-start(bf16[46,16,128]{2,1,0:T(8,128)(2,1)S(1)} %get-tuple-element.83), channel_id=1, source_target_pairs={{0,64},{8,72},{16,80},{24,88},{32,96},{40,104},{48,112},{56,120},{... | collective-permute-start | bytes 565256 | tf_op jit(solution)/shard_map/ppermute | solution.py:290
  179.3 2.0 pair_sum.5
  182.6 1.7 collective-permute-start.13
  184.3 2.8 %collective-permute-done.20 = bf16[46,16,128]{2,1,0:T(8,128)(2,1)S(1)} collective-permute-done((bf16[46,16,128]{2,1,0:T(8,128)(2,1)S(1)}, bf16[46,16,128]{2,1,0:T(8,128)(2,1)S(1)}, u32[]{:S(2)}, u32[]{:S(2)}) %collective-permute-start.20) | collective-permute-done | bytes 188448 | tf_op jit(solution)/shard_map/ppermute | solution.py:290
  187.7 4.1 %collective-permute-done.11 = bf16[45,16,128]{2,1,0:T(8,128)(2,1)S(1)} collective-permute-done((bf16[45,16,128]{2,1,0:T(8,128)(2,1)S(1)}, bf16[45,16,128]{2,1,0:T(8,128)(2,1)S(1)}, u32[]{:S(2)}, u32[]{:S(2)}) %collective-permute-start.11) | collective-permute-done | bytes 184352 | tf_op jit(solution)/shard_map/ppermute | solution.py:290
  191.7 3.3 %collective-permute-done.12 = bf16[45,16,128]{2,1,0:T(8,128)(2,1)S(1)} collective-permute-done((bf16[45,16,128]{2,1,0:T(8,128)(2,1)S(1)}, bf16[45,16,128]{2,1,0:T(8,128)(2,1)S(1)}, u32[]{:S(2)}, u32[]{:S(2)}) %collective-permute-start.12) | collective-permute-done | bytes 184352 | tf_op jit(solution)/shard_map/ppermute | solution.py:290
  196.1 2.9 %collective-permute-start.24 = (bf16[46,16,128]{2,1,0:T(8,128)(2,1)S(1)}, bf16[46,16,128]{2,1,0:T(8,128)(2,1)S(1)}, u32[]{:S(2)}, u32[]{:S(2)}) collective-permute-start(bf16[46,16,128]{2,1,0:T(8,128)(2,1)S(1)} %add_convert_fusion), channel_id=1, source_target_pairs={{0,64},{8,72},{16,80},{24,88},{32,96},{40,104},{48,112},{56,120},{... | collective-permute-start | bytes 565256 | tf_op jit(solution)/shard_map/ppermute | solution.py:296
  200.6 3.7 %collective-permute-start.16 = (bf16[45,16,128]{2,1,0:T(8,128)(2,1)S(1)}, bf16[45,16,128]{2,1,0:T(8,128)(2,1)S(1)}, u32[]{:S(2)}, u32[]{:S(2)}) collective-permute-start(bf16[45,16,128]{2,1,0:T(8,128)(2,1)S(1)} %add_convert_fusion.4), channel_id=1, source_target_pairs={{0,64},{8,72},{16,80},{24,88},{32,96},{40,104},{48,112},{56,120},{... | collective-permute-start | bytes 552968 | tf_op jit(solution)/shard_map/ppermute | solution.py:296
  204.3 2.8 %collective-permute-done.24 = bf16[46,16,128]{2,1,0:T(8,128)(2,1)S(1)} collective-permute-done((bf16[46,16,128]{2,1,0:T(8,128)(2,1)S(1)}, bf16[46,16,128]{2,1,0:T(8,128)(2,1)S(1)}, u32[]{:S(2)}, u32[]{:S(2)}) %collective-permute-start.24) | collective-permute-done | bytes 188448 | tf_op jit(solution)/shard_map/ppermute | solution.py:296
  207.2 3.7 %collective-permute-start.26 = (bf16[4,46,16,128]{3,2,1,0:T(8,128)(2,1)S(1)}, bf16[4,46,16,128]{3,2,1,0:T(8,128)(2,1)S(1)}, u32[]{:S(2)}, u32[]{:S(2)}) collective-permute-start(bf16[4,46,16,128]{3,2,1,0:T(8,128)(2,1)S(1)} %pad_maximum_fusion.1.mine_ref), channel_id=1, source_target_pairs={{0,8},{8,0},{16,24},{24,16},{32,40},{40,32},{48,56},{56,48},{64,72... | collective-permute-start | bytes 2261000 | tf_op jit(solution)/shard_map/ppermute | solution.py:298
  211.1 3.9 %collective-permute-done.16 = bf16[45,16,128]{2,1,0:T(8,128)(2,1)S(1)} collective-permute-done((bf16[45,16,128]{2,1,0:T(8,128)(2,1)S(1)}, bf16[45,16,128]{2,1,0:T(8,128)(2,1)S(1)}, u32[]{:S(2)}, u32[]{:S(2)}) %collective-permute-start.16) | collective-permute-done | bytes 184352 | tf_op jit(solution)/shard_map/ppermute | solution.py:296
  215.1 1.7 collective-permute-start.18
  216.8 2.9 %place.3.refs_0_ = bf16[137,16,1024]{2,1,0:T(8,128)(2,1)} custom-call(s32[8]{0:T(128)S(1)} %stack.80.tiles_ref, bf16[4,46,16,128]{3,2,1,0:T(8,128)(2,1)S(1)} %pad_maximum_fusion.mine_ref, bf16[4,46,16,128]{3,2,1,0:T(8,128)(2,1)} %collective-permute-done.9.theirs_ref), custom_call_target="tpu_custom_call" | custom-call | bytes 3014656 | tf_op jit(solution)/shard_map/place/pallas_call | solution.py:218
  219.7 2.0 place.4.refs_0_
  221.8 2.5 %place.5 = bf16[137,16,1024]{2,1,0:T(8,128)(2,1)} custom-call(s32[8]{0:T(128)S(1)} %stack.80.tiles_ref, bf16[4,45,16,128]{3,2,1,0:T(8,128)(2,1)S(1)} %pad_maximum_fusion.2.mine_ref, bf16[4,45,16,128]{3,2,1,0:T(8,128)(2,1)S(1)} %collective-permute-done.18.theirs_ref, bf16[137,16,1024]{2,1,0:T(8,128)(2,1)} %place.4.refs_0_), custom_call_target="tpu_custom_call", output_to_operand_aliasing={{}: (3, {})} | custom-call | bytes 2949120 | tf_op jit(solution)/shard_map/place/pallas_call | solution.py:218
  (88 shorter events, 24.7 us)
Async XLA Ops:
  0.9 10.9 %copy-start.16 = (bf16[1024,1024]{1,0:T(8,128)(2,1)S(1)}, bf16[1024,1024]{1,0:T(8,128)(2,1)}, u32[]{:S(2)}) copy-start(bf16[1024,1024]{1,0:T(8,128)(2,1)} %constant.69.clone.basis_ref) | copy-start | bytes 6291460
  10.6 1.1 copy-start.12
  14.6 29.5 %all-to-all-start.1 = ((bf16[8,46,16,128]{3,2,1,0:T(8,128)(2,1)}), bf16[8,46,16,128]{3,2,1,0:T(8,128)(2,1)S(1)}, u32[]{:S(2)}, u32[]{:S(2)}) async-start(bf16[8,46,16,128]{3,2,1,0:T(8,128)(2,1)} %forward.4), calls=%async_computation.1 | async-start | bytes 3014656 | tf_op jit(solution)/shard_map/all_to_all | solution.py:251
  22.9 1.6 copy-start.17
  26.5 1.1 copy-start.8
  27.6 20.3 %copy-start.19 = (bf16[128,128]{1,0:T(8,128)(2,1)S(1)}, bf16[128,128]{1,0:T(8,128)(2,1)}, u32[]{:S(2)}) copy-start(bf16[128,128]{1,0:T(8,128)(2,1)} %constant.70.clone) | copy-start | bytes 98308
  27.6 20.3 %copy-start.20 = (s32[128]{0:T(128)S(1)}, s32[128]{0:T(128)}, u32[]{:S(2)}) copy-start(s32[128]{0:T(128)} %param.12) | copy-start | bytes 1540
  44.1 24.1 %all-to-all-start = ((bf16[8,46,16,128]{3,2,1,0:T(8,128)(2,1)}), bf16[8,46,16,128]{3,2,1,0:T(8,128)(2,1)S(1)}, u32[]{:S(2)}, u32[]{:S(2)}) async-start(bf16[8,46,16,128]{3,2,1,0:T(8,128)(2,1)} %copy-done.8), calls=%async_computation | async-start | bytes 3014656 | tf_op jit(solution)/shard_map/all_to_all | solution.py:251
  48.3 1.4 copy-start.13
  49.6 1.6 copy-start.18
  51.2 3.4 %copy-start.10 = (f32[128,128]{1,0:T(8,128)S(1)}, f32[128,128]{1,0:T(8,128)}, u32[]{:S(2)}) copy-start(f32[128,128]{1,0:T(8,128)} %weights_ref.5) | copy-start | bytes 196612
  69.3 25.1 %all-to-all-start.3 = ((bf16[8,46,16,128]{3,2,1,0:T(8,128)(2,1)}), bf16[8,46,16,128]{3,2,1,0:T(8,128)(2,1)S(1)}, u32[]{:S(2)}, u32[]{:S(2)}) async-start(bf16[8,46,16,128]{3,2,1,0:T(8,128)(2,1)} %copy-done.6), calls=%async_computation.3 | async-start | bytes 3014656 | tf_op jit(solution)/shard_map/all_to_all | solution.py:251
  94.4 4.7 %copy-start.3 = (bf16[8,46,16,128]{3,2,1,0:T(8,128)(2,1)}, bf16[8,46,16,128]{3,2,1,0:T(8,128)(2,1)S(1)}, u32[]{:S(2)}) copy-start(bf16[8,46,16,128]{3,2,1,0:T(8,128)(2,1)S(1)} %all-to-all-done.3.x_ref) | copy-start | bytes 4521988
  94.4 24.1 %all-to-all-start.2 = ((bf16[8,45,16,128]{3,2,1,0:T(8,128)(2,1)}), bf16[8,45,16,128]{3,2,1,0:T(8,128)(2,1)}, u32[]{:S(2)}, u32[]{:S(2)}) async-start(bf16[8,45,16,128]{3,2,1,0:T(8,128)(2,1)} %copy-done.9), calls=%async_computation.2 | async-start | bytes 2949120 | tf_op jit(solution)/shard_map/all_to_all | solution.py:251
  99.3 1.4 copy-start.2
  100.7 2.4 %copy-start = (bf16[1024,1024]{1,0:T(8,128)(2,1)S(1)}, bf16[1024,1024]{1,0:T(8,128)(2,1)}, u32[]{:S(2)}) copy-start(bf16[1024,1024]{1,0:T(8,128)(2,1)} %constant.68.clone.basis_ref) | copy-start | bytes 6291460
  102.0 1.1 copy-start.5
  103.1 1.4 copy-start.4
  109.3 14.0 %collective-permute-start = (bf16[4,46,16,128]{3,2,1,0:T(8,128)(2,1)}, bf16[4,46,16,128]{3,2,1,0:T(8,128)(2,1)}, u32[]{:S(2)}, u32[]{:S(2)}) collective-permute-start(bf16[4,46,16,128]{3,2,1,0:T(8,128)(2,1)} %get-tuple-element.55), channel_id=1, source_target_pairs={{0,8},{8,0},{16,24},{24,16},{32,40},{40,32},{48,56},{56,48},{64,72... | collective-permute-start | bytes 2261000 | tf_op jit(solution)/shard_map/ppermute | solution.py:286
  118.5 23.8 %all-to-all-start.5 = ((bf16[8,46,16,128]{3,2,1,0:T(8,128)(2,1)}), bf16[8,46,16,128]{3,2,1,0:T(8,128)(2,1)}, u32[]{:S(2)}, u32[]{:S(2)}) async-start(bf16[8,46,16,128]{3,2,1,0:T(8,128)(2,1)} %copy-done.5), calls=%async_computation.5 | async-start | bytes 3014656 | tf_op jit(solution)/shard_map/all_to_all | solution.py:251
  124.5 5.8 %collective-permute-start.1 = (bf16[46,16,128]{2,1,0:T(8,128)(2,1)S(1)}, bf16[46,16,128]{2,1,0:T(8,128)(2,1)S(1)}, u32[]{:S(2)}, u32[]{:S(2)}) collective-permute-start(bf16[46,16,128]{2,1,0:T(8,128)(2,1)S(1)} %get-tuple-element.63), channel_id=1, source_target_pairs={{0,32},{8,40},{16,48},{24,56},{32,64},{40,72},{48,80},{56,88},{64,... | collective-permute-start | bytes 565256 | tf_op jit(solution)/shard_map/ppermute | solution.py:290
  125.9 8.5 %collective-permute-start.2 = (bf16[46,16,128]{2,1,0:T(8,128)(2,1)S(1)}, bf16[46,16,128]{2,1,0:T(8,128)(2,1)S(1)}, u32[]{:S(2)}, u32[]{:S(2)}) collective-permute-start(bf16[46,16,128]{2,1,0:T(8,128)(2,1)S(1)} %get-tuple-element.64), channel_id=1, source_target_pairs={{0,64},{8,72},{16,80},{24,88},{32,96},{40,104},{48,112},{56,120},{... | collective-permute-start | bytes 565256 | tf_op jit(solution)/shard_map/ppermute | solution.py:290
  128.5 5.9 %collective-permute-start.3 = (bf16[46,16,128]{2,1,0:T(8,128)(2,1)S(1)}, bf16[46,16,128]{2,1,0:T(8,128)(2,1)S(1)}, u32[]{:S(2)}, u32[]{:S(2)}) collective-permute-start(bf16[46,16,128]{2,1,0:T(8,128)(2,1)S(1)} %get-tuple-element.65), channel_id=1, source_target_pairs={{0,96},{8,104},{16,112},{24,120},{32,0},{40,8},{48,16},{56,24},{64... | collective-permute-start | bytes 565256 | tf_op jit(solution)/shard_map/ppermute | solution.py:290
  134.5 12.1 %collective-permute-start.4 = (bf16[46,16,128]{2,1,0:T(8,128)(2,1)S(1)}, bf16[46,16,128]{2,1,0:T(8,128)(2,1)S(1)}, u32[]{:S(2)}, u32[]{:S(2)}) collective-permute-start(bf16[46,16,128]{2,1,0:T(8,128)(2,1)S(1)} %add_convert_fusion.3), channel_id=1, source_target_pairs={{0,16},{8,24},{16,0},{24,8},{32,48},{40,56},{48,32},{56,40},{64,80... | collective-permute-start | bytes 565256 | tf_op jit(solution)/shard_map/ppermute | solution.py:292
  142.3 23.9 %all-to-all-start.4 = ((bf16[8,45,16,128]{3,2,1,0:T(8,128)(2,1)}), bf16[8,45,16,128]{3,2,1,0:T(8,128)(2,1)}, u32[]{:S(2)}, u32[]{:S(2)}) async-start(bf16[8,45,16,128]{3,2,1,0:T(8,128)(2,1)} %copy-done.7), calls=%async_computation.4 | async-start | bytes 2949120 | tf_op jit(solution)/shard_map/all_to_all | solution.py:251
  146.6 16.7 %collective-permute-start.8 = (bf16[46,16,128]{2,1,0:T(8,128)(2,1)S(1)}, bf16[46,16,128]{2,1,0:T(8,128)(2,1)S(1)}, u32[]{:S(2)}, u32[]{:S(2)}) collective-permute-start(bf16[46,16,128]{2,1,0:T(8,128)(2,1)S(1)} %add_convert_fusion.2), channel_id=1, source_target_pairs={{0,32},{8,40},{16,48},{24,56},{32,64},{40,72},{48,80},{56,88},{64,... | collective-permute-start | bytes 565256 | tf_op jit(solution)/shard_map/ppermute | solution.py:296
  148.0 15.3 %collective-permute-start.7 = (bf16[46,16,128]{2,1,0:T(8,128)(2,1)S(1)}, bf16[46,16,128]{2,1,0:T(8,128)(2,1)S(1)}, u32[]{:S(2)}, u32[]{:S(2)}) collective-permute-start(bf16[46,16,128]{2,1,0:T(8,128)(2,1)S(1)} %add_convert_fusion.2), channel_id=1, source_target_pairs={{0,64},{8,72},{16,80},{24,88},{32,96},{40,104},{48,112},{56,120},{... | collective-permute-start | bytes 565256 | tf_op jit(solution)/shard_map/ppermute | solution.py:296
  150.6 12.7 %collective-permute-start.6 = (bf16[46,16,128]{2,1,0:T(8,128)(2,1)S(1)}, bf16[46,16,128]{2,1,0:T(8,128)(2,1)S(1)}, u32[]{:S(2)}, u32[]{:S(2)}) collective-permute-start(bf16[46,16,128]{2,1,0:T(8,128)(2,1)S(1)} %add_convert_fusion.2), channel_id=1, source_target_pairs={{0,96},{8,104},{16,112},{24,120},{32,0},{40,8},{48,16},{56,24},{64... | collective-permute-start | bytes 565256 | tf_op jit(solution)/shard_map/ppermute | solution.py:296
  156.1 9.1 %collective-permute-start.5 = (bf16[4,46,16,128]{3,2,1,0:T(8,128)(2,1)S(1)}, bf16[4,46,16,128]{3,2,1,0:T(8,128)(2,1)S(1)}, u32[]{:S(2)}, u32[]{:S(2)}) collective-permute-start(bf16[4,46,16,128]{3,2,1,0:T(8,128)(2,1)S(1)} %get-tuple-element.68), channel_id=1, source_target_pairs={{0,8},{8,0},{16,24},{24,16},{32,40},{40,32},{48,56},{56,48},{64,72... | collective-permute-start | bytes 2261000 | tf_op jit(solution)/shard_map/ppermute | solution.py:286
  163.4 3.0 %collective-permute-start.9 = (bf16[4,46,16,128]{3,2,1,0:T(8,128)(2,1)S(1)}, bf16[4,46,16,128]{3,2,1,0:T(8,128)(2,1)}, u32[]{:S(2)}, u32[]{:S(2)}) collective-permute-start(bf16[4,46,16,128]{3,2,1,0:T(8,128)(2,1)S(1)} %pad_maximum_fusion.mine_ref), channel_id=1, source_target_pairs={{0,8},{8,0},{16,24},{24,16},{32,40},{40,32},{48,56},{56,48},{64,72... | collective-permute-start | bytes 2261000 | tf_op jit(solution)/shard_map/ppermute | solution.py:298
  166.4 7.9 %copy-start.15 = (bf16[46,16,128]{2,1,0:T(8,128)(2,1)S(1)}, bf16[46,16,128]{2,1,0:T(8,128)(2,1)}, u32[]{:S(2)}) copy-start(bf16[46,16,128]{2,1,0:T(8,128)(2,1)} %copy-done.14) | copy-start | bytes 565252
  171.3 8.0 %collective-permute-start.10 = (bf16[4,45,16,128]{3,2,1,0:T(8,128)(2,1)S(1)}, bf16[4,45,16,128]{3,2,1,0:T(8,128)(2,1)S(1)}, u32[]{:S(2)}, u32[]{:S(2)}) collective-permute-start(bf16[4,45,16,128]{3,2,1,0:T(8,128)(2,1)S(1)} %get-tuple-element.76), channel_id=1, source_target_pairs={{0,8},{8,0},{16,24},{24,16},{32,40},{40,32},{48,56},{56,48},{64,72... | collective-permute-start | bytes 2211848 | tf_op jit(solution)/shard_map/ppermute | solution.py:286
  174.3 8.3 %collective-permute-start.19 = (bf16[46,16,128]{2,1,0:T(8,128)(2,1)S(1)}, bf16[46,16,128]{2,1,0:T(8,128)(2,1)S(1)}, u32[]{:S(2)}, u32[]{:S(2)}) collective-permute-start(bf16[46,16,128]{2,1,0:T(8,128)(2,1)S(1)} %copy-done.15), channel_id=1, source_target_pairs={{0,32},{8,40},{16,48},{24,56},{32,64},{40,72},{48,80},{56,88},{64,... | collective-permute-start | bytes 565256 | tf_op jit(solution)/shard_map/ppermute | solution.py:290
  175.6 11.5 %collective-permute-start.20 = (bf16[46,16,128]{2,1,0:T(8,128)(2,1)S(1)}, bf16[46,16,128]{2,1,0:T(8,128)(2,1)S(1)}, u32[]{:S(2)}, u32[]{:S(2)}) collective-permute-start(bf16[46,16,128]{2,1,0:T(8,128)(2,1)S(1)} %get-tuple-element.83), channel_id=1, source_target_pairs={{0,64},{8,72},{16,80},{24,88},{32,96},{40,104},{48,112},{56,120},{... | collective-permute-start | bytes 565256 | tf_op jit(solution)/shard_map/ppermute | solution.py:290
  178.2 8.9 %collective-permute-start.21 = (bf16[46,16,128]{2,1,0:T(8,128)(2,1)S(1)}, bf16[46,16,128]{2,1,0:T(8,128)(2,1)S(1)}, u32[]{:S(2)}, u32[]{:S(2)}) collective-permute-start(bf16[46,16,128]{2,1,0:T(8,128)(2,1)S(1)} %get-tuple-element.84), channel_id=1, source_target_pairs={{0,96},{8,104},{16,112},{24,120},{32,0},{40,8},{48,16},{56,24},{64... | collective-permute-start | bytes 565256 | tf_op jit(solution)/shard_map/ppermute | solution.py:290
  181.3 10.4 %collective-permute-start.11 = (bf16[45,16,128]{2,1,0:T(8,128)(2,1)S(1)}, bf16[45,16,128]{2,1,0:T(8,128)(2,1)S(1)}, u32[]{:S(2)}, u32[]{:S(2)}) collective-permute-start(bf16[45,16,128]{2,1,0:T(8,128)(2,1)S(1)} %get-tuple-element.78), channel_id=1, source_target_pairs={{0,32},{8,40},{16,48},{24,56},{32,64},{40,72},{48,80},{56,88},{64,... | collective-permute-start | bytes 552968 | tf_op jit(solution)/shard_map/ppermute | solution.py:290
  181.8 13.2 %collective-permute-start.12 = (bf16[45,16,128]{2,1,0:T(8,128)(2,1)S(1)}, bf16[45,16,128]{2,1,0:T(8,128)(2,1)S(1)}, u32[]{:S(2)}, u32[]{:S(2)}) collective-permute-start(bf16[45,16,128]{2,1,0:T(8,128)(2,1)S(1)} %get-tuple-element.79), channel_id=1, source_target_pairs={{0,64},{8,72},{16,80},{24,88},{32,96},{40,104},{48,112},{56,120},{... | collective-permute-start | bytes 552968 | tf_op jit(solution)/shard_map/ppermute | solution.py:290
  182.6 12.4 %collective-permute-start.13 = (bf16[45,16,128]{2,1,0:T(8,128)(2,1)S(1)}, bf16[45,16,128]{2,1,0:T(8,128)(2,1)S(1)}, u32[]{:S(2)}, u32[]{:S(2)}) collective-permute-start(bf16[45,16,128]{2,1,0:T(8,128)(2,1)S(1)} %get-tuple-element.80), channel_id=1, source_target_pairs={{0,96},{8,104},{16,112},{24,120},{32,0},{40,8},{48,16},{56,24},{64... | collective-permute-start | bytes 552968 | tf_op jit(solution)/shard_map/ppermute | solution.py:290
  187.2 8.4 %collective-permute-start.22 = (bf16[46,16,128]{2,1,0:T(8,128)(2,1)S(1)}, bf16[46,16,128]{2,1,0:T(8,128)(2,1)S(1)}, u32[]{:S(2)}, u32[]{:S(2)}) collective-permute-start(bf16[46,16,128]{2,1,0:T(8,128)(2,1)S(1)} %add_convert_fusion.1), channel_id=1, source_target_pairs={{0,16},{8,24},{16,0},{24,8},{32,48},{40,56},{48,32},{56,40},{64,80... | collective-permute-start | bytes 565256 | tf_op jit(solution)/shard_map/ppermute | solution.py:292
  195.1 5.4 %collective-permute-start.14 = (bf16[45,16,128]{2,1,0:T(8,128)(2,1)S(1)}, bf16[45,16,128]{2,1,0:T(8,128)(2,1)S(1)}, u32[]{:S(2)}, u32[]{:S(2)}) collective-permute-start(bf16[45,16,128]{2,1,0:T(8,128)(2,1)S(1)} %add_convert_fusion.5), channel_id=1, source_target_pairs={{0,16},{8,24},{16,0},{24,8},{32,48},{40,56},{48,32},{56,40},{64,80... | collective-permute-start | bytes 552968 | tf_op jit(solution)/shard_map/ppermute | solution.py:292
  195.6 8.7 %collective-permute-start.25 = (bf16[46,16,128]{2,1,0:T(8,128)(2,1)S(1)}, bf16[46,16,128]{2,1,0:T(8,128)(2,1)S(1)}, u32[]{:S(2)}, u32[]{:S(2)}) collective-permute-start(bf16[46,16,128]{2,1,0:T(8,128)(2,1)S(1)} %add_convert_fusion), channel_id=1, source_target_pairs={{0,32},{8,40},{16,48},{24,56},{32,64},{40,72},{48,80},{56,88},{64,... | collective-permute-start | bytes 565256 | tf_op jit(solution)/shard_map/ppermute | solution.py:296
  196.1 11.0 %collective-permute-start.24 = (bf16[46,16,128]{2,1,0:T(8,128)(2,1)S(1)}, bf16[46,16,128]{2,1,0:T(8,128)(2,1)S(1)}, u32[]{:S(2)}, u32[]{:S(2)}) collective-permute-start(bf16[46,16,128]{2,1,0:T(8,128)(2,1)S(1)} %add_convert_fusion), channel_id=1, source_target_pairs={{0,64},{8,72},{16,80},{24,88},{32,96},{40,104},{48,112},{56,120},{... | collective-permute-start | bytes 565256 | tf_op jit(solution)/shard_map/ppermute | solution.py:296
  199.0 8.1 %collective-permute-start.23 = (bf16[46,16,128]{2,1,0:T(8,128)(2,1)S(1)}, bf16[46,16,128]{2,1,0:T(8,128)(2,1)S(1)}, u32[]{:S(2)}, u32[]{:S(2)}) collective-permute-start(bf16[46,16,128]{2,1,0:T(8,128)(2,1)S(1)} %add_convert_fusion), channel_id=1, source_target_pairs={{0,96},{8,104},{16,112},{24,120},{32,0},{40,8},{48,16},{56,24},{64... | collective-permute-start | bytes 565256 | tf_op jit(solution)/shard_map/ppermute | solution.py:296
  200.5 10.6 %collective-permute-start.17 = (bf16[45,16,128]{2,1,0:T(8,128)(2,1)S(1)}, bf16[45,16,128]{2,1,0:T(8,128)(2,1)S(1)}, u32[]{:S(2)}, u32[]{:S(2)}) collective-permute-start(bf16[45,16,128]{2,1,0:T(8,128)(2,1)S(1)} %add_convert_fusion.4), channel_id=1, source_target_pairs={{0,32},{8,40},{16,48},{24,56},{32,64},{40,72},{48,80},{56,88},{64,... | collective-permute-start | bytes 552968 | tf_op jit(solution)/shard_map/ppermute | solution.py:296
  200.6 14.4 %collective-permute-start.16 = (bf16[45,16,128]{2,1,0:T(8,128)(2,1)S(1)}, bf16[45,16,128]{2,1,0:T(8,128)(2,1)S(1)}, u32[]{:S(2)}, u32[]{:S(2)}) collective-permute-start(bf16[45,16,128]{2,1,0:T(8,128)(2,1)S(1)} %add_convert_fusion.4), channel_id=1, source_target_pairs={{0,64},{8,72},{16,80},{24,88},{32,96},{40,104},{48,112},{56,120},{... | collective-permute-start | bytes 552968 | tf_op jit(solution)/shard_map/ppermute | solution.py:296
  204.3 10.7 %collective-permute-start.15 = (bf16[45,16,128]{2,1,0:T(8,128)(2,1)S(1)}, bf16[45,16,128]{2,1,0:T(8,128)(2,1)S(1)}, u32[]{:S(2)}, u32[]{:S(2)}) collective-permute-start(bf16[45,16,128]{2,1,0:T(8,128)(2,1)S(1)} %add_convert_fusion.4), channel_id=1, source_target_pairs={{0,96},{8,104},{16,112},{24,120},{32,0},{40,8},{48,16},{56,24},{64... | collective-permute-start | bytes 552968 | tf_op jit(solution)/shard_map/ppermute | solution.py:296
  207.2 12.5 %collective-permute-start.26 = (bf16[4,46,16,128]{3,2,1,0:T(8,128)(2,1)S(1)}, bf16[4,46,16,128]{3,2,1,0:T(8,128)(2,1)S(1)}, u32[]{:S(2)}, u32[]{:S(2)}) collective-permute-start(bf16[4,46,16,128]{3,2,1,0:T(8,128)(2,1)S(1)} %pad_maximum_fusion.1.mine_ref), channel_id=1, source_target_pairs={{0,8},{8,0},{16,24},{24,16},{32,40},{40,32},{48,56},{56,48},{64,72... | collective-permute-start | bytes 2261000 | tf_op jit(solution)/shard_map/ppermute | solution.py:298
  215.1 6.7 %collective-permute-start.18 = (bf16[4,45,16,128]{3,2,1,0:T(8,128)(2,1)S(1)}, bf16[4,45,16,128]{3,2,1,0:T(8,128)(2,1)S(1)}, u32[]{:S(2)}, u32[]{:S(2)}) collective-permute-start(bf16[4,45,16,128]{3,2,1,0:T(8,128)(2,1)S(1)} %pad_maximum_fusion.2.mine_ref), channel_id=1, source_target_pairs={{0,8},{8,0},{16,24},{24,16},{32,40},{40,32},{48,56},{56,48},{64,72... | collective-permute-start | bytes 2211848 | tf_op jit(solution)/shard_map/ppermute | solution.py:298
  (6 other events, 6.0 us)

commit v4 on v3

--- a/solution.py
+++ b/solution.py
@@ -93,10 +93,12 @@
         out_ref[d] = coeffs[:, d * LANES : (d + 1) * LANES].reshape(step, stored, LANES)
 
 
-def forward(basis, x):
+def forward(basis, x, at=0):
     size, stored, columns = x.shape
     parts = columns // LANES
     step = min(STEP, size)
+    first = at // step
+    assert first * step == at
     return pl.pallas_call(
         forward_kernel,
         grid=(pl.cdiv(size, step),),
@@ -104,15 +106,16 @@
             pl.BlockSpec((columns, columns), lambda i: (0, 0)),
             pl.BlockSpec((step, stored, columns), lambda i: (i, 0, 0)),
         ],
-        out_specs=pl.BlockSpec((parts, step, stored, LANES), lambda i: (0, i, 0, 0)),
-        out_shape=jax.ShapeDtypeStruct((parts, size, stored, LANES), BF16),
+        out_specs=pl.BlockSpec((parts, step, stored, LANES), lambda i: (0, first + i, 0, 0)),
+        out_shape=pltpu.HBM((parts, at + size, stored, LANES), BF16),
         compiler_params=params(),
         cost_estimate=cost(2 * x.size * columns, 2 * x.size + basis.size),
         name="forward",
     )(basis, x)
 
 
-def filter_kernel(basis_ref, basis_t_ref, weights_ref, x_ref, out_ref):
+def filter_kernel(basis_ref, basis_t_ref, weights_ref, x_ref, *refs):
+    out_ref = refs[-1]
     parts, step, stored, width = x_ref.shape
     x = jnp.concatenate([x_ref[:, l].reshape(parts * stored, width) for l in range(step)], axis=1)
     spectral = jnp.dot(basis_ref[...], x, preferred_element_type=F32)
@@ -123,21 +126,28 @@
         out_ref[:, l] = back[:, l * width : (l + 1) * width].reshape(parts, stored, width)
 
 
-def filter_rows(basis, basis_t, weights, x):
-    parts, size, stored, width = x.shape
-    step = min(STEP, size)
+def filter_rows(basis, basis_t, weights, x, start, size, buffer=None):
+    parts, _, stored, width = x.shape
+    step = min(STEP, size)
+    first = start // step
+    assert first * step == start
     whole = lambda a: pl.BlockSpec(a.shape, lambda i: (0, 0))
-    block = pl.BlockSpec((parts, step, stored, width), lambda i: (0, i, 0, 0))
+    held = [] if buffer is None else [buffer]
+    shape = (parts, size, stored, width) if buffer is None else buffer.shape
+    total = parts * size * stored * width
     return pl.pallas_call(
         filter_kernel,
         grid=(pl.cdiv(size, step),),
-        in_specs=[whole(basis), whole(basis_t), whole(weights), block],
-        out_specs=block,
-        out_shape=jax.ShapeDtypeStruct(x.shape, BF16),
-        compiler_params=params(),
-        cost_estimate=cost(4 * parts * stored * x.size, 2 * x.size),
+        in_specs=[whole(basis), whole(basis_t), whole(weights)]
+        + [pl.BlockSpec((parts, step, stored, width), lambda i: (0, first + i, 0, 0))]
+        + [pl.BlockSpec(memory_space=pl.ANY)] * len(held),
+        out_specs=pl.BlockSpec((parts, step, stored, width), lambda i: (0, i, 0, 0)),
+        out_shape=pltpu.HBM(shape, BF16),
+        input_output_aliases={4: 0} if held else {},
+        compiler_params=params(),
+        cost_estimate=cost(4 * parts * stored * total, 2 * total),
         name="filter",
-    )(basis, basis_t, weights, x)
+    )(basis, basis_t, weights, x, *[pltpu.with_memory_space_constraint(a, pltpu.HBM) for a in held])
 
 
 def backward_kernel(tiles_ref, basis_ref, member_ref, x_ref, keep_ref, give_ref, held):
@@ -151,14 +161,14 @@
         give_ref[q] = held[:, at_tile(tiles_ref[half + q])].reshape(step, stored, width)
 
 
-def backward(tiles, basis, member, x, start):
-    parts, size, stored, width = x.shape
+def backward(tiles, basis, member, x, start, size):
+    parts, _, stored, width = x.shape
     columns = parts * width
     step = min(STEP, size)
     first = start // step
     assert first * step == start
     half = pl.BlockSpec((parts // 2, step, stored, width), lambda i, *_: (0, i, 0, 0))
-    total = x.size
+    total = parts * size * stored * width
     return pl.pallas_call(
         backward_kernel,
         grid_spec=pltpu.PrefetchScalarGridSpec(
@@ -277,54 +287,52 @@
     starts = [sum(CHUNKS[:i]) for i in range(len(CHUNKS))]
 
     def spread(i):
-        return forward(basis_xt, localized[i])
-
-    def damp(pieces):
-        return filter_rows(basis_y, basis_yt, spectral_weights, pieces)
+        return forward(basis_xt, localized[i], CHUNKS[i - 1] if i else 0)
+
+    def damp(i, came, buffer=None):
+        start = CHUNKS[i - 1] if i else 0
+        return filter_rows(basis_y, basis_yt, spectral_weights, came, start, CHUNKS[i], buffer)
+
+    def regrid(i, came):
+        return backward(tiles, basis_x, member, came, starts[i], CHUNKS[i])
 
     def fold(keep, give):
-        return keep, pair_sum(keep, lax.ppermute(give, "mem", mem_to(0, 0, 1)))
+        return pair_sum(keep, lax.ppermute(give, "mem", mem_to(0, 0, 1)))
+
+    def scatter(kept):
+        return [kept[0]] + [lax.ppermute(kept[dy], "mem", mem_to(dy, 0, 0)) for dy in range(1, Y)]
+
+    def cross(part):
+        return lax.ppermute(part, "mem", mem_to(0, 1, 0))
+
+    def collect(part):
+        return [part] + [lax.ppermute(part, "mem", mem_to(-dy, 0, 0)) for dy in range(1, Y)]
+
+    def give(parts):
+        mine = jnp.stack(parts)
+        return mine, lax.ppermute(mine, "mem", mem_to(0, 0, 1))
 
     def along_y(keep):
-        part = add(
-            keep[0], *[lax.ppermute(keep[dy], "mem", mem_to(dy, 0, 0)) for dy in range(1, Y)]
-        )
-        return add(part, lax.ppermute(part, "mem", mem_to(0, 1, 0)))
-
-    def spread_y(part):
-        mine = jnp.stack(
-            [part] + [lax.ppermute(part, "mem", mem_to(-dy, 0, 0)) for dy in range(1, Y)]
-        )
-        return mine, lax.ppermute(mine, "mem", mem_to(0, 0, 1))
-
-    c0 = spread(0)
-    r0 = swap(c0)
-    c1 = spread(1)
-    r1 = swap(c1)
-    c2 = spread(2)
-    r0, c2 = tie((r0, c2))
-    g0 = damp(r0)
-    s0 = swap(g0)
-    r1, g0, c2 = tie((r1, g0, c2))
-    g1 = damp(r1)
-    r2 = swap(c2)
-    s0, g1 = tie((s0, g1))
-    s1 = swap(g1)
-    keep0, give0 = backward(tiles, basis_x, member, s0, starts[0])
-    keep0, half0 = fold(keep0, give0)
-    r2, half0 = tie((r2, half0))
-    g2 = damp(r2)
-    s2 = swap(g2)
+        part = add(*scatter(keep))
+        return add(part, cross(part))
+
+    came = swap(spread(0))
+    buffer = spread(1)
+    came, buffer = tie((came, buffer))
+    came = swap(damp(0, came, buffer))
+    buffer = spread(2)
+    came, buffer = tie((came, buffer))
+    next_came = swap(damp(1, came, buffer))
+    half0 = fold(*regrid(0, came))
     sum0 = along_y(half0)
-    s1, sum0 = tie((s1, sum0))
-    keep1, give1 = backward(tiles, basis_x, member, s1, starts[1])
-    keep1, half1 = fold(keep1, give1)
-    done0 = spread_y(sum0)
-    s2, half1, done0 = tie((s2, half1, done0))
-    keep2, give2 = backward(tiles, basis_x, member, s2, starts[2])
-    keep2, half2 = fold(keep2, give2)
-    done1 = spread_y(along_y(half1))
-    done2 = spread_y(along_y(half2))
+    came, sum0 = tie((next_came, sum0))
+    last = swap(damp(2, came))
+    half1 = fold(*regrid(1, came))
+    done0 = give(collect(sum0))
+    last, half1, done0 = tie((last, half1, done0))
+    half2 = fold(*regrid(2, last))
+    done1 = give(collect(along_y(half1)))
+    done2 = give(collect(along_y(half2)))
     out = None
     for i, (mine, theirs) in enumerate((done0, done1, done2)):
         out = place(tiles, mine, theirs, out, starts[i], levels)

time: 225 us -> 219 us (0.973)
  starting transfers between devices: 76 us -> 67.3 us
  waiting for transfers between devices: 83 us -> 89.4 us
  local copies, waits for them, and re-layouts: 16.9 us -> 10.8 us
  Pallas kernels: 47 us -> 49.3 us
    ppermute x27, waiting for transfers between devices: 24.4 us -> 41.2 us  [the longest x9 18.1 us: scatter(): lax.ppermute(kept[dy], 'mem', mem_to(dy, 0, 0))]
    all_to_all x6 -> x4, waiting for transfers between devices: 58.7 us -> 48.2 us  [swap(): return lax.all_to_all(pieces, 'space', 0, 0, tiled=True)]
    all_to_all x6 -> x4, starting transfers between devices: 30.7 us -> 23.6 us  [swap(): return lax.all_to_all(pieces, 'space', 0, 0, tiled=True)]
    unnamed x42 -> x32, local copies, waits for them, and re-layouts: 16.7 us -> 10.6 us
    pallas_call x3, Pallas kernels: 5.22 us -> 8.53 us  [filter_rows(): pl.pallas_call(filter_kernel, grid=(pl.cdiv(size, step),), in_specs=[whol...]
  transfers between devices with their start and end apart: 33 -> 31, of which waited for: 16 -> 17; matrix products, arithmetic and copies ran while one was open for 1% -> 1% of each run, Pallas kernels for 12% -> 10%
where the time goes in v4:
time: 219 us; the launch traced here: 218 us
  waiting for transfers between devices  89.4 us (41%)
  starting transfers between devices  67.3 us (31%)
  Pallas kernels  49.3 us (23%)
  local copies, waits for them, and re-layouts  10.8 us (5%)
    all_to_all x4, waiting for transfers between devices, swap(): return lax.all_to_all(pieces, 'space', 0, 0, tiled=True)  48.2 us
    all_to_all x4, starting transfers between devices, swap(): return lax.all_to_all(pieces, 'space', 0, 0, tiled=True)  23.6 us
    ppermute x9, waiting for transfers between devices, scatter(): lax.ppermute(kept[dy], 'mem', mem_to(dy, 0, 0))  18.1 us
    pallas_call x3, Pallas kernels, backward(): pl.pallas_call(backward_kernel, grid_spec=pltpu.PrefetchScalarGridSpec(nu...  13.4 us
    ppermute x9, starting transfers between devices, scatter(): lax.ppermute(kept[dy], 'mem', mem_to(dy, 0, 0))  13 us
    ppermute x9, starting transfers between devices, collect(): lax.ppermute(part, 'mem', mem_to(-dy, 0, 0))  12.9 us
    ppermute x3, waiting for transfers between devices, cross(): return lax.ppermute(part, 'mem', mem_to(0, 1, 0))  12.4 us
    ppermute x3, starting transfers between devices, fold(): return pair_sum(keep, lax.ppermute(give, 'mem', mem_to(0, 0, 1)))  12.2 us
  transfers between devices with their start and end apart: 31, of which 17 were waited for; matrix products, arithmetic and copies ran while one was open for 1% of the time, Pallas kernels for 10%

profile of v4, /device:TPU:1, one launch (start us, length us, event | category | flops | bytes accessed | tf_op | source)
XLA Modules:
  0.0 218.0 jit_solution(16792834707862103927)
XLA Ops:
  0.9 9.7 %mix.1 = (bf16[46,16,1024]{2,1,0:T(8,128)(2,1)S(1)}, bf16[46,16,1024]{2,1,0:T(8,128)(2,1)S(1)}, bf16[45,16,1024]{2,1,0:T(8,128)(2,1)S(1)}) custom-call(bf16[137,137]{1,0:T(8,128)(2,1)S(1)} %copy-done.11, bf16[137,16,1024]{2,1,0:T(8,128)(2,1)} %bitcast.24, bf16[137,16,1024]{2,1,0:T(8,128)(2,1)} %increment_ref.1), custom_call_target="tpu_custom_call" | custom-call | tf_op jit(solution)/shard_map/mix/pallas_call | solution.py:67
  12.9 2.8 %forward.3 = bf16[8,46,16,128]{3,2,1,0:T(8,128)(2,1)} custom-call(bf16[1024,1024]{1,0:T(8,128)(2,1)S(1)} %copy-done.2, bf16[46,16,1024]{2,1,0:T(8,128)(2,1)S(1)} %get-tuple-element.39.x_ref), custom_call_target="tpu_custom_call" | custom-call | flops 1543503872 | bytes 5111808 | tf_op jit(solution)/shard_map/forward/pallas_call | solution.py:102
  15.7 8.3 %all-to-all-start = ((bf16[8,46,16,128]{3,2,1,0:T(8,128)(2,1)}), bf16[8,46,16,128]{3,2,1,0:T(8,128)(2,1)}, u32[]{:S(2)}, u32[]{:S(2)}) async-start(bf16[8,46,16,128]{3,2,1,0:T(8,128)(2,1)} %forward.3), calls=%async_computation | async-start | bytes 3014656 | tf_op jit(solution)/shard_map/all_to_all | solution.py:261
  24.3 1.4 copy-done.5
  25.7 2.8 %forward.4.refs_0_ = bf16[8,92,16,128]{3,2,1,0:T(8,128)(2,1)} custom-call(bf16[1024,1024]{1,0:T(8,128)(2,1)S(1)} %copy-done.2, bf16[46,16,1024]{2,1,0:T(8,128)(2,1)S(1)} %copy-done.5), custom_call_target="tpu_custom_call" | custom-call | flops 1543503872 | bytes 5111808 | tf_op jit(solution)/shard_map/forward/pallas_call | solution.py:102
  28.5 16.8 %all-to-all-done.x_ref = bf16[8,46,16,128]{3,2,1,0:T(8,128)(2,1)} async-done(((bf16[8,46,16,128]{3,2,1,0:T(8,128)(2,1)}), bf16[8,46,16,128]{3,2,1,0:T(8,128)(2,1)}, u32[]{:S(2)}, u32[]{:S(2)}) %all-to-all-start) | async-done | bytes 1507360 | tf_op jit(solution)/shard_map/all_to_all | solution.py:261
  45.3 3.1 %filter.3 = bf16[8,92,16,128]{3,2,1,0:T(8,128)(2,1)} custom-call(bf16[128,128]{1,0:T(8,128)(2,1)S(1)} %copy.15.basis_ref, bf16[128,128]{1,0:T(8,128)(2,1)S(1)} %convolution_convert_fusion.basis_t_ref, f32[128,128]{1,0:T(8,128)S(1)} %copy-done.10, bf16[8,46,16,128]{3,2,1,0:T(8,128)(2,1)} %all-to-all-done.x_ref, ...), custom_call_target="tpu_custom_call", output_to_operand_aliasing={{}: (4, {})} | custom-call | flops 385875968 | bytes 3014656 | tf_op jit(solution)/shard_map/filter/pallas_call | solution.py:138
  48.4 3.8 %all-to-all-start.1 = ((bf16[8,92,16,128]{3,2,1,0:T(8,128)(2,1)}), bf16[8,92,16,128]{3,2,1,0:T(8,128)(2,1)S(1)}, u32[]{:S(2)}, u32[]{:S(2)}) async-start(bf16[8,92,16,128]{3,2,1,0:T(8,128)(2,1)} %filter.3), calls=%async_computation.1 | async-start | bytes 6029312 | tf_op jit(solution)/shard_map/all_to_all | solution.py:261
  52.2 1.6 copy-done.3
  53.8 1.4 copy-done.7
  55.2 2.8 %forward.5.refs_0_ = bf16[8,91,16,128]{3,2,1,0:T(8,128)(2,1)} custom-call(bf16[1024,1024]{1,0:T(8,128)(2,1)S(1)} %copy-done.3, bf16[45,16,1024]{2,1,0:T(8,128)(2,1)S(1)} %copy-done.7), custom_call_target="tpu_custom_call" | custom-call | flops 1509949440 | bytes 5046272 | tf_op jit(solution)/shard_map/forward/pallas_call | solution.py:102
  58.0 30.8 %all-to-all-done.1.x_ref = bf16[8,92,16,128]{3,2,1,0:T(8,128)(2,1)S(1)} async-done(((bf16[8,92,16,128]{3,2,1,0:T(8,128)(2,1)}), bf16[8,92,16,128]{3,2,1,0:T(8,128)(2,1)S(1)}, u32[]{:S(2)}, u32[]{:S(2)}) %all-to-all-start.1) | async-done | bytes 3014688 | tf_op jit(solution)/shard_map/all_to_all | solution.py:261
  88.9 2.1 filter.4
  91.0 4.5 %all-to-all-start.2 = ((bf16[8,91,16,128]{3,2,1,0:T(8,128)(2,1)}), bf16[8,91,16,128]{3,2,1,0:T(8,128)(2,1)}, u32[]{:S(2)}, u32[]{:S(2)}) async-start(bf16[8,91,16,128]{3,2,1,0:T(8,128)(2,1)} %filter.4), calls=%async_computation.2 | async-start | bytes 5963776 | tf_op jit(solution)/shard_map/all_to_all | solution.py:261
  95.6 1.6 copy-done
  97.2 4.1 %backward.3 = (bf16[4,46,16,128]{3,2,1,0:T(8,128)(2,1)S(1)}, bf16[4,46,16,128]{3,2,1,0:T(8,128)(2,1)S(1)}) custom-call(s32[8]{0:T(128)S(1)} %stack.80.tiles_ref, bf16[1024,1024]{1,0:T(8,128)(2,1)S(1)} %copy-done, bf16[137,16,1024]{2,1,0:T(8,128)(2,1)} %bitcast.25, bf16[8,92,16,128]{3,2,1,0:T(8,128)(2,1)S(1)} %all-to-all-done.1.x_ref), custom_call_target="tpu_custom_call" | custom-call | flops 1543503872 | bytes 6619136 | tf_op jit(solution)/shard_map/backward/pallas_call | solution.py:172
  101.3 2.7 %collective-permute-start = (bf16[4,46,16,128]{3,2,1,0:T(8,128)(2,1)S(1)}, bf16[4,46,16,128]{3,2,1,0:T(8,128)(2,1)S(1)}, u32[]{:S(2)}, u32[]{:S(2)}) collective-permute-start(bf16[4,46,16,128]{3,2,1,0:T(8,128)(2,1)S(1)} %get-tuple-element.47), channel_id=1, source_target_pairs={{0,8},{8,0},{16,24},{24,16},{32,40},{40,32},{48,56},{56,48},{64,72... | collective-permute-start | bytes 2261000 | tf_op jit(solution)/shard_map/ppermute | solution.py:300
  104.0 1.9 collective-permute-done.b_ref
  106.2 1.4 collective-permute-start.1
  107.6 2.6 %collective-permute-start.2 = (bf16[46,16,128]{2,1,0:T(8,128)(2,1)S(1)}, bf16[46,16,128]{2,1,0:T(8,128)(2,1)S(1)}, u32[]{:S(2)}, u32[]{:S(2)}) collective-permute-start(bf16[46,16,128]{2,1,0:T(8,128)(2,1)S(1)} %get-tuple-element.50), channel_id=1, source_target_pairs={{0,64},{8,72},{16,80},{24,88},{32,96},{40,104},{48,112},{56,120},{... | collective-permute-start | bytes 565256 | tf_op jit(solution)/shard_map/ppermute | solution.py:303
  111.3 2.4 %collective-permute-done.1 = bf16[46,16,128]{2,1,0:T(8,128)(2,1)S(1)} collective-permute-done((bf16[46,16,128]{2,1,0:T(8,128)(2,1)S(1)}, bf16[46,16,128]{2,1,0:T(8,128)(2,1)S(1)}, u32[]{:S(2)}, u32[]{:S(2)}) %collective-permute-start.1) | collective-permute-done | bytes 188448 | tf_op jit(solution)/shard_map/ppermute | solution.py:303
  113.7 5.1 %collective-permute-done.2 = bf16[46,16,128]{2,1,0:T(8,128)(2,1)S(1)} collective-permute-done((bf16[46,16,128]{2,1,0:T(8,128)(2,1)S(1)}, bf16[46,16,128]{2,1,0:T(8,128)(2,1)S(1)}, u32[]{:S(2)}, u32[]{:S(2)}) %collective-permute-start.2) | collective-permute-done | bytes 188448 | tf_op jit(solution)/shard_map/ppermute | solution.py:303
  119.3 11.4 %collective-permute-done.4 = bf16[46,16,128]{2,1,0:T(8,128)(2,1)S(1)} collective-permute-done((bf16[46,16,128]{2,1,0:T(8,128)(2,1)S(1)}, bf16[46,16,128]{2,1,0:T(8,128)(2,1)S(1)}, u32[]{:S(2)}, u32[]{:S(2)}) %collective-permute-start.4) | collective-permute-done | bytes 188448 | tf_op jit(solution)/shard_map/ppermute | solution.py:306
  131.1 3.3 %filter.5 = bf16[8,45,16,128]{3,2,1,0:T(8,128)(2,1)} custom-call(bf16[128,128]{1,0:T(8,128)(2,1)S(1)} %copy.15.basis_ref, bf16[128,128]{1,0:T(8,128)(2,1)S(1)} %convolution_convert_fusion.basis_t_ref, f32[128,128]{1,0:T(8,128)S(1)} %copy-done.10, bf16[8,91,16,128]{3,2,1,0:T(8,128)(2,1)} %all-to-all-done.2.x_ref), custom_call_target="tpu_custom_call" | custom-call | flops 377487360 | bytes 2949120 | tf_op jit(solution)/shard_map/filter/pallas_call | solution.py:138
  134.4 6.9 %all-to-all-start.3 = ((bf16[8,45,16,128]{3,2,1,0:T(8,128)(2,1)}), bf16[8,45,16,128]{3,2,1,0:T(8,128)(2,1)}, u32[]{:S(2)}, u32[]{:S(2)}) async-start(bf16[8,45,16,128]{3,2,1,0:T(8,128)(2,1)} %filter.5), calls=%async_computation.3 | async-start | bytes 2949120 | tf_op jit(solution)/shard_map/all_to_all | solution.py:261
  142.7 2.6 %collective-permute-start.7 = (bf16[46,16,128]{2,1,0:T(8,128)(2,1)S(1)}, bf16[46,16,128]{2,1,0:T(8,128)(2,1)S(1)}, u32[]{:S(2)}, u32[]{:S(2)}) collective-permute-start(bf16[46,16,128]{2,1,0:T(8,128)(2,1)S(1)} %add_convert_fusion.2), channel_id=1, source_target_pairs={{0,64},{8,72},{16,80},{24,88},{32,96},{40,104},{48,112},{56,120},{... | collective-permute-start | bytes 565256 | tf_op jit(solution)/shard_map/ppermute | solution.py:309
  146.4 4.4 %backward.4 = (bf16[4,46,16,128]{3,2,1,0:T(8,128)(2,1)S(1)}, bf16[4,46,16,128]{3,2,1,0:T(8,128)(2,1)S(1)}) custom-call(s32[8]{0:T(128)S(1)} %stack.80.tiles_ref, bf16[1024,1024]{1,0:T(8,128)(2,1)S(1)} %copy-done.1, bf16[137,16,1024]{2,1,0:T(8,128)(2,1)} %bitcast.26, bf16[8,91,16,128]{3,2,1,0:T(8,128)(2,1)} %all-to-all-done.2.x_ref), custom_call_target="tpu_custom_call" | custom-call | flops 1543503872 | bytes 6619136 | tf_op jit(solution)/shard_map/backward/pallas_call | solution.py:172
  150.8 4.7 %collective-permute-start.5 = (bf16[4,46,16,128]{3,2,1,0:T(8,128)(2,1)S(1)}, bf16[4,46,16,128]{3,2,1,0:T(8,128)(2,1)S(1)}, u32[]{:S(2)}, u32[]{:S(2)}) collective-permute-start(bf16[4,46,16,128]{3,2,1,0:T(8,128)(2,1)S(1)} %get-tuple-element.54), channel_id=1, source_target_pairs={{0,8},{8,0},{16,24},{24,16},{32,40},{40,32},{48,56},{56,48},{64,72... | collective-permute-start | bytes 2261000 | tf_op jit(solution)/shard_map/ppermute | solution.py:300
  155.9 1.5 collective-permute-done.5.b_ref
  159.5 4.9 %backward.5 = (bf16[4,45,16,128]{3,2,1,0:T(8,128)(2,1)S(1)}, bf16[4,45,16,128]{3,2,1,0:T(8,128)(2,1)S(1)}) custom-call(s32[8]{0:T(128)S(1)} %stack.80.tiles_ref, bf16[1024,1024]{1,0:T(8,128)(2,1)S(1)} %copy-done.1, bf16[137,16,1024]{2,1,0:T(8,128)(2,1)} %bitcast.27, bf16[8,45,16,128]{3,2,1,0:T(8,128)(2,1)} %all-to-all-done.3.x_ref), custom_call_target="tpu_custom_call" | custom-call | flops 1509949440 | bytes 6520832 | tf_op jit(solution)/shard_map/backward/pallas_call | solution.py:172
  164.5 4.8 %collective-permute-start.10 = (bf16[4,45,16,128]{3,2,1,0:T(8,128)(2,1)S(1)}, bf16[4,45,16,128]{3,2,1,0:T(8,128)(2,1)S(1)}, u32[]{:S(2)}, u32[]{:S(2)}) collective-permute-start(bf16[4,45,16,128]{3,2,1,0:T(8,128)(2,1)S(1)} %get-tuple-element.62), channel_id=1, source_target_pairs={{0,8},{8,0},{16,24},{24,16},{32,40},{40,32},{48,56},{56,48},{64,72... | collective-permute-start | bytes 2211848 | tf_op jit(solution)/shard_map/ppermute | solution.py:300
  169.3 1.3 collective-permute-start.19
  170.6 2.6 %collective-permute-start.20 = (bf16[46,16,128]{2,1,0:T(8,128)(2,1)S(1)}, bf16[46,16,128]{2,1,0:T(8,128)(2,1)S(1)}, u32[]{:S(2)}, u32[]{:S(2)}) collective-permute-start(bf16[46,16,128]{2,1,0:T(8,128)(2,1)S(1)} %get-tuple-element.69), channel_id=1, source_target_pairs={{0,64},{8,72},{16,80},{24,88},{32,96},{40,104},{48,112},{56,120},{... | collective-permute-start | bytes 565256 | tf_op jit(solution)/shard_map/ppermute | solution.py:303
  174.3 2.0 pair_sum.5
  177.6 1.7 collective-permute-start.13
  179.3 2.8 %collective-permute-done.20 = bf16[46,16,128]{2,1,0:T(8,128)(2,1)S(1)} collective-permute-done((bf16[46,16,128]{2,1,0:T(8,128)(2,1)S(1)}, bf16[46,16,128]{2,1,0:T(8,128)(2,1)S(1)}, u32[]{:S(2)}, u32[]{:S(2)}) %collective-permute-start.20) | collective-permute-done | bytes 188448 | tf_op jit(solution)/shard_map/ppermute | solution.py:303
  182.3 4.4 %collective-permute-done.11 = bf16[45,16,128]{2,1,0:T(8,128)(2,1)S(1)} collective-permute-done((bf16[45,16,128]{2,1,0:T(8,128)(2,1)S(1)}, bf16[45,16,128]{2,1,0:T(8,128)(2,1)S(1)}, u32[]{:S(2)}, u32[]{:S(2)}) %collective-permute-start.11) | collective-permute-done | bytes 184352 | tf_op jit(solution)/shard_map/ppermute | solution.py:303
  186.7 3.3 %collective-permute-done.12 = bf16[45,16,128]{2,1,0:T(8,128)(2,1)S(1)} collective-permute-done((bf16[45,16,128]{2,1,0:T(8,128)(2,1)S(1)}, bf16[45,16,128]{2,1,0:T(8,128)(2,1)S(1)}, u32[]{:S(2)}, u32[]{:S(2)}) %collective-permute-start.12) | collective-permute-done | bytes 184352 | tf_op jit(solution)/shard_map/ppermute | solution.py:303
  190.7 2.9 %collective-permute-start.24 = (bf16[46,16,128]{2,1,0:T(8,128)(2,1)S(1)}, bf16[46,16,128]{2,1,0:T(8,128)(2,1)S(1)}, u32[]{:S(2)}, u32[]{:S(2)}) collective-permute-start(bf16[46,16,128]{2,1,0:T(8,128)(2,1)S(1)} %add_convert_fusion), channel_id=1, source_target_pairs={{0,64},{8,72},{16,80},{24,88},{32,96},{40,104},{48,112},{56,120},{... | collective-permute-start | bytes 565256 | tf_op jit(solution)/shard_map/ppermute | solution.py:309
  195.6 3.7 %collective-permute-start.16 = (bf16[45,16,128]{2,1,0:T(8,128)(2,1)S(1)}, bf16[45,16,128]{2,1,0:T(8,128)(2,1)S(1)}, u32[]{:S(2)}, u32[]{:S(2)}) collective-permute-start(bf16[45,16,128]{2,1,0:T(8,128)(2,1)S(1)} %add_convert_fusion.4), channel_id=1, source_target_pairs={{0,64},{8,72},{16,80},{24,88},{32,96},{40,104},{48,112},{56,120},{... | collective-permute-start | bytes 552968 | tf_op jit(solution)/shard_map/ppermute | solution.py:309
  199.3 2.7 %collective-permute-done.24 = bf16[46,16,128]{2,1,0:T(8,128)(2,1)S(1)} collective-permute-done((bf16[46,16,128]{2,1,0:T(8,128)(2,1)S(1)}, bf16[46,16,128]{2,1,0:T(8,128)(2,1)S(1)}, u32[]{:S(2)}, u32[]{:S(2)}) %collective-permute-start.24) | collective-permute-done | bytes 188448 | tf_op jit(solution)/shard_map/ppermute | solution.py:309
  202.1 3.2 %collective-permute-start.26 = (bf16[4,46,16,128]{3,2,1,0:T(8,128)(2,1)S(1)}, bf16[4,46,16,128]{3,2,1,0:T(8,128)(2,1)S(1)}, u32[]{:S(2)}, u32[]{:S(2)}) collective-permute-start(bf16[4,46,16,128]{3,2,1,0:T(8,128)(2,1)S(1)} %pad_maximum_fusion.1.mine_ref), channel_id=1, source_target_pairs={{0,8},{8,0},{16,24},{24,16},{32,40},{40,32},{48,56},{56,48},{64,72... | collective-permute-start | bytes 2261000 | tf_op jit(solution)/shard_map/ppermute | solution.py:313
  205.3 1.6 collective-permute-done.17
  206.9 3.0 %collective-permute-done.16 = bf16[45,16,128]{2,1,0:T(8,128)(2,1)S(1)} collective-permute-done((bf16[45,16,128]{2,1,0:T(8,128)(2,1)S(1)}, bf16[45,16,128]{2,1,0:T(8,128)(2,1)S(1)}, u32[]{:S(2)}, u32[]{:S(2)}) %collective-permute-start.16) | collective-permute-done | bytes 184352 | tf_op jit(solution)/shard_map/ppermute | solution.py:309
  210.0 1.5 collective-permute-start.18
  211.5 2.0 place.3.refs_0_
  213.5 2.0 place.4.refs_0_
  215.5 2.5 %place.5 = bf16[137,16,1024]{2,1,0:T(8,128)(2,1)} custom-call(s32[8]{0:T(128)S(1)} %stack.80.tiles_ref, bf16[4,45,16,128]{3,2,1,0:T(8,128)(2,1)S(1)} %pad_maximum_fusion.2.mine_ref, bf16[4,45,16,128]{3,2,1,0:T(8,128)(2,1)S(1)} %collective-permute-done.18.theirs_ref, bf16[137,16,1024]{2,1,0:T(8,128)(2,1)} %place.4.refs_0_), custom_call_target="tpu_custom_call", output_to_operand_aliasing={{}: (3, {})} | custom-call | bytes 2949120 | tf_op jit(solution)/shard_map/place/pallas_call | solution.py:228
  (74 shorter events, 16.2 us)
Async XLA Ops:
  0.0 0.9 copy-start.11
  0.9 12.0 %copy-start.2 = (bf16[1024,1024]{1,0:T(8,128)(2,1)S(1)}, bf16[1024,1024]{1,0:T(8,128)(2,1)}, u32[]{:S(2)}) copy-start(bf16[1024,1024]{1,0:T(8,128)(2,1)} %constant.69.clone.basis_ref) | copy-start | bytes 6291460
  10.6 1.1 copy-start.4
  11.7 1.1 copy-start.6
  12.8 11.1 %copy-start.14 = (bf16[128,128]{1,0:T(8,128)(2,1)S(1)}, bf16[128,128]{1,0:T(8,128)(2,1)}, u32[]{:S(2)}) copy-start(bf16[128,128]{1,0:T(8,128)(2,1)} %constant.70.clone) | copy-start | bytes 98308
  12.9 11.1 %copy-start.15 = (s32[128]{0:T(128)S(1)}, s32[128]{0:T(128)}, u32[]{:S(2)}) copy-start(s32[128]{0:T(128)} %param.12) | copy-start | bytes 1540
  15.7 29.6 %all-to-all-start = ((bf16[8,46,16,128]{3,2,1,0:T(8,128)(2,1)}), bf16[8,46,16,128]{3,2,1,0:T(8,128)(2,1)}, u32[]{:S(2)}, u32[]{:S(2)}) async-start(bf16[8,46,16,128]{3,2,1,0:T(8,128)(2,1)} %forward.3), calls=%async_computation | async-start | bytes 3014656 | tf_op jit(solution)/shard_map/all_to_all | solution.py:261
  24.3 1.4 copy-start.5
  25.7 19.6 %copy-start.10 = (f32[128,128]{1,0:T(8,128)S(1)}, f32[128,128]{1,0:T(8,128)}, u32[]{:S(2)}) copy-start(f32[128,128]{1,0:T(8,128)} %weights_ref.5) | copy-start | bytes 196612
  48.4 40.5 %all-to-all-start.1 = ((bf16[8,92,16,128]{3,2,1,0:T(8,128)(2,1)}), bf16[8,92,16,128]{3,2,1,0:T(8,128)(2,1)S(1)}, u32[]{:S(2)}, u32[]{:S(2)}) async-start(bf16[8,92,16,128]{3,2,1,0:T(8,128)(2,1)} %filter.3), calls=%async_computation.1 | async-start | bytes 6029312 | tf_op jit(solution)/shard_map/all_to_all | solution.py:261
  52.2 1.6 copy-start.3
  53.8 1.4 copy-start.7
  91.0 40.2 %all-to-all-start.2 = ((bf16[8,91,16,128]{3,2,1,0:T(8,128)(2,1)}), bf16[8,91,16,128]{3,2,1,0:T(8,128)(2,1)}, u32[]{:S(2)}, u32[]{:S(2)}) async-start(bf16[8,91,16,128]{3,2,1,0:T(8,128)(2,1)} %filter.4), calls=%async_computation.2 | async-start | bytes 5963776 | tf_op jit(solution)/shard_map/all_to_all | solution.py:261
  95.6 1.6 copy-start
  101.3 4.6 %collective-permute-start = (bf16[4,46,16,128]{3,2,1,0:T(8,128)(2,1)S(1)}, bf16[4,46,16,128]{3,2,1,0:T(8,128)(2,1)S(1)}, u32[]{:S(2)}, u32[]{:S(2)}) collective-permute-start(bf16[4,46,16,128]{3,2,1,0:T(8,128)(2,1)S(1)} %get-tuple-element.47), channel_id=1, source_target_pairs={{0,8},{8,0},{16,24},{24,16},{32,40},{40,32},{48,56},{56,48},{64,72... | collective-permute-start | bytes 2261000 | tf_op jit(solution)/shard_map/ppermute | solution.py:300
  106.2 7.5 %collective-permute-start.1 = (bf16[46,16,128]{2,1,0:T(8,128)(2,1)S(1)}, bf16[46,16,128]{2,1,0:T(8,128)(2,1)S(1)}, u32[]{:S(2)}, u32[]{:S(2)}) collective-permute-start(bf16[46,16,128]{2,1,0:T(8,128)(2,1)S(1)} %get-tuple-element.49), channel_id=1, source_target_pairs={{0,32},{8,40},{16,48},{24,56},{32,64},{40,72},{48,80},{56,88},{64,... | collective-permute-start | bytes 565256 | tf_op jit(solution)/shard_map/ppermute | solution.py:303
  107.6 11.3 %collective-permute-start.2 = (bf16[46,16,128]{2,1,0:T(8,128)(2,1)S(1)}, bf16[46,16,128]{2,1,0:T(8,128)(2,1)S(1)}, u32[]{:S(2)}, u32[]{:S(2)}) collective-permute-start(bf16[46,16,128]{2,1,0:T(8,128)(2,1)S(1)} %get-tuple-element.50), channel_id=1, source_target_pairs={{0,64},{8,72},{16,80},{24,88},{32,96},{40,104},{48,112},{56,120},{... | collective-permute-start | bytes 565256 | tf_op jit(solution)/shard_map/ppermute | solution.py:303
  110.2 8.6 %collective-permute-start.3 = (bf16[46,16,128]{2,1,0:T(8,128)(2,1)S(1)}, bf16[46,16,128]{2,1,0:T(8,128)(2,1)S(1)}, u32[]{:S(2)}, u32[]{:S(2)}) collective-permute-start(bf16[46,16,128]{2,1,0:T(8,128)(2,1)S(1)} %get-tuple-element.51), channel_id=1, source_target_pairs={{0,96},{8,104},{16,112},{24,120},{32,0},{40,8},{48,16},{56,24},{64... | collective-permute-start | bytes 565256 | tf_op jit(solution)/shard_map/ppermute | solution.py:303
  118.9 11.8 %collective-permute-start.4 = (bf16[46,16,128]{2,1,0:T(8,128)(2,1)S(1)}, bf16[46,16,128]{2,1,0:T(8,128)(2,1)S(1)}, u32[]{:S(2)}, u32[]{:S(2)}) collective-permute-start(bf16[46,16,128]{2,1,0:T(8,128)(2,1)S(1)} %add_convert_fusion.3), channel_id=1, source_target_pairs={{0,16},{8,24},{16,0},{24,8},{32,48},{40,56},{48,32},{56,40},{64,80... | collective-permute-start | bytes 565256 | tf_op jit(solution)/shard_map/ppermute | solution.py:306
  130.8 15.6 %copy-start.1 = (bf16[1024,1024]{1,0:T(8,128)(2,1)S(1)}, bf16[1024,1024]{1,0:T(8,128)(2,1)}, u32[]{:S(2)}) copy-start(bf16[1024,1024]{1,0:T(8,128)(2,1)} %constant.68.clone.basis_ref) | copy-start | bytes 6291460
  134.4 25.1 %all-to-all-start.3 = ((bf16[8,45,16,128]{3,2,1,0:T(8,128)(2,1)}), bf16[8,45,16,128]{3,2,1,0:T(8,128)(2,1)}, u32[]{:S(2)}, u32[]{:S(2)}) async-start(bf16[8,45,16,128]{3,2,1,0:T(8,128)(2,1)} %filter.5), calls=%async_computation.3 | async-start | bytes 2949120 | tf_op jit(solution)/shard_map/all_to_all | solution.py:261
  141.4 14.1 %collective-permute-start.8 = (bf16[46,16,128]{2,1,0:T(8,128)(2,1)S(1)}, bf16[46,16,128]{2,1,0:T(8,128)(2,1)S(1)}, u32[]{:S(2)}, u32[]{:S(2)}) collective-permute-start(bf16[46,16,128]{2,1,0:T(8,128)(2,1)S(1)} %add_convert_fusion.2), channel_id=1, source_target_pairs={{0,32},{8,40},{16,48},{24,56},{32,64},{40,72},{48,80},{56,88},{64,... | collective-permute-start | bytes 565256 | tf_op jit(solution)/shard_map/ppermute | solution.py:309
  142.7 12.8 %collective-permute-start.7 = (bf16[46,16,128]{2,1,0:T(8,128)(2,1)S(1)}, bf16[46,16,128]{2,1,0:T(8,128)(2,1)S(1)}, u32[]{:S(2)}, u32[]{:S(2)}) collective-permute-start(bf16[46,16,128]{2,1,0:T(8,128)(2,1)S(1)} %add_convert_fusion.2), channel_id=1, source_target_pairs={{0,64},{8,72},{16,80},{24,88},{32,96},{40,104},{48,112},{56,120},{... | collective-permute-start | bytes 565256 | tf_op jit(solution)/shard_map/ppermute | solution.py:309
  145.3 10.2 %collective-permute-start.6 = (bf16[46,16,128]{2,1,0:T(8,128)(2,1)S(1)}, bf16[46,16,128]{2,1,0:T(8,128)(2,1)S(1)}, u32[]{:S(2)}, u32[]{:S(2)}) collective-permute-start(bf16[46,16,128]{2,1,0:T(8,128)(2,1)S(1)} %add_convert_fusion.2), channel_id=1, source_target_pairs={{0,96},{8,104},{16,112},{24,120},{32,0},{40,8},{48,16},{56,24},{64... | collective-permute-start | bytes 565256 | tf_op jit(solution)/shard_map/ppermute | solution.py:309
  150.8 6.6 %collective-permute-start.5 = (bf16[4,46,16,128]{3,2,1,0:T(8,128)(2,1)S(1)}, bf16[4,46,16,128]{3,2,1,0:T(8,128)(2,1)S(1)}, u32[]{:S(2)}, u32[]{:S(2)}) collective-permute-start(bf16[4,46,16,128]{3,2,1,0:T(8,128)(2,1)S(1)} %get-tuple-element.54), channel_id=1, source_target_pairs={{0,8},{8,0},{16,24},{24,16},{32,40},{40,32},{48,56},{56,48},{64,72... | collective-permute-start | bytes 2261000 | tf_op jit(solution)/shard_map/ppermute | solution.py:300
  155.6 2.8 %collective-permute-start.9 = (bf16[4,46,16,128]{3,2,1,0:T(8,128)(2,1)S(1)}, bf16[4,46,16,128]{3,2,1,0:T(8,128)(2,1)S(1)}, u32[]{:S(2)}, u32[]{:S(2)}) collective-permute-start(bf16[4,46,16,128]{3,2,1,0:T(8,128)(2,1)S(1)} %pad_maximum_fusion.mine_ref), channel_id=1, source_target_pairs={{0,8},{8,0},{16,24},{24,16},{32,40},{40,32},{48,56},{56,48},{64,72... | collective-permute-start | bytes 2261000 | tf_op jit(solution)/shard_map/ppermute | solution.py:313
  157.7 0.7 copy-start.12
  158.4 0.9 copy-start.8
  159.5 9.8 %copy-start.13 = (bf16[46,16,128]{2,1,0:T(8,128)(2,1)S(1)}, bf16[46,16,128]{2,1,0:T(8,128)(2,1)}, u32[]{:S(2)}) copy-start(bf16[46,16,128]{2,1,0:T(8,128)(2,1)} %copy-done.12) | copy-start | bytes 565252
  164.5 9.8 %collective-permute-start.10 = (bf16[4,45,16,128]{3,2,1,0:T(8,128)(2,1)S(1)}, bf16[4,45,16,128]{3,2,1,0:T(8,128)(2,1)S(1)}, u32[]{:S(2)}, u32[]{:S(2)}) collective-permute-start(bf16[4,45,16,128]{3,2,1,0:T(8,128)(2,1)S(1)} %get-tuple-element.62), channel_id=1, source_target_pairs={{0,8},{8,0},{16,24},{24,16},{32,40},{40,32},{48,56},{56,48},{64,72... | collective-permute-start | bytes 2211848 | tf_op jit(solution)/shard_map/ppermute | solution.py:300
  169.3 8.3 %collective-permute-start.19 = (bf16[46,16,128]{2,1,0:T(8,128)(2,1)S(1)}, bf16[46,16,128]{2,1,0:T(8,128)(2,1)S(1)}, u32[]{:S(2)}, u32[]{:S(2)}) collective-permute-start(bf16[46,16,128]{2,1,0:T(8,128)(2,1)S(1)} %copy-done.13), channel_id=1, source_target_pairs={{0,32},{8,40},{16,48},{24,56},{32,64},{40,72},{48,80},{56,88},{64,... | collective-permute-start | bytes 565256 | tf_op jit(solution)/shard_map/ppermute | solution.py:303
  170.6 11.5 %collective-permute-start.20 = (bf16[46,16,128]{2,1,0:T(8,128)(2,1)S(1)}, bf16[46,16,128]{2,1,0:T(8,128)(2,1)S(1)}, u32[]{:S(2)}, u32[]{:S(2)}) collective-permute-start(bf16[46,16,128]{2,1,0:T(8,128)(2,1)S(1)} %get-tuple-element.69), channel_id=1, source_target_pairs={{0,64},{8,72},{16,80},{24,88},{32,96},{40,104},{48,112},{56,120},{... | collective-permute-start | bytes 565256 | tf_op jit(solution)/shard_map/ppermute | solution.py:303
  173.2 8.9 %collective-permute-start.21 = (bf16[46,16,128]{2,1,0:T(8,128)(2,1)S(1)}, bf16[46,16,128]{2,1,0:T(8,128)(2,1)S(1)}, u32[]{:S(2)}, u32[]{:S(2)}) collective-permute-start(bf16[46,16,128]{2,1,0:T(8,128)(2,1)S(1)} %get-tuple-element.70), channel_id=1, source_target_pairs={{0,96},{8,104},{16,112},{24,120},{32,0},{40,8},{48,16},{56,24},{64... | collective-permute-start | bytes 565256 | tf_op jit(solution)/shard_map/ppermute | solution.py:303
  176.3 10.4 %collective-permute-start.11 = (bf16[45,16,128]{2,1,0:T(8,128)(2,1)S(1)}, bf16[45,16,128]{2,1,0:T(8,128)(2,1)S(1)}, u32[]{:S(2)}, u32[]{:S(2)}) collective-permute-start(bf16[45,16,128]{2,1,0:T(8,128)(2,1)S(1)} %get-tuple-element.64), channel_id=1, source_target_pairs={{0,32},{8,40},{16,48},{24,56},{32,64},{40,72},{48,80},{56,88},{64,... | collective-permute-start | bytes 552968 | tf_op jit(solution)/shard_map/ppermute | solution.py:303
  176.8 13.2 %collective-permute-start.12 = (bf16[45,16,128]{2,1,0:T(8,128)(2,1)S(1)}, bf16[45,16,128]{2,1,0:T(8,128)(2,1)S(1)}, u32[]{:S(2)}, u32[]{:S(2)}) collective-permute-start(bf16[45,16,128]{2,1,0:T(8,128)(2,1)S(1)} %get-tuple-element.65), channel_id=1, source_target_pairs={{0,64},{8,72},{16,80},{24,88},{32,96},{40,104},{48,112},{56,120},{... | collective-permute-start | bytes 552968 | tf_op jit(solution)/shard_map/ppermute | solution.py:303
  177.6 33.9 %copy-start.9 = (bf16[4,46,16,128]{3,2,1,0:T(8,128)(2,1)S(1)}, bf16[4,46,16,128]{3,2,1,0:T(8,128)(2,1)}, u32[]{:S(2)}) copy-start(bf16[4,46,16,128]{3,2,1,0:T(8,128)(2,1)} %copy-done.8) | copy-start | bytes 2260996
  177.6 12.4 %collective-permute-start.13 = (bf16[45,16,128]{2,1,0:T(8,128)(2,1)S(1)}, bf16[45,16,128]{2,1,0:T(8,128)(2,1)S(1)}, u32[]{:S(2)}, u32[]{:S(2)}) collective-permute-start(bf16[45,16,128]{2,1,0:T(8,128)(2,1)S(1)} %get-tuple-element.66), channel_id=1, source_target_pairs={{0,96},{8,104},{16,112},{24,120},{32,0},{40,8},{48,16},{56,24},{64... | collective-permute-start | bytes 552968 | tf_op jit(solution)/shard_map/ppermute | solution.py:303
  182.2 8.0 %collective-permute-start.22 = (bf16[46,16,128]{2,1,0:T(8,128)(2,1)S(1)}, bf16[46,16,128]{2,1,0:T(8,128)(2,1)S(1)}, u32[]{:S(2)}, u32[]{:S(2)}) collective-permute-start(bf16[46,16,128]{2,1,0:T(8,128)(2,1)S(1)} %add_convert_fusion.1), channel_id=1, source_target_pairs={{0,16},{8,24},{16,0},{24,8},{32,48},{40,56},{48,32},{56,40},{64,80... | collective-permute-start | bytes 565256 | tf_op jit(solution)/shard_map/ppermute | solution.py:306
  190.1 5.4 %collective-permute-start.14 = (bf16[45,16,128]{2,1,0:T(8,128)(2,1)S(1)}, bf16[45,16,128]{2,1,0:T(8,128)(2,1)S(1)}, u32[]{:S(2)}, u32[]{:S(2)}) collective-permute-start(bf16[45,16,128]{2,1,0:T(8,128)(2,1)S(1)} %add_convert_fusion.5), channel_id=1, source_target_pairs={{0,16},{8,24},{16,0},{24,8},{32,48},{40,56},{48,32},{56,40},{64,80... | collective-permute-start | bytes 552968 | tf_op jit(solution)/shard_map/ppermute | solution.py:306
  190.3 9.1 %collective-permute-start.25 = (bf16[46,16,128]{2,1,0:T(8,128)(2,1)S(1)}, bf16[46,16,128]{2,1,0:T(8,128)(2,1)S(1)}, u32[]{:S(2)}, u32[]{:S(2)}) collective-permute-start(bf16[46,16,128]{2,1,0:T(8,128)(2,1)S(1)} %add_convert_fusion), channel_id=1, source_target_pairs={{0,32},{8,40},{16,48},{24,56},{32,64},{40,72},{48,80},{56,88},{64,... | collective-permute-start | bytes 565256 | tf_op jit(solution)/shard_map/ppermute | solution.py:309
  190.7 11.3 %collective-permute-start.24 = (bf16[46,16,128]{2,1,0:T(8,128)(2,1)S(1)}, bf16[46,16,128]{2,1,0:T(8,128)(2,1)S(1)}, u32[]{:S(2)}, u32[]{:S(2)}) collective-permute-start(bf16[46,16,128]{2,1,0:T(8,128)(2,1)S(1)} %add_convert_fusion), channel_id=1, source_target_pairs={{0,64},{8,72},{16,80},{24,88},{32,96},{40,104},{48,112},{56,120},{... | collective-permute-start | bytes 565256 | tf_op jit(solution)/shard_map/ppermute | solution.py:309
  193.7 8.4 %collective-permute-start.23 = (bf16[46,16,128]{2,1,0:T(8,128)(2,1)S(1)}, bf16[46,16,128]{2,1,0:T(8,128)(2,1)S(1)}, u32[]{:S(2)}, u32[]{:S(2)}) collective-permute-start(bf16[46,16,128]{2,1,0:T(8,128)(2,1)S(1)} %add_convert_fusion), channel_id=1, source_target_pairs={{0,96},{8,104},{16,112},{24,120},{32,0},{40,8},{48,16},{56,24},{64... | collective-permute-start | bytes 565256 | tf_op jit(solution)/shard_map/ppermute | solution.py:309
  195.5 11.4 %collective-permute-start.17 = (bf16[45,16,128]{2,1,0:T(8,128)(2,1)S(1)}, bf16[45,16,128]{2,1,0:T(8,128)(2,1)S(1)}, u32[]{:S(2)}, u32[]{:S(2)}) collective-permute-start(bf16[45,16,128]{2,1,0:T(8,128)(2,1)S(1)} %add_convert_fusion.4), channel_id=1, source_target_pairs={{0,32},{8,40},{16,48},{24,56},{32,64},{40,72},{48,80},{56,88},{64,... | collective-permute-start | bytes 552968 | tf_op jit(solution)/shard_map/ppermute | solution.py:309
  195.6 14.3 %collective-permute-start.16 = (bf16[45,16,128]{2,1,0:T(8,128)(2,1)S(1)}, bf16[45,16,128]{2,1,0:T(8,128)(2,1)S(1)}, u32[]{:S(2)}, u32[]{:S(2)}) collective-permute-start(bf16[45,16,128]{2,1,0:T(8,128)(2,1)S(1)} %add_convert_fusion.4), channel_id=1, source_target_pairs={{0,64},{8,72},{16,80},{24,88},{32,96},{40,104},{48,112},{56,120},{... | collective-permute-start | bytes 552968 | tf_op jit(solution)/shard_map/ppermute | solution.py:309
  199.3 10.6 %collective-permute-start.15 = (bf16[45,16,128]{2,1,0:T(8,128)(2,1)S(1)}, bf16[45,16,128]{2,1,0:T(8,128)(2,1)S(1)}, u32[]{:S(2)}, u32[]{:S(2)}) collective-permute-start(bf16[45,16,128]{2,1,0:T(8,128)(2,1)S(1)} %add_convert_fusion.4), channel_id=1, source_target_pairs={{0,96},{8,104},{16,112},{24,120},{32,0},{40,8},{48,16},{56,24},{64... | collective-permute-start | bytes 552968 | tf_op jit(solution)/shard_map/ppermute | solution.py:309
  202.1 11.4 %collective-permute-start.26 = (bf16[4,46,16,128]{3,2,1,0:T(8,128)(2,1)S(1)}, bf16[4,46,16,128]{3,2,1,0:T(8,128)(2,1)S(1)}, u32[]{:S(2)}, u32[]{:S(2)}) collective-permute-start(bf16[4,46,16,128]{3,2,1,0:T(8,128)(2,1)S(1)} %pad_maximum_fusion.1.mine_ref), channel_id=1, source_target_pairs={{0,8},{8,0},{16,24},{24,16},{32,40},{40,32},{48,56},{56,48},{64,72... | collective-permute-start | bytes 2261000 | tf_op jit(solution)/shard_map/ppermute | solution.py:313
  210.0 5.5 %collective-permute-start.18 = (bf16[4,45,16,128]{3,2,1,0:T(8,128)(2,1)S(1)}, bf16[4,45,16,128]{3,2,1,0:T(8,128)(2,1)S(1)}, u32[]{:S(2)}, u32[]{:S(2)}) collective-permute-start(bf16[4,45,16,128]{3,2,1,0:T(8,128)(2,1)S(1)} %pad_maximum_fusion.2.mine_ref), channel_id=1, source_target_pairs={{0,8},{8,0},{16,24},{24,16},{32,40},{40,32},{48,56},{56,48},{64,72... | collective-permute-start | bytes 2211848 | tf_op jit(solution)/shard_map/ppermute | solution.py:313

commit v5 on v4

--- a/solution.py
+++ b/solution.py
@@ -13,6 +13,7 @@
 VMEM_LIMIT = 20 * 1024 * 1024
 CHUNKS = (46, 46, 45)
 STEP = 23
+SHORT = 23
 
 
 def wave_table(length):
@@ -37,43 +38,61 @@
     return pltpu.CompilerParams(vmem_limit_bytes=VMEM_LIMIT)
 
 
-def mix_kernel(vertical_ref, member_ref, increment_ref, *refs):
-    *out_refs, rows, mixed = refs
-    levels, stored, _ = member_ref.shape
-    tiles = rows.shape[0]
-    product = member_ref[...].astype(F32) * increment_ref[...].astype(F32)
-    product = product.reshape(levels * stored, tiles * LANES)
-    for t in range(tiles):
-        rows[t] = product[:, t * LANES : (t + 1) * LANES]
+def mix_kernel(vertical_ref, basis_ref, member_ref, increment_ref, coeffs_ref, *refs):
+    *out_refs, total = refs
     vertical = vertical_ref[...]
-    for p in range(stored):
-        at = pl.ds(p, levels, stride=stored)
-        block = jnp.concatenate([rows[t, at, :] for t in range(tiles)], axis=1).astype(BF16)
-        block = jnp.dot(vertical, block, preferred_element_type=F32)
-        for t in range(tiles):
-            mixed[t, at, :] = block[:, t * LANES : (t + 1) * LANES]
-    start = 0
+    product = jnp.swapaxes(member_ref[...] * increment_ref[...], 0, 1)
+    mixed = [
+        jnp.dot(vertical, product[p], preferred_element_type=F32).astype(BF16)
+        for p in range(product.shape[0])
+    ]
+    mixed = jnp.swapaxes(jnp.stack(mixed, axis=0), 0, 1)
+    parts, start, stored, _ = coeffs_ref.shape
+    first = mixed[:start].reshape(start * stored, mixed.shape[-1])
+    more = jnp.dot(first, basis_ref[...], preferred_element_type=F32)
+    step, last = pl.program_id(0), pl.num_programs(0) - 1
+
+    @pl.when(step == 0)
+    def _():
+        total[...] = more
+
+    @pl.when((step > 0) & (step < last))
+    def _():
+        total[...] += more
+
+    @pl.when(step == last)
+    def _():
+        done = (total[...] + more).astype(BF16)
+        for s in range(parts):
+            coeffs_ref[s] = done[:, s * LANES : (s + 1) * LANES].reshape(start, stored, LANES)
+
     for out_ref in out_refs:
         size = out_ref.shape[0]
-        for t in range(tiles):
-            part = mixed[t, start * stored : (start + size) * stored, :].astype(BF16)
-            out_ref[:, :, t * LANES : (t + 1) * LANES] = part.reshape(size, stored, LANES)
+        out_ref[...] = mixed[start : start + size]
         start += size
 
 
-def mix(vertical, member, increment, chunks, width=256):
+def mix(vertical, basis, member, increment, chunks, width=256):
     levels, stored, columns = member.shape
+    parts = columns // LANES
     wide = lambda size: pl.BlockSpec((size, stored, width), lambda i: (0, 0, i))
+    first = (parts, chunks[0], stored, LANES)
     return pl.pallas_call(
         mix_kernel,
         grid=(columns // width,),
-        in_specs=[pl.BlockSpec((levels, levels), lambda i: (0, 0)), wide(levels), wide(levels)],
-        out_specs=[wide(size) for size in chunks],
-        out_shape=[jax.ShapeDtypeStruct((size, stored, columns), BF16) for size in chunks],
-        scratch_shapes=[pltpu.VMEM((width // LANES, levels * stored, LANES), F32)] * 2,
-        compiler_params=params(),
+        in_specs=[
+            pl.BlockSpec((levels, levels), lambda i: (0, 0)),
+            pl.BlockSpec((width, columns), lambda i: (i, 0)),
+            wide(levels),
+            wide(levels),
+        ],
+        out_specs=[pl.BlockSpec(first, lambda i: (0, 0, 0, 0))] + [wide(n) for n in chunks[1:]],
+        out_shape=[pltpu.HBM(first, BF16)]
+        + [pltpu.HBM((n, stored, columns), BF16) for n in chunks[1:]],
+        scratch_shapes=[pltpu.VMEM((chunks[0] * stored, columns), F32)],
+        compiler_params=pltpu.CompilerParams(vmem_limit_bytes=40 * 1024 * 1024),
         name="mix",
-    )(vertical, *[pltpu.with_memory_space_constraint(a, pltpu.HBM) for a in (member, increment)])
+    )(vertical, *[pltpu.with_memory_space_constraint(a, pltpu.HBM) for a in (basis, member, increment)])
 
 
 def cost(flops, values):
@@ -111,7 +130,7 @@
         compiler_params=params(),
         cost_estimate=cost(2 * x.size * columns, 2 * x.size + basis.size),
         name="forward",
-    )(basis, x)
+    )(basis, pltpu.with_memory_space_constraint(x, pltpu.HBM))
 
 
 def filter_kernel(basis_ref, basis_t_ref, weights_ref, x_ref, *refs):
@@ -128,7 +147,7 @@
 
 def filter_rows(basis, basis_t, weights, x, start, size, buffer=None):
     parts, _, stored, width = x.shape
-    step = min(STEP, size)
+    step = min(SHORT, size)
     first = start // step
     assert first * step == start
     whole = lambda a: pl.BlockSpec(a.shape, lambda i: (0, 0))
@@ -283,11 +302,11 @@
     chosen = (lax.broadcasted_iota(jnp.int32, (rows, rows), 0) == held).astype(BF16)
     basis_y = jnp.dot(jnp.asarray(wave_table(rows)), chosen, preferred_element_type=F32).astype(BF16)
     basis_yt = basis_y.T
-    localized = mix(vertical, member, increment, CHUNKS)
+    localized = mix(vertical, basis_xt, member, increment, CHUNKS)
     starts = [sum(CHUNKS[:i]) for i in range(len(CHUNKS))]
 
     def spread(i):
-        return forward(basis_xt, localized[i], CHUNKS[i - 1] if i else 0)
+        return forward(basis_xt, localized[i], CHUNKS[i - 1])
 
     def damp(i, came, buffer=None):
         start = CHUNKS[i - 1] if i else 0
@@ -316,7 +335,7 @@
         part = add(*scatter(keep))
         return add(part, cross(part))
 
-    came = swap(spread(0))
+    came = swap(localized[0])
     buffer = spread(1)
     came, buffer = tie((came, buffer))
     came = swap(damp(0, came, buffer))

time: 219 us -> 214 us (0.977)
  local copies, waits for them, and re-layouts: 10.8 us -> 5.84 us
    unnamed x32 -> x24, local copies, waits for them, and re-layouts: 10.6 us -> 5.65 us
    pallas_call x3 -> x2, Pallas kernels: 8.42 us -> 7.87 us  [forward(): pl.pallas_call(forward_kernel, grid=(pl.cdiv(size, step),), in_specs=[pl....]
  transfers between devices with their start and end apart: 31 -> 31, of which waited for: 17 -> 17; matrix products, arithmetic and copies ran while one was open for 1% -> 1% of each run, Pallas kernels for 10% -> 11%
where the time goes in v5:
time: 214 us
  waiting for transfers between devices  89.9 us (42%)
  starting transfers between devices  67.4 us (31%)
  Pallas kernels  49.3 us (23%)
  local copies, waits for them, and re-layouts  5.84 us (3%)
    all_to_all x4, waiting for transfers between devices, swap(): return lax.all_to_all(pieces, 'space', 0, 0, tiled=True)  48.7 us
    all_to_all x4, starting transfers between devices, swap(): return lax.all_to_all(pieces, 'space', 0, 0, tiled=True)  23.8 us
    ppermute x9, waiting for transfers between devices, scatter(): lax.ppermute(kept[dy], 'mem', mem_to(dy, 0, 0))  18.1 us
    pallas_call x3, Pallas kernels, backward(): pl.pallas_call(backward_kernel, grid_spec=pltpu.PrefetchScalarGridSpec(nu...  13.4 us
    ppermute x9, starting transfers between devices, scatter(): lax.ppermute(kept[dy], 'mem', mem_to(dy, 0, 0))  13 us
    ppermute x9, starting transfers between devices, collect(): lax.ppermute(part, 'mem', mem_to(-dy, 0, 0))  12.9 us
    ppermute x3, waiting for transfers between devices, cross(): return lax.ppermute(part, 'mem', mem_to(0, 1, 0))  12.5 us
    ppermute x3, starting transfers between devices, fold(): return pair_sum(keep, lax.ppermute(give, 'mem', mem_to(0, 0, 1)))  12.2 us
  transfers between devices with their start and end apart: 31, of which 17 were waited for; matrix products, arithmetic and copies ran while one was open for 1% of the time, Pallas kernels for 11%

profile of v5, /device:TPU:1, one launch (start us, length us, event | category | flops | bytes accessed | tf_op | source)
XLA Modules:
  0.0 213.7 jit_solution(16074648664114420754)
XLA Ops:
  0.9 10.3 %mix.1 = (bf16[8,46,16,128]{3,2,1,0:T(8,128)(2,1)}, bf16[46,16,1024]{2,1,0:T(8,128)(2,1)}, bf16[45,16,1024]{2,1,0:T(8,128)(2,1)}) custom-call(bf16[137,137]{1,0:T(8,128)(2,1)S(1)} %copy-done.7, bf16[1024,1024]{1,0:T(8,128)(2,1)} %constant.69.clone.basis_ref, bf16[137,16,1024]{2,1,0:T(8,128)(2,1)} %bitcast.24, bf16[137,16,1024]{2,1,0:T(8,128)(2,1)} %increment_ref.1), custom_call_target="tpu_custom_call" | custom-call | tf_op jit(solution)/shard_map/mix/pallas_call | solution.py:80
  11.2 8.5 %all-to-all-start = ((bf16[8,46,16,128]{3,2,1,0:T(8,128)(2,1)}), bf16[8,46,16,128]{3,2,1,0:T(8,128)(2,1)}, u32[]{:S(2)}, u32[]{:S(2)}) async-start(bf16[8,46,16,128]{3,2,1,0:T(8,128)(2,1)} %get-tuple-element.39), calls=%async_computation | async-start | bytes 3014656 | tf_op jit(solution)/shard_map/all_to_all | solution.py:280
  20.0 4.0 %forward.2.refs_0_ = bf16[8,92,16,128]{3,2,1,0:T(8,128)(2,1)} custom-call(bf16[1024,1024]{1,0:T(8,128)(2,1)S(1)} %copy-done.2, bf16[46,16,1024]{2,1,0:T(8,128)(2,1)} %get-tuple-element.40.x_ref), custom_call_target="tpu_custom_call" | custom-call | flops 1543503872 | bytes 5111808 | tf_op jit(solution)/shard_map/forward/pallas_call | solution.py:121
  24.0 17.0 %all-to-all-done.x_ref = bf16[8,46,16,128]{3,2,1,0:T(8,128)(2,1)} async-done(((bf16[8,46,16,128]{3,2,1,0:T(8,128)(2,1)}), bf16[8,46,16,128]{3,2,1,0:T(8,128)(2,1)}, u32[]{:S(2)}, u32[]{:S(2)}) %all-to-all-start) | async-done | bytes 1507360 | tf_op jit(solution)/shard_map/all_to_all | solution.py:280
  41.0 3.1 %filter.3 = bf16[8,92,16,128]{3,2,1,0:T(8,128)(2,1)} custom-call(bf16[128,128]{1,0:T(8,128)(2,1)S(1)} %copy.15.basis_ref, bf16[128,128]{1,0:T(8,128)(2,1)S(1)} %convolution_convert_fusion.basis_t_ref, f32[128,128]{1,0:T(8,128)S(1)} %copy-done.6, bf16[8,46,16,128]{3,2,1,0:T(8,128)(2,1)} %all-to-all-done.x_ref, ...), custom_call_target="tpu_custom_call", output_to_operand_aliasing={{}: (4, {})} | custom-call | flops 385875968 | bytes 3014656 | tf_op jit(solution)/shard_map/filter/pallas_call | solution.py:157
  44.1 3.8 %all-to-all-start.1 = ((bf16[8,92,16,128]{3,2,1,0:T(8,128)(2,1)}), bf16[8,92,16,128]{3,2,1,0:T(8,128)(2,1)S(1)}, u32[]{:S(2)}, u32[]{:S(2)}) async-start(bf16[8,92,16,128]{3,2,1,0:T(8,128)(2,1)} %filter.3), calls=%async_computation.1 | async-start | bytes 6029312 | tf_op jit(solution)/shard_map/all_to_all | solution.py:280
  47.9 1.6 copy-done.3
  49.5 3.9 %forward.3.refs_0_ = bf16[8,91,16,128]{3,2,1,0:T(8,128)(2,1)} custom-call(bf16[1024,1024]{1,0:T(8,128)(2,1)S(1)} %copy-done.3, bf16[45,16,1024]{2,1,0:T(8,128)(2,1)} %get-tuple-element.43.x_ref), custom_call_target="tpu_custom_call" | custom-call | flops 1509949440 | bytes 5046272 | tf_op jit(solution)/shard_map/forward/pallas_call | solution.py:121
  53.4 31.1 %all-to-all-done.1.x_ref = bf16[8,92,16,128]{3,2,1,0:T(8,128)(2,1)S(1)} async-done(((bf16[8,92,16,128]{3,2,1,0:T(8,128)(2,1)}), bf16[8,92,16,128]{3,2,1,0:T(8,128)(2,1)S(1)}, u32[]{:S(2)}, u32[]{:S(2)}) %all-to-all-start.1) | async-done | bytes 3014688 | tf_op jit(solution)/shard_map/all_to_all | solution.py:280
  84.5 2.1 filter.4
  86.7 4.5 %all-to-all-start.2 = ((bf16[8,91,16,128]{3,2,1,0:T(8,128)(2,1)}), bf16[8,91,16,128]{3,2,1,0:T(8,128)(2,1)}, u32[]{:S(2)}, u32[]{:S(2)}) async-start(bf16[8,91,16,128]{3,2,1,0:T(8,128)(2,1)} %filter.4), calls=%async_computation.2 | async-start | bytes 5963776 | tf_op jit(solution)/shard_map/all_to_all | solution.py:280
  91.3 1.6 copy-done
  92.9 4.1 %backward.3 = (bf16[4,46,16,128]{3,2,1,0:T(8,128)(2,1)S(1)}, bf16[4,46,16,128]{3,2,1,0:T(8,128)(2,1)S(1)}) custom-call(s32[8]{0:T(128)S(1)} %stack.80.tiles_ref, bf16[1024,1024]{1,0:T(8,128)(2,1)S(1)} %copy-done, bf16[137,16,1024]{2,1,0:T(8,128)(2,1)} %bitcast.25, bf16[8,92,16,128]{3,2,1,0:T(8,128)(2,1)S(1)} %all-to-all-done.1.x_ref), custom_call_target="tpu_custom_call" | custom-call | flops 1543503872 | bytes 6619136 | tf_op jit(solution)/shard_map/backward/pallas_call | solution.py:191
  97.0 2.7 %collective-permute-start = (bf16[4,46,16,128]{3,2,1,0:T(8,128)(2,1)S(1)}, bf16[4,46,16,128]{3,2,1,0:T(8,128)(2,1)S(1)}, u32[]{:S(2)}, u32[]{:S(2)}) collective-permute-start(bf16[4,46,16,128]{3,2,1,0:T(8,128)(2,1)S(1)} %get-tuple-element.47), channel_id=1, source_target_pairs={{0,8},{8,0},{16,24},{24,16},{32,40},{40,32},{48,56},{56,48},{64,72... | collective-permute-start | bytes 2261000 | tf_op jit(solution)/shard_map/ppermute | solution.py:319
  99.7 1.9 collective-permute-done.b_ref
  101.9 1.4 collective-permute-start.1
  103.3 2.6 %collective-permute-start.2 = (bf16[46,16,128]{2,1,0:T(8,128)(2,1)S(1)}, bf16[46,16,128]{2,1,0:T(8,128)(2,1)S(1)}, u32[]{:S(2)}, u32[]{:S(2)}) collective-permute-start(bf16[46,16,128]{2,1,0:T(8,128)(2,1)S(1)} %get-tuple-element.50), channel_id=1, source_target_pairs={{0,64},{8,72},{16,80},{24,88},{32,96},{40,104},{48,112},{56,120},{... | collective-permute-start | bytes 565256 | tf_op jit(solution)/shard_map/ppermute | solution.py:322
  106.9 2.4 %collective-permute-done.1 = bf16[46,16,128]{2,1,0:T(8,128)(2,1)S(1)} collective-permute-done((bf16[46,16,128]{2,1,0:T(8,128)(2,1)S(1)}, bf16[46,16,128]{2,1,0:T(8,128)(2,1)S(1)}, u32[]{:S(2)}, u32[]{:S(2)}) %collective-permute-start.1) | collective-permute-done | bytes 188448 | tf_op jit(solution)/shard_map/ppermute | solution.py:322
  109.4 5.1 %collective-permute-done.2 = bf16[46,16,128]{2,1,0:T(8,128)(2,1)S(1)} collective-permute-done((bf16[46,16,128]{2,1,0:T(8,128)(2,1)S(1)}, bf16[46,16,128]{2,1,0:T(8,128)(2,1)S(1)}, u32[]{:S(2)}, u32[]{:S(2)}) %collective-permute-start.2) | collective-permute-done | bytes 188448 | tf_op jit(solution)/shard_map/ppermute | solution.py:322
  115.0 11.4 %collective-permute-done.4 = bf16[46,16,128]{2,1,0:T(8,128)(2,1)S(1)} collective-permute-done((bf16[46,16,128]{2,1,0:T(8,128)(2,1)S(1)}, bf16[46,16,128]{2,1,0:T(8,128)(2,1)S(1)}, u32[]{:S(2)}, u32[]{:S(2)}) %collective-permute-start.4) | collective-permute-done | bytes 188448 | tf_op jit(solution)/shard_map/ppermute | solution.py:325
  126.8 3.3 %filter.5 = bf16[8,45,16,128]{3,2,1,0:T(8,128)(2,1)} custom-call(bf16[128,128]{1,0:T(8,128)(2,1)S(1)} %copy.15.basis_ref, bf16[128,128]{1,0:T(8,128)(2,1)S(1)} %convolution_convert_fusion.basis_t_ref, f32[128,128]{1,0:T(8,128)S(1)} %copy-done.6, bf16[8,91,16,128]{3,2,1,0:T(8,128)(2,1)} %all-to-all-done.2.x_ref), custom_call_target="tpu_custom_call" | custom-call | flops 377487360 | bytes 2949120 | tf_op jit(solution)/shard_map/filter/pallas_call | solution.py:157
  130.1 6.9 %all-to-all-start.3 = ((bf16[8,45,16,128]{3,2,1,0:T(8,128)(2,1)}), bf16[8,45,16,128]{3,2,1,0:T(8,128)(2,1)}, u32[]{:S(2)}, u32[]{:S(2)}) async-start(bf16[8,45,16,128]{3,2,1,0:T(8,128)(2,1)} %filter.5), calls=%async_computation.3 | async-start | bytes 2949120 | tf_op jit(solution)/shard_map/all_to_all | solution.py:280
  137.1 1.3 collective-permute-start.8
  138.4 2.6 %collective-permute-start.7 = (bf16[46,16,128]{2,1,0:T(8,128)(2,1)S(1)}, bf16[46,16,128]{2,1,0:T(8,128)(2,1)S(1)}, u32[]{:S(2)}, u32[]{:S(2)}) collective-permute-start(bf16[46,16,128]{2,1,0:T(8,128)(2,1)S(1)} %add_convert_fusion.2), channel_id=1, source_target_pairs={{0,64},{8,72},{16,80},{24,88},{32,96},{40,104},{48,112},{56,120},{... | collective-permute-start | bytes 565256 | tf_op jit(solution)/shard_map/ppermute | solution.py:328
  141.0 1.1 collective-permute-start.6
  142.0 4.4 %backward.4 = (bf16[4,46,16,128]{3,2,1,0:T(8,128)(2,1)S(1)}, bf16[4,46,16,128]{3,2,1,0:T(8,128)(2,1)S(1)}) custom-call(s32[8]{0:T(128)S(1)} %stack.80.tiles_ref, bf16[1024,1024]{1,0:T(8,128)(2,1)S(1)} %copy-done.1, bf16[137,16,1024]{2,1,0:T(8,128)(2,1)} %bitcast.26, bf16[8,91,16,128]{3,2,1,0:T(8,128)(2,1)} %all-to-all-done.2.x_ref), custom_call_target="tpu_custom_call" | custom-call | flops 1543503872 | bytes 6619136 | tf_op jit(solution)/shard_map/backward/pallas_call | solution.py:191
  146.4 4.7 %collective-permute-start.5 = (bf16[4,46,16,128]{3,2,1,0:T(8,128)(2,1)S(1)}, bf16[4,46,16,128]{3,2,1,0:T(8,128)(2,1)S(1)}, u32[]{:S(2)}, u32[]{:S(2)}) collective-permute-start(bf16[4,46,16,128]{3,2,1,0:T(8,128)(2,1)S(1)} %get-tuple-element.54), channel_id=1, source_target_pairs={{0,8},{8,0},{16,24},{24,16},{32,40},{40,32},{48,56},{56,48},{64,72... | collective-permute-start | bytes 2261000 | tf_op jit(solution)/shard_map/ppermute | solution.py:319
  151.6 1.5 collective-permute-done.5.b_ref
  155.2 4.9 %backward.5 = (bf16[4,45,16,128]{3,2,1,0:T(8,128)(2,1)S(1)}, bf16[4,45,16,128]{3,2,1,0:T(8,128)(2,1)S(1)}) custom-call(s32[8]{0:T(128)S(1)} %stack.80.tiles_ref, bf16[1024,1024]{1,0:T(8,128)(2,1)S(1)} %copy-done.1, bf16[137,16,1024]{2,1,0:T(8,128)(2,1)} %bitcast.27, bf16[8,45,16,128]{3,2,1,0:T(8,128)(2,1)} %all-to-all-done.3.x_ref), custom_call_target="tpu_custom_call" | custom-call | flops 1509949440 | bytes 6520832 | tf_op jit(solution)/shard_map/backward/pallas_call | solution.py:191
  160.1 4.8 %collective-permute-start.10 = (bf16[4,45,16,128]{3,2,1,0:T(8,128)(2,1)S(1)}, bf16[4,45,16,128]{3,2,1,0:T(8,128)(2,1)S(1)}, u32[]{:S(2)}, u32[]{:S(2)}) collective-permute-start(bf16[4,45,16,128]{3,2,1,0:T(8,128)(2,1)S(1)} %get-tuple-element.62), channel_id=1, source_target_pairs={{0,8},{8,0},{16,24},{24,16},{32,40},{40,32},{48,56},{56,48},{64,72... | collective-permute-start | bytes 2211848 | tf_op jit(solution)/shard_map/ppermute | solution.py:319
  164.9 1.3 collective-permute-start.19
  166.3 2.6 %collective-permute-start.20 = (bf16[46,16,128]{2,1,0:T(8,128)(2,1)S(1)}, bf16[46,16,128]{2,1,0:T(8,128)(2,1)S(1)}, u32[]{:S(2)}, u32[]{:S(2)}) collective-permute-start(bf16[46,16,128]{2,1,0:T(8,128)(2,1)S(1)} %get-tuple-element.69), channel_id=1, source_target_pairs={{0,64},{8,72},{16,80},{24,88},{32,96},{40,104},{48,112},{56,120},{... | collective-permute-start | bytes 565256 | tf_op jit(solution)/shard_map/ppermute | solution.py:322
  169.9 2.0 pair_sum.5
  173.2 1.7 collective-permute-start.13
  174.9 2.8 %collective-permute-done.20 = bf16[46,16,128]{2,1,0:T(8,128)(2,1)S(1)} collective-permute-done((bf16[46,16,128]{2,1,0:T(8,128)(2,1)S(1)}, bf16[46,16,128]{2,1,0:T(8,128)(2,1)S(1)}, u32[]{:S(2)}, u32[]{:S(2)}) %collective-permute-start.20) | collective-permute-done | bytes 188448 | tf_op jit(solution)/shard_map/ppermute | solution.py:322
  177.9 4.4 %collective-permute-done.11 = bf16[45,16,128]{2,1,0:T(8,128)(2,1)S(1)} collective-permute-done((bf16[45,16,128]{2,1,0:T(8,128)(2,1)S(1)}, bf16[45,16,128]{2,1,0:T(8,128)(2,1)S(1)}, u32[]{:S(2)}, u32[]{:S(2)}) %collective-permute-start.11) | collective-permute-done | bytes 184352 | tf_op jit(solution)/shard_map/ppermute | solution.py:322
  182.4 3.3 %collective-permute-done.12 = bf16[45,16,128]{2,1,0:T(8,128)(2,1)S(1)} collective-permute-done((bf16[45,16,128]{2,1,0:T(8,128)(2,1)S(1)}, bf16[45,16,128]{2,1,0:T(8,128)(2,1)S(1)}, u32[]{:S(2)}, u32[]{:S(2)}) %collective-permute-start.12) | collective-permute-done | bytes 184352 | tf_op jit(solution)/shard_map/ppermute | solution.py:322
  186.4 2.9 %collective-permute-start.24 = (bf16[46,16,128]{2,1,0:T(8,128)(2,1)S(1)}, bf16[46,16,128]{2,1,0:T(8,128)(2,1)S(1)}, u32[]{:S(2)}, u32[]{:S(2)}) collective-permute-start(bf16[46,16,128]{2,1,0:T(8,128)(2,1)S(1)} %add_convert_fusion), channel_id=1, source_target_pairs={{0,64},{8,72},{16,80},{24,88},{32,96},{40,104},{48,112},{56,120},{... | collective-permute-start | bytes 565256 | tf_op jit(solution)/shard_map/ppermute | solution.py:328
  190.1 1.1 collective-permute-done.14
  191.3 3.7 %collective-permute-start.16 = (bf16[45,16,128]{2,1,0:T(8,128)(2,1)S(1)}, bf16[45,16,128]{2,1,0:T(8,128)(2,1)S(1)}, u32[]{:S(2)}, u32[]{:S(2)}) collective-permute-start(bf16[45,16,128]{2,1,0:T(8,128)(2,1)S(1)} %add_convert_fusion.4), channel_id=1, source_target_pairs={{0,64},{8,72},{16,80},{24,88},{32,96},{40,104},{48,112},{56,120},{... | collective-permute-start | bytes 552968 | tf_op jit(solution)/shard_map/ppermute | solution.py:328
  195.0 2.7 %collective-permute-done.24 = bf16[46,16,128]{2,1,0:T(8,128)(2,1)S(1)} collective-permute-done((bf16[46,16,128]{2,1,0:T(8,128)(2,1)S(1)}, bf16[46,16,128]{2,1,0:T(8,128)(2,1)S(1)}, u32[]{:S(2)}, u32[]{:S(2)}) %collective-permute-start.24) | collective-permute-done | bytes 188448 | tf_op jit(solution)/shard_map/ppermute | solution.py:328
  197.8 3.2 %collective-permute-start.26 = (bf16[4,46,16,128]{3,2,1,0:T(8,128)(2,1)S(1)}, bf16[4,46,16,128]{3,2,1,0:T(8,128)(2,1)S(1)}, u32[]{:S(2)}, u32[]{:S(2)}) collective-permute-start(bf16[4,46,16,128]{3,2,1,0:T(8,128)(2,1)S(1)} %pad_maximum_fusion.1.mine_ref), channel_id=1, source_target_pairs={{0,8},{8,0},{16,24},{24,16},{32,40},{40,32},{48,56},{56,48},{64,72... | collective-permute-start | bytes 2261000 | tf_op jit(solution)/shard_map/ppermute | solution.py:332
  201.0 1.5 collective-permute-done.17
  202.5 3.0 %collective-permute-done.16 = bf16[45,16,128]{2,1,0:T(8,128)(2,1)S(1)} collective-permute-done((bf16[45,16,128]{2,1,0:T(8,128)(2,1)S(1)}, bf16[45,16,128]{2,1,0:T(8,128)(2,1)S(1)}, u32[]{:S(2)}, u32[]{:S(2)}) %collective-permute-start.16) | collective-permute-done | bytes 184352 | tf_op jit(solution)/shard_map/ppermute | solution.py:328
  205.7 1.5 collective-permute-start.18
  207.1 2.0 place.3.refs_0_
  209.1 2.0 place.4.refs_0_
  211.2 2.5 %place.5 = bf16[137,16,1024]{2,1,0:T(8,128)(2,1)} custom-call(s32[8]{0:T(128)S(1)} %stack.80.tiles_ref, bf16[4,45,16,128]{3,2,1,0:T(8,128)(2,1)S(1)} %pad_maximum_fusion.2.mine_ref, bf16[4,45,16,128]{3,2,1,0:T(8,128)(2,1)S(1)} %collective-permute-done.18.theirs_ref, bf16[137,16,1024]{2,1,0:T(8,128)(2,1)} %place.4.refs_0_), custom_call_target="tpu_custom_call", output_to_operand_aliasing={{}: (3, {})} | custom-call | bytes 2949120 | tf_op jit(solution)/shard_map/place/pallas_call | solution.py:247
  (65 shorter events, 10.5 us)
Async XLA Ops:
  0.0 0.9 copy-start.7
  11.2 8.5 %copy-start.10 = (bf16[128,128]{1,0:T(8,128)(2,1)S(1)}, bf16[128,128]{1,0:T(8,128)(2,1)}, u32[]{:S(2)}) copy-start(bf16[128,128]{1,0:T(8,128)(2,1)} %constant.70.clone) | copy-start | bytes 98308
  11.2 8.5 %copy-start.11 = (s32[128]{0:T(128)S(1)}, s32[128]{0:T(128)}, u32[]{:S(2)}) copy-start(s32[128]{0:T(128)} %param.12) | copy-start | bytes 1540
  11.2 8.8 %copy-start.2 = (bf16[1024,1024]{1,0:T(8,128)(2,1)S(1)}, bf16[1024,1024]{1,0:T(8,128)(2,1)}, u32[]{:S(2)}) copy-start(bf16[1024,1024]{1,0:T(8,128)(2,1)} %constant.69.clone.basis_ref) | copy-start | bytes 6291460
  11.2 29.8 %all-to-all-start = ((bf16[8,46,16,128]{3,2,1,0:T(8,128)(2,1)}), bf16[8,46,16,128]{3,2,1,0:T(8,128)(2,1)}, u32[]{:S(2)}, u32[]{:S(2)}) async-start(bf16[8,46,16,128]{3,2,1,0:T(8,128)(2,1)} %get-tuple-element.39), calls=%async_computation | async-start | bytes 3014656 | tf_op jit(solution)/shard_map/all_to_all | solution.py:280
  20.0 21.0 %copy-start.6 = (f32[128,128]{1,0:T(8,128)S(1)}, f32[128,128]{1,0:T(8,128)}, u32[]{:S(2)}) copy-start(f32[128,128]{1,0:T(8,128)} %weights_ref.5) | copy-start | bytes 196612
  44.1 40.5 %all-to-all-start.1 = ((bf16[8,92,16,128]{3,2,1,0:T(8,128)(2,1)}), bf16[8,92,16,128]{3,2,1,0:T(8,128)(2,1)S(1)}, u32[]{:S(2)}, u32[]{:S(2)}) async-start(bf16[8,92,16,128]{3,2,1,0:T(8,128)(2,1)} %filter.3), calls=%async_computation.1 | async-start | bytes 6029312 | tf_op jit(solution)/shard_map/all_to_all | solution.py:280
  47.9 1.6 copy-start.3
  86.7 40.2 %all-to-all-start.2 = ((bf16[8,91,16,128]{3,2,1,0:T(8,128)(2,1)}), bf16[8,91,16,128]{3,2,1,0:T(8,128)(2,1)}, u32[]{:S(2)}, u32[]{:S(2)}) async-start(bf16[8,91,16,128]{3,2,1,0:T(8,128)(2,1)} %filter.4), calls=%async_computation.2 | async-start | bytes 5963776 | tf_op jit(solution)/shard_map/all_to_all | solution.py:280
  91.3 1.6 copy-start
  97.0 4.6 %collective-permute-start = (bf16[4,46,16,128]{3,2,1,0:T(8,128)(2,1)S(1)}, bf16[4,46,16,128]{3,2,1,0:T(8,128)(2,1)S(1)}, u32[]{:S(2)}, u32[]{:S(2)}) collective-permute-start(bf16[4,46,16,128]{3,2,1,0:T(8,128)(2,1)S(1)} %get-tuple-element.47), channel_id=1, source_target_pairs={{0,8},{8,0},{16,24},{24,16},{32,40},{40,32},{48,56},{56,48},{64,72... | collective-permute-start | bytes 2261000 | tf_op jit(solution)/shard_map/ppermute | solution.py:319
  101.9 7.5 %collective-permute-start.1 = (bf16[46,16,128]{2,1,0:T(8,128)(2,1)S(1)}, bf16[46,16,128]{2,1,0:T(8,128)(2,1)S(1)}, u32[]{:S(2)}, u32[]{:S(2)}) collective-permute-start(bf16[46,16,128]{2,1,0:T(8,128)(2,1)S(1)} %get-tuple-element.49), channel_id=1, source_target_pairs={{0,32},{8,40},{16,48},{24,56},{32,64},{40,72},{48,80},{56,88},{64,... | collective-permute-start | bytes 565256 | tf_op jit(solution)/shard_map/ppermute | solution.py:322
  103.3 11.2 %collective-permute-start.2 = (bf16[46,16,128]{2,1,0:T(8,128)(2,1)S(1)}, bf16[46,16,128]{2,1,0:T(8,128)(2,1)S(1)}, u32[]{:S(2)}, u32[]{:S(2)}) collective-permute-start(bf16[46,16,128]{2,1,0:T(8,128)(2,1)S(1)} %get-tuple-element.50), channel_id=1, source_target_pairs={{0,64},{8,72},{16,80},{24,88},{32,96},{40,104},{48,112},{56,120},{... | collective-permute-start | bytes 565256 | tf_op jit(solution)/shard_map/ppermute | solution.py:322
  105.9 8.6 %collective-permute-start.3 = (bf16[46,16,128]{2,1,0:T(8,128)(2,1)S(1)}, bf16[46,16,128]{2,1,0:T(8,128)(2,1)S(1)}, u32[]{:S(2)}, u32[]{:S(2)}) collective-permute-start(bf16[46,16,128]{2,1,0:T(8,128)(2,1)S(1)} %get-tuple-element.51), channel_id=1, source_target_pairs={{0,96},{8,104},{16,112},{24,120},{32,0},{40,8},{48,16},{56,24},{64... | collective-permute-start | bytes 565256 | tf_op jit(solution)/shard_map/ppermute | solution.py:322
  114.6 11.8 %collective-permute-start.4 = (bf16[46,16,128]{2,1,0:T(8,128)(2,1)S(1)}, bf16[46,16,128]{2,1,0:T(8,128)(2,1)S(1)}, u32[]{:S(2)}, u32[]{:S(2)}) collective-permute-start(bf16[46,16,128]{2,1,0:T(8,128)(2,1)S(1)} %add_convert_fusion.3), channel_id=1, source_target_pairs={{0,16},{8,24},{16,0},{24,8},{32,48},{40,56},{48,32},{56,40},{64,80... | collective-permute-start | bytes 565256 | tf_op jit(solution)/shard_map/ppermute | solution.py:325
  126.5 15.6 %copy-start.1 = (bf16[1024,1024]{1,0:T(8,128)(2,1)S(1)}, bf16[1024,1024]{1,0:T(8,128)(2,1)}, u32[]{:S(2)}) copy-start(bf16[1024,1024]{1,0:T(8,128)(2,1)} %constant.68.clone.basis_ref) | copy-start | bytes 6291460
  130.1 25.0 %all-to-all-start.3 = ((bf16[8,45,16,128]{3,2,1,0:T(8,128)(2,1)}), bf16[8,45,16,128]{3,2,1,0:T(8,128)(2,1)}, u32[]{:S(2)}, u32[]{:S(2)}) async-start(bf16[8,45,16,128]{3,2,1,0:T(8,128)(2,1)} %filter.5), calls=%async_computation.3 | async-start | bytes 2949120 | tf_op jit(solution)/shard_map/all_to_all | solution.py:280
  137.1 14.1 %collective-permute-start.8 = (bf16[46,16,128]{2,1,0:T(8,128)(2,1)S(1)}, bf16[46,16,128]{2,1,0:T(8,128)(2,1)S(1)}, u32[]{:S(2)}, u32[]{:S(2)}) collective-permute-start(bf16[46,16,128]{2,1,0:T(8,128)(2,1)S(1)} %add_convert_fusion.2), channel_id=1, source_target_pairs={{0,32},{8,40},{16,48},{24,56},{32,64},{40,72},{48,80},{56,88},{64,... | collective-permute-start | bytes 565256 | tf_op jit(solution)/shard_map/ppermute | solution.py:328
  138.4 12.8 %collective-permute-start.7 = (bf16[46,16,128]{2,1,0:T(8,128)(2,1)S(1)}, bf16[46,16,128]{2,1,0:T(8,128)(2,1)S(1)}, u32[]{:S(2)}, u32[]{:S(2)}) collective-permute-start(bf16[46,16,128]{2,1,0:T(8,128)(2,1)S(1)} %add_convert_fusion.2), channel_id=1, source_target_pairs={{0,64},{8,72},{16,80},{24,88},{32,96},{40,104},{48,112},{56,120},{... | collective-permute-start | bytes 565256 | tf_op jit(solution)/shard_map/ppermute | solution.py:328
  141.0 10.2 %collective-permute-start.6 = (bf16[46,16,128]{2,1,0:T(8,128)(2,1)S(1)}, bf16[46,16,128]{2,1,0:T(8,128)(2,1)S(1)}, u32[]{:S(2)}, u32[]{:S(2)}) collective-permute-start(bf16[46,16,128]{2,1,0:T(8,128)(2,1)S(1)} %add_convert_fusion.2), channel_id=1, source_target_pairs={{0,96},{8,104},{16,112},{24,120},{32,0},{40,8},{48,16},{56,24},{64... | collective-permute-start | bytes 565256 | tf_op jit(solution)/shard_map/ppermute | solution.py:328
  146.4 6.6 %collective-permute-start.5 = (bf16[4,46,16,128]{3,2,1,0:T(8,128)(2,1)S(1)}, bf16[4,46,16,128]{3,2,1,0:T(8,128)(2,1)S(1)}, u32[]{:S(2)}, u32[]{:S(2)}) collective-permute-start(bf16[4,46,16,128]{3,2,1,0:T(8,128)(2,1)S(1)} %get-tuple-element.54), channel_id=1, source_target_pairs={{0,8},{8,0},{16,24},{24,16},{32,40},{40,32},{48,56},{56,48},{64,72... | collective-permute-start | bytes 2261000 | tf_op jit(solution)/shard_map/ppermute | solution.py:319
  151.3 2.8 %collective-permute-start.9 = (bf16[4,46,16,128]{3,2,1,0:T(8,128)(2,1)S(1)}, bf16[4,46,16,128]{3,2,1,0:T(8,128)(2,1)S(1)}, u32[]{:S(2)}, u32[]{:S(2)}) collective-permute-start(bf16[4,46,16,128]{3,2,1,0:T(8,128)(2,1)S(1)} %pad_maximum_fusion.mine_ref), channel_id=1, source_target_pairs={{0,8},{8,0},{16,24},{24,16},{32,40},{40,32},{48,56},{56,48},{64,72... | collective-permute-start | bytes 2261000 | tf_op jit(solution)/shard_map/ppermute | solution.py:332
  153.3 0.7 copy-start.8
  154.1 0.9 copy-start.4
  155.2 9.8 %copy-start.9 = (bf16[46,16,128]{2,1,0:T(8,128)(2,1)S(1)}, bf16[46,16,128]{2,1,0:T(8,128)(2,1)}, u32[]{:S(2)}) copy-start(bf16[46,16,128]{2,1,0:T(8,128)(2,1)} %copy-done.8) | copy-start | bytes 565252
  160.1 9.8 %collective-permute-start.10 = (bf16[4,45,16,128]{3,2,1,0:T(8,128)(2,1)S(1)}, bf16[4,45,16,128]{3,2,1,0:T(8,128)(2,1)S(1)}, u32[]{:S(2)}, u32[]{:S(2)}) collective-permute-start(bf16[4,45,16,128]{3,2,1,0:T(8,128)(2,1)S(1)} %get-tuple-element.62), channel_id=1, source_target_pairs={{0,8},{8,0},{16,24},{24,16},{32,40},{40,32},{48,56},{56,48},{64,72... | collective-permute-start | bytes 2211848 | tf_op jit(solution)/shard_map/ppermute | solution.py:319
  164.9 8.3 %collective-permute-start.19 = (bf16[46,16,128]{2,1,0:T(8,128)(2,1)S(1)}, bf16[46,16,128]{2,1,0:T(8,128)(2,1)S(1)}, u32[]{:S(2)}, u32[]{:S(2)}) collective-permute-start(bf16[46,16,128]{2,1,0:T(8,128)(2,1)S(1)} %copy-done.9), channel_id=1, source_target_pairs={{0,32},{8,40},{16,48},{24,56},{32,64},{40,72},{48,80},{56,88},{64,... | collective-permute-start | bytes 565256 | tf_op jit(solution)/shard_map/ppermute | solution.py:322
  166.3 11.5 %collective-permute-start.20 = (bf16[46,16,128]{2,1,0:T(8,128)(2,1)S(1)}, bf16[46,16,128]{2,1,0:T(8,128)(2,1)S(1)}, u32[]{:S(2)}, u32[]{:S(2)}) collective-permute-start(bf16[46,16,128]{2,1,0:T(8,128)(2,1)S(1)} %get-tuple-element.69), channel_id=1, source_target_pairs={{0,64},{8,72},{16,80},{24,88},{32,96},{40,104},{48,112},{56,120},{... | collective-permute-start | bytes 565256 | tf_op jit(solution)/shard_map/ppermute | solution.py:322
  168.9 8.9 %collective-permute-start.21 = (bf16[46,16,128]{2,1,0:T(8,128)(2,1)S(1)}, bf16[46,16,128]{2,1,0:T(8,128)(2,1)S(1)}, u32[]{:S(2)}, u32[]{:S(2)}) collective-permute-start(bf16[46,16,128]{2,1,0:T(8,128)(2,1)S(1)} %get-tuple-element.70), channel_id=1, source_target_pairs={{0,96},{8,104},{16,112},{24,120},{32,0},{40,8},{48,16},{56,24},{64... | collective-permute-start | bytes 565256 | tf_op jit(solution)/shard_map/ppermute | solution.py:322
  172.0 10.4 %collective-permute-start.11 = (bf16[45,16,128]{2,1,0:T(8,128)(2,1)S(1)}, bf16[45,16,128]{2,1,0:T(8,128)(2,1)S(1)}, u32[]{:S(2)}, u32[]{:S(2)}) collective-permute-start(bf16[45,16,128]{2,1,0:T(8,128)(2,1)S(1)} %get-tuple-element.64), channel_id=1, source_target_pairs={{0,32},{8,40},{16,48},{24,56},{32,64},{40,72},{48,80},{56,88},{64,... | collective-permute-start | bytes 552968 | tf_op jit(solution)/shard_map/ppermute | solution.py:322
  172.4 13.2 %collective-permute-start.12 = (bf16[45,16,128]{2,1,0:T(8,128)(2,1)S(1)}, bf16[45,16,128]{2,1,0:T(8,128)(2,1)S(1)}, u32[]{:S(2)}, u32[]{:S(2)}) collective-permute-start(bf16[45,16,128]{2,1,0:T(8,128)(2,1)S(1)} %get-tuple-element.65), channel_id=1, source_target_pairs={{0,64},{8,72},{16,80},{24,88},{32,96},{40,104},{48,112},{56,120},{... | collective-permute-start | bytes 552968 | tf_op jit(solution)/shard_map/ppermute | solution.py:322
  173.2 33.9 %copy-start.5 = (bf16[4,46,16,128]{3,2,1,0:T(8,128)(2,1)S(1)}, bf16[4,46,16,128]{3,2,1,0:T(8,128)(2,1)}, u32[]{:S(2)}) copy-start(bf16[4,46,16,128]{3,2,1,0:T(8,128)(2,1)} %copy-done.4) | copy-start | bytes 2260996
  173.2 12.4 %collective-permute-start.13 = (bf16[45,16,128]{2,1,0:T(8,128)(2,1)S(1)}, bf16[45,16,128]{2,1,0:T(8,128)(2,1)S(1)}, u32[]{:S(2)}, u32[]{:S(2)}) collective-permute-start(bf16[45,16,128]{2,1,0:T(8,128)(2,1)S(1)} %get-tuple-element.66), channel_id=1, source_target_pairs={{0,96},{8,104},{16,112},{24,120},{32,0},{40,8},{48,16},{56,24},{64... | collective-permute-start | bytes 552968 | tf_op jit(solution)/shard_map/ppermute | solution.py:322
  177.9 8.0 %collective-permute-start.22 = (bf16[46,16,128]{2,1,0:T(8,128)(2,1)S(1)}, bf16[46,16,128]{2,1,0:T(8,128)(2,1)S(1)}, u32[]{:S(2)}, u32[]{:S(2)}) collective-permute-start(bf16[46,16,128]{2,1,0:T(8,128)(2,1)S(1)} %add_convert_fusion.1), channel_id=1, source_target_pairs={{0,16},{8,24},{16,0},{24,8},{32,48},{40,56},{48,32},{56,40},{64,80... | collective-permute-start | bytes 565256 | tf_op jit(solution)/shard_map/ppermute | solution.py:325
  185.8 5.4 %collective-permute-start.14 = (bf16[45,16,128]{2,1,0:T(8,128)(2,1)S(1)}, bf16[45,16,128]{2,1,0:T(8,128)(2,1)S(1)}, u32[]{:S(2)}, u32[]{:S(2)}) collective-permute-start(bf16[45,16,128]{2,1,0:T(8,128)(2,1)S(1)} %add_convert_fusion.5), channel_id=1, source_target_pairs={{0,16},{8,24},{16,0},{24,8},{32,48},{40,56},{48,32},{56,40},{64,80... | collective-permute-start | bytes 552968 | tf_op jit(solution)/shard_map/ppermute | solution.py:325
  185.9 9.1 %collective-permute-start.25 = (bf16[46,16,128]{2,1,0:T(8,128)(2,1)S(1)}, bf16[46,16,128]{2,1,0:T(8,128)(2,1)S(1)}, u32[]{:S(2)}, u32[]{:S(2)}) collective-permute-start(bf16[46,16,128]{2,1,0:T(8,128)(2,1)S(1)} %add_convert_fusion), channel_id=1, source_target_pairs={{0,32},{8,40},{16,48},{24,56},{32,64},{40,72},{48,80},{56,88},{64,... | collective-permute-start | bytes 565256 | tf_op jit(solution)/shard_map/ppermute | solution.py:328
  186.4 11.3 %collective-permute-start.24 = (bf16[46,16,128]{2,1,0:T(8,128)(2,1)S(1)}, bf16[46,16,128]{2,1,0:T(8,128)(2,1)S(1)}, u32[]{:S(2)}, u32[]{:S(2)}) collective-permute-start(bf16[46,16,128]{2,1,0:T(8,128)(2,1)S(1)} %add_convert_fusion), channel_id=1, source_target_pairs={{0,64},{8,72},{16,80},{24,88},{32,96},{40,104},{48,112},{56,120},{... | collective-permute-start | bytes 565256 | tf_op jit(solution)/shard_map/ppermute | solution.py:328
  189.3 8.4 %collective-permute-start.23 = (bf16[46,16,128]{2,1,0:T(8,128)(2,1)S(1)}, bf16[46,16,128]{2,1,0:T(8,128)(2,1)S(1)}, u32[]{:S(2)}, u32[]{:S(2)}) collective-permute-start(bf16[46,16,128]{2,1,0:T(8,128)(2,1)S(1)} %add_convert_fusion), channel_id=1, source_target_pairs={{0,96},{8,104},{16,112},{24,120},{32,0},{40,8},{48,16},{56,24},{64... | collective-permute-start | bytes 565256 | tf_op jit(solution)/shard_map/ppermute | solution.py:328
  191.2 11.3 %collective-permute-start.17 = (bf16[45,16,128]{2,1,0:T(8,128)(2,1)S(1)}, bf16[45,16,128]{2,1,0:T(8,128)(2,1)S(1)}, u32[]{:S(2)}, u32[]{:S(2)}) collective-permute-start(bf16[45,16,128]{2,1,0:T(8,128)(2,1)S(1)} %add_convert_fusion.4), channel_id=1, source_target_pairs={{0,32},{8,40},{16,48},{24,56},{32,64},{40,72},{48,80},{56,88},{64,... | collective-permute-start | bytes 552968 | tf_op jit(solution)/shard_map/ppermute | solution.py:328
  191.3 14.3 %collective-permute-start.16 = (bf16[45,16,128]{2,1,0:T(8,128)(2,1)S(1)}, bf16[45,16,128]{2,1,0:T(8,128)(2,1)S(1)}, u32[]{:S(2)}, u32[]{:S(2)}) collective-permute-start(bf16[45,16,128]{2,1,0:T(8,128)(2,1)S(1)} %add_convert_fusion.4), channel_id=1, source_target_pairs={{0,64},{8,72},{16,80},{24,88},{32,96},{40,104},{48,112},{56,120},{... | collective-permute-start | bytes 552968 | tf_op jit(solution)/shard_map/ppermute | solution.py:328
  195.0 10.6 %collective-permute-start.15 = (bf16[45,16,128]{2,1,0:T(8,128)(2,1)S(1)}, bf16[45,16,128]{2,1,0:T(8,128)(2,1)S(1)}, u32[]{:S(2)}, u32[]{:S(2)}) collective-permute-start(bf16[45,16,128]{2,1,0:T(8,128)(2,1)S(1)} %add_convert_fusion.4), channel_id=1, source_target_pairs={{0,96},{8,104},{16,112},{24,120},{32,0},{40,8},{48,16},{56,24},{64... | collective-permute-start | bytes 552968 | tf_op jit(solution)/shard_map/ppermute | solution.py:328
  197.8 11.4 %collective-permute-start.26 = (bf16[4,46,16,128]{3,2,1,0:T(8,128)(2,1)S(1)}, bf16[4,46,16,128]{3,2,1,0:T(8,128)(2,1)S(1)}, u32[]{:S(2)}, u32[]{:S(2)}) collective-permute-start(bf16[4,46,16,128]{3,2,1,0:T(8,128)(2,1)S(1)} %pad_maximum_fusion.1.mine_ref), channel_id=1, source_target_pairs={{0,8},{8,0},{16,24},{24,16},{32,40},{40,32},{48,56},{56,48},{64,72... | collective-permute-start | bytes 2261000 | tf_op jit(solution)/shard_map/ppermute | solution.py:332
  205.7 5.5 %collective-permute-start.18 = (bf16[4,45,16,128]{3,2,1,0:T(8,128)(2,1)S(1)}, bf16[4,45,16,128]{3,2,1,0:T(8,128)(2,1)S(1)}, u32[]{:S(2)}, u32[]{:S(2)}) collective-permute-start(bf16[4,45,16,128]{3,2,1,0:T(8,128)(2,1)S(1)} %pad_maximum_fusion.2.mine_ref), channel_id=1, source_target_pairs={{0,8},{8,0},{16,24},{24,16},{32,40},{40,32},{48,56},{56,48},{64,72... | collective-permute-start | bytes 2211848 | tf_op jit(solution)/shard_map/ppermute | solution.py:332

commit v6 on v5

--- a/solution.py
+++ b/solution.py
@@ -10,7 +10,7 @@
 
 BF16, F32 = jnp.bfloat16, jnp.float32
 LANES = 128
-VMEM_LIMIT = 20 * 1024 * 1024
+VMEM_LIMIT = 30 * 1024 * 1024
 CHUNKS = (46, 46, 45)
 STEP = 23
 SHORT = 23
@@ -351,11 +351,11 @@
     last, half1, done0 = tie((last, half1, done0))
     half2 = fold(*regrid(2, last))
     done1 = give(collect(along_y(half1)))
-    done2 = give(collect(along_y(half2)))
-    out = None
-    for i, (mine, theirs) in enumerate((done0, done1, done2)):
-        out = place(tiles, mine, theirs, out, starts[i], levels)
-    return out
+    done2 = collect(along_y(half2))
+    out = place(tiles, *done0, None, starts[0], levels)
+    done2, out = tie((done2, out))
+    out = place(tiles, *done1, out, starts[1], levels)
+    return place(tiles, *give(done2), out, starts[2], levels)
 
 
 def solution(mesh):

time: 214 us -> 214 us (level)
  starting transfers between devices: 67.4 us -> 64.6 us
  waiting for transfers between devices: 89.9 us -> 92.2 us
    ppermute x9, starting transfers between devices: 12.9 us -> 9.98 us  [collect(): lax.ppermute(part, 'mem', mem_to(-dy, 0, 0))]
  transfers between devices with their start and end apart: 31 -> 31, of which waited for: 17 -> 15; matrix products, arithmetic and copies ran while one was open for 1% -> 1% of each run, Pallas kernels for 11% -> 11%
where the time goes in v6:
time: 214 us; the launch traced here: 213 us
  waiting for transfers between devices  92.2 us (43%)
  starting transfers between devices  64.6 us (30%)
  Pallas kernels  49.3 us (23%)
  local copies, waits for them, and re-layouts  5.84 us (3%)
    all_to_all x4, waiting for transfers between devices, swap(): return lax.all_to_all(pieces, 'space', 0, 0, tiled=True)  48.5 us
    all_to_all x4, starting transfers between devices, swap(): return lax.all_to_all(pieces, 'space', 0, 0, tiled=True)  23.8 us
    ppermute x9, waiting for transfers between devices, scatter(): lax.ppermute(kept[dy], 'mem', mem_to(dy, 0, 0))  18.1 us
    ppermute x3, waiting for transfers between devices, cross(): return lax.ppermute(part, 'mem', mem_to(0, 1, 0))  13.7 us
    pallas_call x3, Pallas kernels, backward(): pl.pallas_call(backward_kernel, grid_spec=pltpu.PrefetchScalarGridSpec(nu...  13.4 us
    ppermute x9, starting transfers between devices, scatter(): lax.ppermute(kept[dy], 'mem', mem_to(dy, 0, 0))  13 us
    ppermute x3, starting transfers between devices, fold(): return pair_sum(keep, lax.ppermute(give, 'mem', mem_to(0, 0, 1)))  11.3 us
    pallas_call x1, Pallas kernels, mix(): pl.pallas_call(mix_kernel, grid=(columns // width,), in_specs=[pl.BlockSp...  10.3 us
  transfers between devices with their start and end apart: 31, of which 15 were waited for; matrix products, arithmetic and copies ran while one was open for 1% of the time, Pallas kernels for 11%

profile of v6, /device:TPU:1, one launch (start us, length us, event | category | flops | bytes accessed | tf_op | source)
XLA Modules:
  0.0 213.2 jit_solution(11307279330177610895)
XLA Ops:
  0.0 0.9 copy-done.7
  0.9 10.3 %mix.1 = (bf16[8,46,16,128]{3,2,1,0:T(8,128)(2,1)}, bf16[46,16,1024]{2,1,0:T(8,128)(2,1)}, bf16[45,16,1024]{2,1,0:T(8,128)(2,1)}) custom-call(bf16[137,137]{1,0:T(8,128)(2,1)S(1)} %copy-done.7, bf16[1024,1024]{1,0:T(8,128)(2,1)} %constant.69.clone.basis_ref, bf16[137,16,1024]{2,1,0:T(8,128)(2,1)} %bitcast.24, bf16[137,16,1024]{2,1,0:T(8,128)(2,1)} %increment_ref.1), custom_call_target="tpu_custom_call" | custom-call | tf_op jit(solution)/shard_map/mix/pallas_call | solution.py:80
  11.2 8.5 %all-to-all-start = ((bf16[8,46,16,128]{3,2,1,0:T(8,128)(2,1)}), bf16[8,46,16,128]{3,2,1,0:T(8,128)(2,1)}, u32[]{:S(2)}, u32[]{:S(2)}) async-start(bf16[8,46,16,128]{3,2,1,0:T(8,128)(2,1)} %get-tuple-element.44), calls=%async_computation | async-start | bytes 3014656 | tf_op jit(solution)/shard_map/all_to_all | solution.py:280
  20.0 4.0 %forward.2.refs_0_ = bf16[8,92,16,128]{3,2,1,0:T(8,128)(2,1)} custom-call(bf16[1024,1024]{1,0:T(8,128)(2,1)S(1)} %copy-done.2, bf16[46,16,1024]{2,1,0:T(8,128)(2,1)} %get-tuple-element.45.x_ref), custom_call_target="tpu_custom_call" | custom-call | flops 1543503872 | bytes 5111808 | tf_op jit(solution)/shard_map/forward/pallas_call | solution.py:121
  24.0 17.0 %all-to-all-done.x_ref = bf16[8,46,16,128]{3,2,1,0:T(8,128)(2,1)} async-done(((bf16[8,46,16,128]{3,2,1,0:T(8,128)(2,1)}), bf16[8,46,16,128]{3,2,1,0:T(8,128)(2,1)}, u32[]{:S(2)}, u32[]{:S(2)}) %all-to-all-start) | async-done | bytes 1507360 | tf_op jit(solution)/shard_map/all_to_all | solution.py:280
  41.0 3.1 %filter.3 = bf16[8,92,16,128]{3,2,1,0:T(8,128)(2,1)} custom-call(bf16[128,128]{1,0:T(8,128)(2,1)S(1)} %copy.15.basis_ref, bf16[128,128]{1,0:T(8,128)(2,1)S(1)} %convolution_convert_fusion.basis_t_ref, f32[128,128]{1,0:T(8,128)S(1)} %copy-done.6, bf16[8,46,16,128]{3,2,1,0:T(8,128)(2,1)} %all-to-all-done.x_ref, ...), custom_call_target="tpu_custom_call", output_to_operand_aliasing={{}: (4, {})} | custom-call | flops 385875968 | bytes 3014656 | tf_op jit(solution)/shard_map/filter/pallas_call | solution.py:157
  44.1 3.8 %all-to-all-start.1 = ((bf16[8,92,16,128]{3,2,1,0:T(8,128)(2,1)}), bf16[8,92,16,128]{3,2,1,0:T(8,128)(2,1)S(1)}, u32[]{:S(2)}, u32[]{:S(2)}) async-start(bf16[8,92,16,128]{3,2,1,0:T(8,128)(2,1)} %filter.3), calls=%async_computation.1 | async-start | bytes 6029312 | tf_op jit(solution)/shard_map/all_to_all | solution.py:280
  47.9 1.6 copy-done.3
  49.5 3.9 %forward.3.refs_0_ = bf16[8,91,16,128]{3,2,1,0:T(8,128)(2,1)} custom-call(bf16[1024,1024]{1,0:T(8,128)(2,1)S(1)} %copy-done.3, bf16[45,16,1024]{2,1,0:T(8,128)(2,1)} %get-tuple-element.48.x_ref), custom_call_target="tpu_custom_call" | custom-call | flops 1509949440 | bytes 5046272 | tf_op jit(solution)/shard_map/forward/pallas_call | solution.py:121
  53.4 31.1 %all-to-all-done.1.x_ref = bf16[8,92,16,128]{3,2,1,0:T(8,128)(2,1)S(1)} async-done(((bf16[8,92,16,128]{3,2,1,0:T(8,128)(2,1)}), bf16[8,92,16,128]{3,2,1,0:T(8,128)(2,1)S(1)}, u32[]{:S(2)}, u32[]{:S(2)}) %all-to-all-start.1) | async-done | bytes 3014688 | tf_op jit(solution)/shard_map/all_to_all | solution.py:280
  84.5 2.1 filter.4
  86.7 4.5 %all-to-all-start.2 = ((bf16[8,91,16,128]{3,2,1,0:T(8,128)(2,1)}), bf16[8,91,16,128]{3,2,1,0:T(8,128)(2,1)}, u32[]{:S(2)}, u32[]{:S(2)}) async-start(bf16[8,91,16,128]{3,2,1,0:T(8,128)(2,1)} %filter.4), calls=%async_computation.2 | async-start | bytes 5963776 | tf_op jit(solution)/shard_map/all_to_all | solution.py:280
  91.3 1.6 copy-done
  92.9 4.1 %backward.3 = (bf16[4,46,16,128]{3,2,1,0:T(8,128)(2,1)S(1)}, bf16[4,46,16,128]{3,2,1,0:T(8,128)(2,1)S(1)}) custom-call(s32[8]{0:T(128)S(1)} %stack.80.tiles_ref, bf16[1024,1024]{1,0:T(8,128)(2,1)S(1)} %copy-done, bf16[137,16,1024]{2,1,0:T(8,128)(2,1)} %bitcast.25, bf16[8,92,16,128]{3,2,1,0:T(8,128)(2,1)S(1)} %all-to-all-done.1.x_ref), custom_call_target="tpu_custom_call" | custom-call | flops 1543503872 | bytes 6619136 | tf_op jit(solution)/shard_map/backward/pallas_call | solution.py:191
  97.0 2.7 %collective-permute-start = (bf16[4,46,16,128]{3,2,1,0:T(8,128)(2,1)S(1)}, bf16[4,46,16,128]{3,2,1,0:T(8,128)(2,1)S(1)}, u32[]{:S(2)}, u32[]{:S(2)}) collective-permute-start(bf16[4,46,16,128]{3,2,1,0:T(8,128)(2,1)S(1)} %get-tuple-element.52), channel_id=1, source_target_pairs={{0,8},{8,0},{16,24},{24,16},{32,40},{40,32},{48,56},{56,48},{64,72... | collective-permute-start | bytes 2261000 | tf_op jit(solution)/shard_map/ppermute | solution.py:319
  99.7 1.9 collective-permute-done.b_ref
  101.9 1.4 collective-permute-start.1
  103.3 2.6 %collective-permute-start.2 = (bf16[46,16,128]{2,1,0:T(8,128)(2,1)S(1)}, bf16[46,16,128]{2,1,0:T(8,128)(2,1)S(1)}, u32[]{:S(2)}, u32[]{:S(2)}) collective-permute-start(bf16[46,16,128]{2,1,0:T(8,128)(2,1)S(1)} %get-tuple-element.55), channel_id=1, source_target_pairs={{0,64},{8,72},{16,80},{24,88},{32,96},{40,104},{48,112},{56,120},{... | collective-permute-start | bytes 565256 | tf_op jit(solution)/shard_map/ppermute | solution.py:322
  105.9 1.1 collective-permute-start.3
  106.9 2.4 %collective-permute-done.1 = bf16[46,16,128]{2,1,0:T(8,128)(2,1)S(1)} collective-permute-done((bf16[46,16,128]{2,1,0:T(8,128)(2,1)S(1)}, bf16[46,16,128]{2,1,0:T(8,128)(2,1)S(1)}, u32[]{:S(2)}, u32[]{:S(2)}) %collective-permute-start.1) | collective-permute-done | bytes 188448 | tf_op jit(solution)/shard_map/ppermute | solution.py:322
  109.4 5.1 %collective-permute-done.2 = bf16[46,16,128]{2,1,0:T(8,128)(2,1)S(1)} collective-permute-done((bf16[46,16,128]{2,1,0:T(8,128)(2,1)S(1)}, bf16[46,16,128]{2,1,0:T(8,128)(2,1)S(1)}, u32[]{:S(2)}, u32[]{:S(2)}) %collective-permute-start.2) | collective-permute-done | bytes 188448 | tf_op jit(solution)/shard_map/ppermute | solution.py:322
  115.0 11.4 %collective-permute-done.4 = bf16[46,16,128]{2,1,0:T(8,128)(2,1)S(1)} collective-permute-done((bf16[46,16,128]{2,1,0:T(8,128)(2,1)S(1)}, bf16[46,16,128]{2,1,0:T(8,128)(2,1)S(1)}, u32[]{:S(2)}, u32[]{:S(2)}) %collective-permute-start.4) | collective-permute-done | bytes 188448 | tf_op jit(solution)/shard_map/ppermute | solution.py:325
  126.8 3.3 %filter.5 = bf16[8,45,16,128]{3,2,1,0:T(8,128)(2,1)} custom-call(bf16[128,128]{1,0:T(8,128)(2,1)S(1)} %copy.15.basis_ref, bf16[128,128]{1,0:T(8,128)(2,1)S(1)} %convolution_convert_fusion.basis_t_ref, f32[128,128]{1,0:T(8,128)S(1)} %copy-done.6, bf16[8,91,16,128]{3,2,1,0:T(8,128)(2,1)} %all-to-all-done.2.x_ref), custom_call_target="tpu_custom_call" | custom-call | flops 377487360 | bytes 2949120 | tf_op jit(solution)/shard_map/filter/pallas_call | solution.py:157
  130.1 6.9 %all-to-all-start.3 = ((bf16[8,45,16,128]{3,2,1,0:T(8,128)(2,1)}), bf16[8,45,16,128]{3,2,1,0:T(8,128)(2,1)}, u32[]{:S(2)}, u32[]{:S(2)}) async-start(bf16[8,45,16,128]{3,2,1,0:T(8,128)(2,1)} %filter.5), calls=%async_computation.3 | async-start | bytes 2949120 | tf_op jit(solution)/shard_map/all_to_all | solution.py:280
  137.1 2.7 %collective-permute-start.6 = (bf16[46,16,128]{2,1,0:T(8,128)(2,1)S(1)}, bf16[46,16,128]{2,1,0:T(8,128)(2,1)S(1)}, u32[]{:S(2)}, u32[]{:S(2)}) collective-permute-start(bf16[46,16,128]{2,1,0:T(8,128)(2,1)S(1)} %add_convert_fusion.2), channel_id=1, source_target_pairs={{0,96},{8,104},{16,112},{24,120},{32,0},{40,8},{48,16},{56,24},{64... | collective-permute-start | bytes 565256 | tf_op jit(solution)/shard_map/ppermute | solution.py:328
  140.8 4.4 %backward.4 = (bf16[4,46,16,128]{3,2,1,0:T(8,128)(2,1)S(1)}, bf16[4,46,16,128]{3,2,1,0:T(8,128)(2,1)S(1)}) custom-call(s32[8]{0:T(128)S(1)} %stack.80.tiles_ref, bf16[1024,1024]{1,0:T(8,128)(2,1)S(1)} %copy-done.1, bf16[137,16,1024]{2,1,0:T(8,128)(2,1)} %bitcast.26, bf16[8,91,16,128]{3,2,1,0:T(8,128)(2,1)} %all-to-all-done.2.x_ref), custom_call_target="tpu_custom_call" | custom-call | flops 1543503872 | bytes 6619136 | tf_op jit(solution)/shard_map/backward/pallas_call | solution.py:191
  145.2 4.7 %collective-permute-start.5 = (bf16[4,46,16,128]{3,2,1,0:T(8,128)(2,1)S(1)}, bf16[4,46,16,128]{3,2,1,0:T(8,128)(2,1)S(1)}, u32[]{:S(2)}, u32[]{:S(2)}) collective-permute-start(bf16[4,46,16,128]{3,2,1,0:T(8,128)(2,1)S(1)} %get-tuple-element.59), channel_id=1, source_target_pairs={{0,8},{8,0},{16,24},{24,16},{32,40},{40,32},{48,56},{56,48},{64,72... | collective-permute-start | bytes 2261000 | tf_op jit(solution)/shard_map/ppermute | solution.py:319
  150.0 3.3 %collective-permute-start.9 = (bf16[4,46,16,128]{3,2,1,0:T(8,128)(2,1)S(1)}, bf16[4,46,16,128]{3,2,1,0:T(8,128)(2,1)S(1)}, u32[]{:S(2)}, u32[]{:S(2)}) collective-permute-start(bf16[4,46,16,128]{3,2,1,0:T(8,128)(2,1)S(1)} %pad_maximum_fusion.mine_ref), channel_id=1, source_target_pairs={{0,8},{8,0},{16,24},{24,16},{32,40},{40,32},{48,56},{56,48},{64,72... | collective-permute-start | bytes 2261000 | tf_op jit(solution)/shard_map/ppermute | solution.py:332
  156.1 4.9 %backward.5 = (bf16[4,45,16,128]{3,2,1,0:T(8,128)(2,1)S(1)}, bf16[4,45,16,128]{3,2,1,0:T(8,128)(2,1)S(1)}) custom-call(s32[8]{0:T(128)S(1)} %stack.80.tiles_ref, bf16[1024,1024]{1,0:T(8,128)(2,1)S(1)} %copy-done.1, bf16[137,16,1024]{2,1,0:T(8,128)(2,1)} %bitcast.27, bf16[8,45,16,128]{3,2,1,0:T(8,128)(2,1)} %all-to-all-done.3.x_ref), custom_call_target="tpu_custom_call" | custom-call | flops 1509949440 | bytes 6520832 | tf_op jit(solution)/shard_map/backward/pallas_call | solution.py:191
  161.0 3.9 %collective-permute-start.10 = (bf16[4,45,16,128]{3,2,1,0:T(8,128)(2,1)S(1)}, bf16[4,45,16,128]{3,2,1,0:T(8,128)(2,1)S(1)}, u32[]{:S(2)}, u32[]{:S(2)}) collective-permute-start(bf16[4,45,16,128]{3,2,1,0:T(8,128)(2,1)S(1)} %get-tuple-element.67), channel_id=1, source_target_pairs={{0,8},{8,0},{16,24},{24,16},{32,40},{40,32},{48,56},{56,48},{64,72... | collective-permute-start | bytes 2211848 | tf_op jit(solution)/shard_map/ppermute | solution.py:319
  164.9 1.3 collective-permute-start.19
  166.3 2.6 %collective-permute-start.20 = (bf16[46,16,128]{2,1,0:T(8,128)(2,1)S(1)}, bf16[46,16,128]{2,1,0:T(8,128)(2,1)S(1)}, u32[]{:S(2)}, u32[]{:S(2)}) collective-permute-start(bf16[46,16,128]{2,1,0:T(8,128)(2,1)S(1)} %get-tuple-element.80), channel_id=1, source_target_pairs={{0,64},{8,72},{16,80},{24,88},{32,96},{40,104},{48,112},{56,120},{... | collective-permute-start | bytes 565256 | tf_op jit(solution)/shard_map/ppermute | solution.py:322
  168.9 1.1 collective-permute-start.21
  169.9 2.0 pair_sum.5
  173.2 1.7 collective-permute-start.13
  174.9 2.8 %collective-permute-done.20 = bf16[46,16,128]{2,1,0:T(8,128)(2,1)S(1)} collective-permute-done((bf16[46,16,128]{2,1,0:T(8,128)(2,1)S(1)}, bf16[46,16,128]{2,1,0:T(8,128)(2,1)S(1)}, u32[]{:S(2)}, u32[]{:S(2)}) %collective-permute-start.20) | collective-permute-done | bytes 188448 | tf_op jit(solution)/shard_map/ppermute | solution.py:322
  178.0 4.4 %collective-permute-done.11 = bf16[45,16,128]{2,1,0:T(8,128)(2,1)S(1)} collective-permute-done((bf16[45,16,128]{2,1,0:T(8,128)(2,1)S(1)}, bf16[45,16,128]{2,1,0:T(8,128)(2,1)S(1)}, u32[]{:S(2)}, u32[]{:S(2)}) %collective-permute-start.11) | collective-permute-done | bytes 184352 | tf_op jit(solution)/shard_map/ppermute | solution.py:322
  182.4 3.3 %collective-permute-done.12 = bf16[45,16,128]{2,1,0:T(8,128)(2,1)S(1)} collective-permute-done((bf16[45,16,128]{2,1,0:T(8,128)(2,1)S(1)}, bf16[45,16,128]{2,1,0:T(8,128)(2,1)S(1)}, u32[]{:S(2)}, u32[]{:S(2)}) %collective-permute-start.12) | collective-permute-done | bytes 184352 | tf_op jit(solution)/shard_map/ppermute | solution.py:322
  185.9 2.2 %collective-permute-start.23 = (bf16[46,16,128]{2,1,0:T(8,128)(2,1)S(1)}, bf16[46,16,128]{2,1,0:T(8,128)(2,1)S(1)}, u32[]{:S(2)}, u32[]{:S(2)}) collective-permute-start(bf16[46,16,128]{2,1,0:T(8,128)(2,1)S(1)} %add_convert_fusion), channel_id=1, source_target_pairs={{0,96},{8,104},{16,112},{24,120},{32,0},{40,8},{48,16},{56,24},{64... | collective-permute-start | bytes 565256 | tf_op jit(solution)/shard_map/ppermute | solution.py:328
  188.9 2.3 %collective-permute-done.14 = bf16[45,16,128]{2,1,0:T(8,128)(2,1)S(1)} collective-permute-done((bf16[45,16,128]{2,1,0:T(8,128)(2,1)S(1)}, bf16[45,16,128]{2,1,0:T(8,128)(2,1)S(1)}, u32[]{:S(2)}, u32[]{:S(2)}) %collective-permute-start.14) | collective-permute-done | bytes 184352 | tf_op jit(solution)/shard_map/ppermute | solution.py:325
  191.2 2.6 %collective-permute-start.15 = (bf16[45,16,128]{2,1,0:T(8,128)(2,1)S(1)}, bf16[45,16,128]{2,1,0:T(8,128)(2,1)S(1)}, u32[]{:S(2)}, u32[]{:S(2)}) collective-permute-start(bf16[45,16,128]{2,1,0:T(8,128)(2,1)S(1)} %add_convert_fusion.4), channel_id=1, source_target_pairs={{0,96},{8,104},{16,112},{24,120},{32,0},{40,8},{48,16},{56,24},{64... | collective-permute-start | bytes 552968 | tf_op jit(solution)/shard_map/ppermute | solution.py:328
  194.5 2.0 place.3.refs_0_
  196.5 4.0 %collective-permute-done.25 = bf16[46,16,128]{2,1,0:T(8,128)(2,1)S(1)} collective-permute-done((bf16[46,16,128]{2,1,0:T(8,128)(2,1)S(1)}, bf16[46,16,128]{2,1,0:T(8,128)(2,1)S(1)}, u32[]{:S(2)}, u32[]{:S(2)}) %collective-permute-start.25) | collective-permute-done | bytes 188448 | tf_op jit(solution)/shard_map/ppermute | solution.py:328
  200.6 1.8 collective-permute-start.26
  203.2 4.4 %collective-permute-done.17 = bf16[45,16,128]{2,1,0:T(8,128)(2,1)S(1)} collective-permute-done((bf16[45,16,128]{2,1,0:T(8,128)(2,1)S(1)}, bf16[45,16,128]{2,1,0:T(8,128)(2,1)S(1)}, u32[]{:S(2)}, u32[]{:S(2)}) %collective-permute-start.17) | collective-permute-done | bytes 184352 | tf_op jit(solution)/shard_map/ppermute | solution.py:328
  207.7 0.9 collective-permute-start.18
  208.6 2.0 place.4.refs_0_
  210.7 2.5 %place.5 = bf16[137,16,1024]{2,1,0:T(8,128)(2,1)} custom-call(s32[8]{0:T(128)S(1)} %stack.80.tiles_ref, bf16[4,45,16,128]{3,2,1,0:T(8,128)(2,1)S(1)} %pad_maximum_fusion.2.mine_ref, bf16[4,45,16,128]{3,2,1,0:T(8,128)(2,1)S(1)} %collective-permute-done.18.theirs_ref, bf16[137,16,1024]{2,1,0:T(8,128)(2,1)} %place.4.refs_0_), custom_call_target="tpu_custom_call", output_to_operand_aliasing={{}: (3, {})} | custom-call | bytes 2949120 | tf_op jit(solution)/shard_map/place/pallas_call | solution.py:247
  (65 shorter events, 9.8 us)
Async XLA Ops:
  0.0 0.9 copy-start.7
  11.2 8.5 %copy-start.10 = (bf16[128,128]{1,0:T(8,128)(2,1)S(1)}, bf16[128,128]{1,0:T(8,128)(2,1)}, u32[]{:S(2)}) copy-start(bf16[128,128]{1,0:T(8,128)(2,1)} %constant.70.clone) | copy-start | bytes 98308
  11.2 8.5 %copy-start.11 = (s32[128]{0:T(128)S(1)}, s32[128]{0:T(128)}, u32[]{:S(2)}) copy-start(s32[128]{0:T(128)} %param.12) | copy-start | bytes 1540
  11.2 8.8 %copy-start.2 = (bf16[1024,1024]{1,0:T(8,128)(2,1)S(1)}, bf16[1024,1024]{1,0:T(8,128)(2,1)}, u32[]{:S(2)}) copy-start(bf16[1024,1024]{1,0:T(8,128)(2,1)} %constant.69.clone.basis_ref) | copy-start | bytes 6291460
  11.2 29.8 %all-to-all-start = ((bf16[8,46,16,128]{3,2,1,0:T(8,128)(2,1)}), bf16[8,46,16,128]{3,2,1,0:T(8,128)(2,1)}, u32[]{:S(2)}, u32[]{:S(2)}) async-start(bf16[8,46,16,128]{3,2,1,0:T(8,128)(2,1)} %get-tuple-element.44), calls=%async_computation | async-start | bytes 3014656 | tf_op jit(solution)/shard_map/all_to_all | solution.py:280
  20.0 21.0 %copy-start.6 = (f32[128,128]{1,0:T(8,128)S(1)}, f32[128,128]{1,0:T(8,128)}, u32[]{:S(2)}) copy-start(f32[128,128]{1,0:T(8,128)} %weights_ref.5) | copy-start | bytes 196612
  44.1 40.5 %all-to-all-start.1 = ((bf16[8,92,16,128]{3,2,1,0:T(8,128)(2,1)}), bf16[8,92,16,128]{3,2,1,0:T(8,128)(2,1)S(1)}, u32[]{:S(2)}, u32[]{:S(2)}) async-start(bf16[8,92,16,128]{3,2,1,0:T(8,128)(2,1)} %filter.3), calls=%async_computation.1 | async-start | bytes 6029312 | tf_op jit(solution)/shard_map/all_to_all | solution.py:280
  47.9 1.6 copy-start.3
  86.7 40.2 %all-to-all-start.2 = ((bf16[8,91,16,128]{3,2,1,0:T(8,128)(2,1)}), bf16[8,91,16,128]{3,2,1,0:T(8,128)(2,1)}, u32[]{:S(2)}, u32[]{:S(2)}) async-start(bf16[8,91,16,128]{3,2,1,0:T(8,128)(2,1)} %filter.4), calls=%async_computation.2 | async-start | bytes 5963776 | tf_op jit(solution)/shard_map/all_to_all | solution.py:280
  91.3 1.6 copy-start
  97.0 4.6 %collective-permute-start = (bf16[4,46,16,128]{3,2,1,0:T(8,128)(2,1)S(1)}, bf16[4,46,16,128]{3,2,1,0:T(8,128)(2,1)S(1)}, u32[]{:S(2)}, u32[]{:S(2)}) collective-permute-start(bf16[4,46,16,128]{3,2,1,0:T(8,128)(2,1)S(1)} %get-tuple-element.52), channel_id=1, source_target_pairs={{0,8},{8,0},{16,24},{24,16},{32,40},{40,32},{48,56},{56,48},{64,72... | collective-permute-start | bytes 2261000 | tf_op jit(solution)/shard_map/ppermute | solution.py:319
  101.9 7.5 %collective-permute-start.1 = (bf16[46,16,128]{2,1,0:T(8,128)(2,1)S(1)}, bf16[46,16,128]{2,1,0:T(8,128)(2,1)S(1)}, u32[]{:S(2)}, u32[]{:S(2)}) collective-permute-start(bf16[46,16,128]{2,1,0:T(8,128)(2,1)S(1)} %get-tuple-element.54), channel_id=1, source_target_pairs={{0,32},{8,40},{16,48},{24,56},{32,64},{40,72},{48,80},{56,88},{64,... | collective-permute-start | bytes 565256 | tf_op jit(solution)/shard_map/ppermute | solution.py:322
  103.3 11.2 %collective-permute-start.2 = (bf16[46,16,128]{2,1,0:T(8,128)(2,1)S(1)}, bf16[46,16,128]{2,1,0:T(8,128)(2,1)S(1)}, u32[]{:S(2)}, u32[]{:S(2)}) collective-permute-start(bf16[46,16,128]{2,1,0:T(8,128)(2,1)S(1)} %get-tuple-element.55), channel_id=1, source_target_pairs={{0,64},{8,72},{16,80},{24,88},{32,96},{40,104},{48,112},{56,120},{... | collective-permute-start | bytes 565256 | tf_op jit(solution)/shard_map/ppermute | solution.py:322
  105.9 8.6 %collective-permute-start.3 = (bf16[46,16,128]{2,1,0:T(8,128)(2,1)S(1)}, bf16[46,16,128]{2,1,0:T(8,128)(2,1)S(1)}, u32[]{:S(2)}, u32[]{:S(2)}) collective-permute-start(bf16[46,16,128]{2,1,0:T(8,128)(2,1)S(1)} %get-tuple-element.56), channel_id=1, source_target_pairs={{0,96},{8,104},{16,112},{24,120},{32,0},{40,8},{48,16},{56,24},{64... | collective-permute-start | bytes 565256 | tf_op jit(solution)/shard_map/ppermute | solution.py:322
  114.6 11.8 %collective-permute-start.4 = (bf16[46,16,128]{2,1,0:T(8,128)(2,1)S(1)}, bf16[46,16,128]{2,1,0:T(8,128)(2,1)S(1)}, u32[]{:S(2)}, u32[]{:S(2)}) collective-permute-start(bf16[46,16,128]{2,1,0:T(8,128)(2,1)S(1)} %add_convert_fusion.3), channel_id=1, source_target_pairs={{0,16},{8,24},{16,0},{24,8},{32,48},{40,56},{48,32},{56,40},{64,80... | collective-permute-start | bytes 565256 | tf_op jit(solution)/shard_map/ppermute | solution.py:325
  126.5 14.4 %copy-start.1 = (bf16[1024,1024]{1,0:T(8,128)(2,1)S(1)}, bf16[1024,1024]{1,0:T(8,128)(2,1)}, u32[]{:S(2)}) copy-start(bf16[1024,1024]{1,0:T(8,128)(2,1)} %constant.68.clone.basis_ref) | copy-start | bytes 6291460
  130.1 25.9 %all-to-all-start.3 = ((bf16[8,45,16,128]{3,2,1,0:T(8,128)(2,1)}), bf16[8,45,16,128]{3,2,1,0:T(8,128)(2,1)}, u32[]{:S(2)}, u32[]{:S(2)}) async-start(bf16[8,45,16,128]{3,2,1,0:T(8,128)(2,1)} %filter.5), calls=%async_computation.3 | async-start | bytes 2949120 | tf_op jit(solution)/shard_map/all_to_all | solution.py:280
  137.1 12.9 %collective-permute-start.6 = (bf16[46,16,128]{2,1,0:T(8,128)(2,1)S(1)}, bf16[46,16,128]{2,1,0:T(8,128)(2,1)S(1)}, u32[]{:S(2)}, u32[]{:S(2)}) collective-permute-start(bf16[46,16,128]{2,1,0:T(8,128)(2,1)S(1)} %add_convert_fusion.2), channel_id=1, source_target_pairs={{0,96},{8,104},{16,112},{24,120},{32,0},{40,8},{48,16},{56,24},{64... | collective-permute-start | bytes 565256 | tf_op jit(solution)/shard_map/ppermute | solution.py:328
  139.8 10.1 %collective-permute-start.7 = (bf16[46,16,128]{2,1,0:T(8,128)(2,1)S(1)}, bf16[46,16,128]{2,1,0:T(8,128)(2,1)S(1)}, u32[]{:S(2)}, u32[]{:S(2)}) collective-permute-start(bf16[46,16,128]{2,1,0:T(8,128)(2,1)S(1)} %add_convert_fusion.2), channel_id=1, source_target_pairs={{0,64},{8,72},{16,80},{24,88},{32,96},{40,104},{48,112},{56,120},{... | collective-permute-start | bytes 565256 | tf_op jit(solution)/shard_map/ppermute | solution.py:328
  140.1 9.8 %collective-permute-start.8 = (bf16[46,16,128]{2,1,0:T(8,128)(2,1)S(1)}, bf16[46,16,128]{2,1,0:T(8,128)(2,1)S(1)}, u32[]{:S(2)}, u32[]{:S(2)}) collective-permute-start(bf16[46,16,128]{2,1,0:T(8,128)(2,1)S(1)} %add_convert_fusion.2), channel_id=1, source_target_pairs={{0,32},{8,40},{16,48},{24,56},{32,64},{40,72},{48,80},{56,88},{64,... | collective-permute-start | bytes 565256 | tf_op jit(solution)/shard_map/ppermute | solution.py:328
  145.2 8.1 %collective-permute-start.5 = (bf16[4,46,16,128]{3,2,1,0:T(8,128)(2,1)S(1)}, bf16[4,46,16,128]{3,2,1,0:T(8,128)(2,1)S(1)}, u32[]{:S(2)}, u32[]{:S(2)}) collective-permute-start(bf16[4,46,16,128]{3,2,1,0:T(8,128)(2,1)S(1)} %get-tuple-element.59), channel_id=1, source_target_pairs={{0,8},{8,0},{16,24},{24,16},{32,40},{40,32},{48,56},{56,48},{64,72... | collective-permute-start | bytes 2261000 | tf_op jit(solution)/shard_map/ppermute | solution.py:319
  150.0 5.1 %collective-permute-start.9 = (bf16[4,46,16,128]{3,2,1,0:T(8,128)(2,1)S(1)}, bf16[4,46,16,128]{3,2,1,0:T(8,128)(2,1)S(1)}, u32[]{:S(2)}, u32[]{:S(2)}) collective-permute-start(bf16[4,46,16,128]{3,2,1,0:T(8,128)(2,1)S(1)} %pad_maximum_fusion.mine_ref), channel_id=1, source_target_pairs={{0,8},{8,0},{16,24},{24,16},{32,40},{40,32},{48,56},{56,48},{64,72... | collective-permute-start | bytes 2261000 | tf_op jit(solution)/shard_map/ppermute | solution.py:332
  153.7 0.7 copy-start.8
  155.2 0.9 copy-start.4
  156.1 8.9 %copy-start.9 = (bf16[46,16,128]{2,1,0:T(8,128)(2,1)S(1)}, bf16[46,16,128]{2,1,0:T(8,128)(2,1)}, u32[]{:S(2)}) copy-start(bf16[46,16,128]{2,1,0:T(8,128)(2,1)} %copy-done.8) | copy-start | bytes 565252
  161.0 33.5 %copy-start.5 = (bf16[4,46,16,128]{3,2,1,0:T(8,128)(2,1)S(1)}, bf16[4,46,16,128]{3,2,1,0:T(8,128)(2,1)}, u32[]{:S(2)}) copy-start(bf16[4,46,16,128]{3,2,1,0:T(8,128)(2,1)} %copy-done.4) | copy-start | bytes 2260996
  161.0 8.9 %collective-permute-start.10 = (bf16[4,45,16,128]{3,2,1,0:T(8,128)(2,1)S(1)}, bf16[4,45,16,128]{3,2,1,0:T(8,128)(2,1)S(1)}, u32[]{:S(2)}, u32[]{:S(2)}) collective-permute-start(bf16[4,45,16,128]{3,2,1,0:T(8,128)(2,1)S(1)} %get-tuple-element.67), channel_id=1, source_target_pairs={{0,8},{8,0},{16,24},{24,16},{32,40},{40,32},{48,56},{56,48},{64,72... | collective-permute-start | bytes 2211848 | tf_op jit(solution)/shard_map/ppermute | solution.py:319
  164.9 8.3 %collective-permute-start.19 = (bf16[46,16,128]{2,1,0:T(8,128)(2,1)S(1)}, bf16[46,16,128]{2,1,0:T(8,128)(2,1)S(1)}, u32[]{:S(2)}, u32[]{:S(2)}) collective-permute-start(bf16[46,16,128]{2,1,0:T(8,128)(2,1)S(1)} %copy-done.9), channel_id=1, source_target_pairs={{0,32},{8,40},{16,48},{24,56},{32,64},{40,72},{48,80},{56,88},{64,... | collective-permute-start | bytes 565256 | tf_op jit(solution)/shard_map/ppermute | solution.py:322
  166.3 11.5 %collective-permute-start.20 = (bf16[46,16,128]{2,1,0:T(8,128)(2,1)S(1)}, bf16[46,16,128]{2,1,0:T(8,128)(2,1)S(1)}, u32[]{:S(2)}, u32[]{:S(2)}) collective-permute-start(bf16[46,16,128]{2,1,0:T(8,128)(2,1)S(1)} %get-tuple-element.80), channel_id=1, source_target_pairs={{0,64},{8,72},{16,80},{24,88},{32,96},{40,104},{48,112},{56,120},{... | collective-permute-start | bytes 565256 | tf_op jit(solution)/shard_map/ppermute | solution.py:322
  168.9 8.9 %collective-permute-start.21 = (bf16[46,16,128]{2,1,0:T(8,128)(2,1)S(1)}, bf16[46,16,128]{2,1,0:T(8,128)(2,1)S(1)}, u32[]{:S(2)}, u32[]{:S(2)}) collective-permute-start(bf16[46,16,128]{2,1,0:T(8,128)(2,1)S(1)} %get-tuple-element.81), channel_id=1, source_target_pairs={{0,96},{8,104},{16,112},{24,120},{32,0},{40,8},{48,16},{56,24},{64... | collective-permute-start | bytes 565256 | tf_op jit(solution)/shard_map/ppermute | solution.py:322
  172.0 10.4 %collective-permute-start.11 = (bf16[45,16,128]{2,1,0:T(8,128)(2,1)S(1)}, bf16[45,16,128]{2,1,0:T(8,128)(2,1)S(1)}, u32[]{:S(2)}, u32[]{:S(2)}) collective-permute-start(bf16[45,16,128]{2,1,0:T(8,128)(2,1)S(1)} %get-tuple-element.69), channel_id=1, source_target_pairs={{0,32},{8,40},{16,48},{24,56},{32,64},{40,72},{48,80},{56,88},{64,... | collective-permute-start | bytes 552968 | tf_op jit(solution)/shard_map/ppermute | solution.py:322
  172.4 13.2 %collective-permute-start.12 = (bf16[45,16,128]{2,1,0:T(8,128)(2,1)S(1)}, bf16[45,16,128]{2,1,0:T(8,128)(2,1)S(1)}, u32[]{:S(2)}, u32[]{:S(2)}) collective-permute-start(bf16[45,16,128]{2,1,0:T(8,128)(2,1)S(1)} %get-tuple-element.70), channel_id=1, source_target_pairs={{0,64},{8,72},{16,80},{24,88},{32,96},{40,104},{48,112},{56,120},{... | collective-permute-start | bytes 552968 | tf_op jit(solution)/shard_map/ppermute | solution.py:322
  173.2 12.4 %collective-permute-start.13 = (bf16[45,16,128]{2,1,0:T(8,128)(2,1)S(1)}, bf16[45,16,128]{2,1,0:T(8,128)(2,1)S(1)}, u32[]{:S(2)}, u32[]{:S(2)}) collective-permute-start(bf16[45,16,128]{2,1,0:T(8,128)(2,1)S(1)} %get-tuple-element.71), channel_id=1, source_target_pairs={{0,96},{8,104},{16,112},{24,120},{32,0},{40,8},{48,16},{56,24},{64... | collective-permute-start | bytes 552968 | tf_op jit(solution)/shard_map/ppermute | solution.py:322
  177.9 8.0 %collective-permute-start.22 = (bf16[46,16,128]{2,1,0:T(8,128)(2,1)S(1)}, bf16[46,16,128]{2,1,0:T(8,128)(2,1)S(1)}, u32[]{:S(2)}, u32[]{:S(2)}) collective-permute-start(bf16[46,16,128]{2,1,0:T(8,128)(2,1)S(1)} %add_convert_fusion.1), channel_id=1, source_target_pairs={{0,16},{8,24},{16,0},{24,8},{32,48},{40,56},{48,32},{56,40},{64,80... | collective-permute-start | bytes 565256 | tf_op jit(solution)/shard_map/ppermute | solution.py:325
  185.8 5.4 %collective-permute-start.14 = (bf16[45,16,128]{2,1,0:T(8,128)(2,1)S(1)}, bf16[45,16,128]{2,1,0:T(8,128)(2,1)S(1)}, u32[]{:S(2)}, u32[]{:S(2)}) collective-permute-start(bf16[45,16,128]{2,1,0:T(8,128)(2,1)S(1)} %add_convert_fusion.5), channel_id=1, source_target_pairs={{0,16},{8,24},{16,0},{24,8},{32,48},{40,56},{48,32},{56,40},{64,80... | collective-permute-start | bytes 552968 | tf_op jit(solution)/shard_map/ppermute | solution.py:325
  185.9 7.9 %collective-permute-start.23 = (bf16[46,16,128]{2,1,0:T(8,128)(2,1)S(1)}, bf16[46,16,128]{2,1,0:T(8,128)(2,1)S(1)}, u32[]{:S(2)}, u32[]{:S(2)}) collective-permute-start(bf16[46,16,128]{2,1,0:T(8,128)(2,1)S(1)} %add_convert_fusion), channel_id=1, source_target_pairs={{0,96},{8,104},{16,112},{24,120},{32,0},{40,8},{48,16},{56,24},{64... | collective-permute-start | bytes 565256 | tf_op jit(solution)/shard_map/ppermute | solution.py:328
  188.1 8.4 %collective-permute-start.24 = (bf16[46,16,128]{2,1,0:T(8,128)(2,1)S(1)}, bf16[46,16,128]{2,1,0:T(8,128)(2,1)S(1)}, u32[]{:S(2)}, u32[]{:S(2)}) collective-permute-start(bf16[46,16,128]{2,1,0:T(8,128)(2,1)S(1)} %add_convert_fusion), channel_id=1, source_target_pairs={{0,64},{8,72},{16,80},{24,88},{32,96},{40,104},{48,112},{56,120},{... | collective-permute-start | bytes 565256 | tf_op jit(solution)/shard_map/ppermute | solution.py:328
  188.2 12.3 %collective-permute-start.25 = (bf16[46,16,128]{2,1,0:T(8,128)(2,1)S(1)}, bf16[46,16,128]{2,1,0:T(8,128)(2,1)S(1)}, u32[]{:S(2)}, u32[]{:S(2)}) collective-permute-start(bf16[46,16,128]{2,1,0:T(8,128)(2,1)S(1)} %add_convert_fusion), channel_id=1, source_target_pairs={{0,32},{8,40},{16,48},{24,56},{32,64},{40,72},{48,80},{56,88},{64,... | collective-permute-start | bytes 565256 | tf_op jit(solution)/shard_map/ppermute | solution.py:328
  191.2 11.1 %collective-permute-start.15 = (bf16[45,16,128]{2,1,0:T(8,128)(2,1)S(1)}, bf16[45,16,128]{2,1,0:T(8,128)(2,1)S(1)}, u32[]{:S(2)}, u32[]{:S(2)}) collective-permute-start(bf16[45,16,128]{2,1,0:T(8,128)(2,1)S(1)} %add_convert_fusion.4), channel_id=1, source_target_pairs={{0,96},{8,104},{16,112},{24,120},{32,0},{40,8},{48,16},{56,24},{64... | collective-permute-start | bytes 552968 | tf_op jit(solution)/shard_map/ppermute | solution.py:328
  193.8 9.4 %collective-permute-start.16 = (bf16[45,16,128]{2,1,0:T(8,128)(2,1)S(1)}, bf16[45,16,128]{2,1,0:T(8,128)(2,1)S(1)}, u32[]{:S(2)}, u32[]{:S(2)}) collective-permute-start(bf16[45,16,128]{2,1,0:T(8,128)(2,1)S(1)} %add_convert_fusion.4), channel_id=1, source_target_pairs={{0,64},{8,72},{16,80},{24,88},{32,96},{40,104},{48,112},{56,120},{... | collective-permute-start | bytes 552968 | tf_op jit(solution)/shard_map/ppermute | solution.py:328
  193.8 13.8 %collective-permute-start.17 = (bf16[45,16,128]{2,1,0:T(8,128)(2,1)S(1)}, bf16[45,16,128]{2,1,0:T(8,128)(2,1)S(1)}, u32[]{:S(2)}, u32[]{:S(2)}) collective-permute-start(bf16[45,16,128]{2,1,0:T(8,128)(2,1)S(1)} %add_convert_fusion.4), channel_id=1, source_target_pairs={{0,32},{8,40},{16,48},{24,56},{32,64},{40,72},{48,80},{56,88},{64,... | collective-permute-start | bytes 552968 | tf_op jit(solution)/shard_map/ppermute | solution.py:328
  200.6 8.1 %collective-permute-start.26 = (bf16[4,46,16,128]{3,2,1,0:T(8,128)(2,1)S(1)}, bf16[4,46,16,128]{3,2,1,0:T(8,128)(2,1)S(1)}, u32[]{:S(2)}, u32[]{:S(2)}) collective-permute-start(bf16[4,46,16,128]{3,2,1,0:T(8,128)(2,1)S(1)} %pad_maximum_fusion.1.mine_ref), channel_id=1, source_target_pairs={{0,8},{8,0},{16,24},{24,16},{32,40},{40,32},{48,56},{56,48},{64,72... | collective-permute-start | bytes 2261000 | tf_op jit(solution)/shard_map/ppermute | solution.py:332
  207.7 2.9 %collective-permute-start.18 = (bf16[4,45,16,128]{3,2,1,0:T(8,128)(2,1)S(1)}, bf16[4,45,16,128]{3,2,1,0:T(8,128)(2,1)S(1)}, u32[]{:S(2)}, u32[]{:S(2)}) collective-permute-start(bf16[4,45,16,128]{3,2,1,0:T(8,128)(2,1)S(1)} %pad_maximum_fusion.2.mine_ref), channel_id=1, source_target_pairs={{0,8},{8,0},{16,24},{24,16},{32,40},{40,32},{48,56},{56,48},{64,72... | collective-permute-start | bytes 2211848 | tf_op jit(solution)/shard_map/ppermute | solution.py:332

commit v7 on v6

--- a/solution.py
+++ b/solution.py
@@ -205,7 +205,7 @@
         compiler_params=params(),
         cost_estimate=cost(2 * total * columns, 3 * total + basis.size),
         name="backward",
-    )(tiles, basis, pltpu.with_memory_space_constraint(member, pltpu.HBM), x)
+    )(tiles, *[pltpu.with_memory_space_constraint(a, pltpu.HBM) for a in (basis, member)], x)
 
 
 def pair_kernel(a_ref, b_ref, *out_refs):

time: 214 us -> 214 us (level)
  local copies, waits for them, and re-layouts: 5.84 us -> 3.35 us
    unnamed x24 -> x16, local copies, waits for them, and re-layouts: 5.65 us -> 3.16 us
where the time goes in v7:
time: 214 us; the launch traced here: 213 us
  waiting for transfers between devices  93.1 us (44%)
  starting transfers between devices  64.7 us (30%)
  Pallas kernels  51 us (24%)
  local copies, waits for them, and re-layouts  3.35 us (2%)
    all_to_all x4, waiting for transfers between devices, swap(): return lax.all_to_all(pieces, 'space', 0, 0, tiled=True)  48.5 us
    all_to_all x4, starting transfers between devices, swap(): return lax.all_to_all(pieces, 'space', 0, 0, tiled=True)  23.8 us
    ppermute x9, waiting for transfers between devices, scatter(): lax.ppermute(kept[dy], 'mem', mem_to(dy, 0, 0))  18.1 us
    pallas_call x3, Pallas kernels, backward(): pl.pallas_call(backward_kernel, grid_spec=pltpu.PrefetchScalarGridSpec(nu...  15.3 us
    ppermute x3, waiting for transfers between devices, cross(): return lax.ppermute(part, 'mem', mem_to(0, 1, 0))  14.6 us
    ppermute x9, starting transfers between devices, scatter(): lax.ppermute(kept[dy], 'mem', mem_to(dy, 0, 0))  13 us
    ppermute x3, starting transfers between devices, fold(): return pair_sum(keep, lax.ppermute(give, 'mem', mem_to(0, 0, 1)))  12.1 us
    pallas_call x1, Pallas kernels, mix(): pl.pallas_call(mix_kernel, grid=(columns // width,), in_specs=[pl.BlockSp...  10.3 us
  transfers between devices with their start and end apart: 31, of which 15 were waited for; matrix products, arithmetic and copies ran while one was open for 1% of the time, Pallas kernels for 11%

profile of v7, /device:TPU:1, one launch (start us, length us, event | category | flops | bytes accessed | tf_op | source)
XLA Modules:
  0.0 213.4 jit_solution(5667839037812624034)
XLA Ops:
  0.0 0.9 copy-done.3
  0.9 10.3 %mix.1 = (bf16[8,46,16,128]{3,2,1,0:T(8,128)(2,1)}, bf16[46,16,1024]{2,1,0:T(8,128)(2,1)}, bf16[45,16,1024]{2,1,0:T(8,128)(2,1)}) custom-call(bf16[137,137]{1,0:T(8,128)(2,1)S(1)} %copy-done.3, bf16[1024,1024]{1,0:T(8,128)(2,1)} %constant.69.clone.basis_ref, bf16[137,16,1024]{2,1,0:T(8,128)(2,1)} %bitcast.24, bf16[137,16,1024]{2,1,0:T(8,128)(2,1)} %increment_ref.1), custom_call_target="tpu_custom_call" | custom-call | tf_op jit(solution)/shard_map/mix/pallas_call | solution.py:80
  11.2 8.5 %all-to-all-start = ((bf16[8,46,16,128]{3,2,1,0:T(8,128)(2,1)}), bf16[8,46,16,128]{3,2,1,0:T(8,128)(2,1)}, u32[]{:S(2)}, u32[]{:S(2)}) async-start(bf16[8,46,16,128]{3,2,1,0:T(8,128)(2,1)} %get-tuple-element.44), calls=%async_computation | async-start | bytes 3014656 | tf_op jit(solution)/shard_map/all_to_all | solution.py:280
  20.0 4.0 %forward.2.refs_0_ = bf16[8,92,16,128]{3,2,1,0:T(8,128)(2,1)} custom-call(bf16[1024,1024]{1,0:T(8,128)(2,1)S(1)} %copy-done, bf16[46,16,1024]{2,1,0:T(8,128)(2,1)} %get-tuple-element.45.x_ref), custom_call_target="tpu_custom_call" | custom-call | flops 1543503872 | bytes 5111808 | tf_op jit(solution)/shard_map/forward/pallas_call | solution.py:121
  24.0 17.0 %all-to-all-done.x_ref = bf16[8,46,16,128]{3,2,1,0:T(8,128)(2,1)} async-done(((bf16[8,46,16,128]{3,2,1,0:T(8,128)(2,1)}), bf16[8,46,16,128]{3,2,1,0:T(8,128)(2,1)}, u32[]{:S(2)}, u32[]{:S(2)}) %all-to-all-start) | async-done | bytes 1507360 | tf_op jit(solution)/shard_map/all_to_all | solution.py:280
  41.0 3.1 %filter.3 = bf16[8,92,16,128]{3,2,1,0:T(8,128)(2,1)} custom-call(bf16[128,128]{1,0:T(8,128)(2,1)S(1)} %copy.15.basis_ref, bf16[128,128]{1,0:T(8,128)(2,1)S(1)} %convolution_convert_fusion.basis_t_ref, f32[128,128]{1,0:T(8,128)S(1)} %copy-done.2, bf16[8,46,16,128]{3,2,1,0:T(8,128)(2,1)} %all-to-all-done.x_ref, ...), custom_call_target="tpu_custom_call", output_to_operand_aliasing={{}: (4, {})} | custom-call | flops 385875968 | bytes 3014656 | tf_op jit(solution)/shard_map/filter/pallas_call | solution.py:157
  44.1 3.8 %all-to-all-start.1 = ((bf16[8,92,16,128]{3,2,1,0:T(8,128)(2,1)}), bf16[8,92,16,128]{3,2,1,0:T(8,128)(2,1)S(1)}, u32[]{:S(2)}, u32[]{:S(2)}) async-start(bf16[8,92,16,128]{3,2,1,0:T(8,128)(2,1)} %filter.3), calls=%async_computation.1 | async-start | bytes 6029312 | tf_op jit(solution)/shard_map/all_to_all | solution.py:280
  47.9 1.6 copy-done.1
  49.5 3.9 %forward.3.refs_0_ = bf16[8,91,16,128]{3,2,1,0:T(8,128)(2,1)} custom-call(bf16[1024,1024]{1,0:T(8,128)(2,1)S(1)} %copy-done.1, bf16[45,16,1024]{2,1,0:T(8,128)(2,1)} %get-tuple-element.48.x_ref), custom_call_target="tpu_custom_call" | custom-call | flops 1509949440 | bytes 5046272 | tf_op jit(solution)/shard_map/forward/pallas_call | solution.py:121
  53.4 31.1 %all-to-all-done.1.x_ref = bf16[8,92,16,128]{3,2,1,0:T(8,128)(2,1)S(1)} async-done(((bf16[8,92,16,128]{3,2,1,0:T(8,128)(2,1)}), bf16[8,92,16,128]{3,2,1,0:T(8,128)(2,1)S(1)}, u32[]{:S(2)}, u32[]{:S(2)}) %all-to-all-start.1) | async-done | bytes 3014688 | tf_op jit(solution)/shard_map/all_to_all | solution.py:280
  84.5 2.1 %filter.4 = bf16[8,91,16,128]{3,2,1,0:T(8,128)(2,1)} custom-call(bf16[128,128]{1,0:T(8,128)(2,1)S(1)} %copy.15.basis_ref, bf16[128,128]{1,0:T(8,128)(2,1)S(1)} %convolution_convert_fusion.basis_t_ref, f32[128,128]{1,0:T(8,128)S(1)} %copy-done.2, bf16[8,92,16,128]{3,2,1,0:T(8,128)(2,1)S(1)} %all-to-all-done.1.x_ref, ...), custom_call_target="tpu_custom_call", output_to_operand_aliasing={{}: (4, {})} | custom-call | flops 385875968 | bytes 3014656 | tf_op jit(solution)/shard_map/filter/pallas_call | solution.py:157
  86.7 4.5 %all-to-all-start.2 = ((bf16[8,91,16,128]{3,2,1,0:T(8,128)(2,1)}), bf16[8,91,16,128]{3,2,1,0:T(8,128)(2,1)}, u32[]{:S(2)}, u32[]{:S(2)}) async-start(bf16[8,91,16,128]{3,2,1,0:T(8,128)(2,1)} %filter.4), calls=%async_computation.2 | async-start | bytes 5963776 | tf_op jit(solution)/shard_map/all_to_all | solution.py:280
  91.3 4.8 %backward.3 = (bf16[4,46,16,128]{3,2,1,0:T(8,128)(2,1)S(1)}, bf16[4,46,16,128]{3,2,1,0:T(8,128)(2,1)S(1)}) custom-call(s32[8]{0:T(128)S(1)} %stack.80.tiles_ref, bf16[1024,1024]{1,0:T(8,128)(2,1)} %constant.68.clone.basis_ref, bf16[137,16,1024]{2,1,0:T(8,128)(2,1)} %bitcast.25, bf16[8,92,16,128]{3,2,1,0:T(8,128)(2,1)S(1)} %all-to-all-done.1.x_ref), custom_call_target="tpu_custom_call" | custom-call | flops 1543503872 | bytes 6619136 | tf_op jit(solution)/shard_map/backward/pallas_call | solution.py:191
  96.1 2.7 %collective-permute-start = (bf16[4,46,16,128]{3,2,1,0:T(8,128)(2,1)S(1)}, bf16[4,46,16,128]{3,2,1,0:T(8,128)(2,1)S(1)}, u32[]{:S(2)}, u32[]{:S(2)}) collective-permute-start(bf16[4,46,16,128]{3,2,1,0:T(8,128)(2,1)S(1)} %get-tuple-element.52), channel_id=1, source_target_pairs={{0,8},{8,0},{16,24},{24,16},{32,40},{40,32},{48,56},{56,48},{64,72... | collective-permute-start | bytes 2261000 | tf_op jit(solution)/shard_map/ppermute | solution.py:319
  98.8 1.9 collective-permute-done.b_ref
  101.0 1.4 collective-permute-start.1
  102.4 2.6 %collective-permute-start.2 = (bf16[46,16,128]{2,1,0:T(8,128)(2,1)S(1)}, bf16[46,16,128]{2,1,0:T(8,128)(2,1)S(1)}, u32[]{:S(2)}, u32[]{:S(2)}) collective-permute-start(bf16[46,16,128]{2,1,0:T(8,128)(2,1)S(1)} %get-tuple-element.55), channel_id=1, source_target_pairs={{0,64},{8,72},{16,80},{24,88},{32,96},{40,104},{48,112},{56,120},{... | collective-permute-start | bytes 565256 | tf_op jit(solution)/shard_map/ppermute | solution.py:322
  105.0 1.1 collective-permute-start.3
  106.1 2.4 %collective-permute-done.1 = bf16[46,16,128]{2,1,0:T(8,128)(2,1)S(1)} collective-permute-done((bf16[46,16,128]{2,1,0:T(8,128)(2,1)S(1)}, bf16[46,16,128]{2,1,0:T(8,128)(2,1)S(1)}, u32[]{:S(2)}, u32[]{:S(2)}) %collective-permute-start.1) | collective-permute-done | bytes 188448 | tf_op jit(solution)/shard_map/ppermute | solution.py:322
  108.5 5.1 %collective-permute-done.2 = bf16[46,16,128]{2,1,0:T(8,128)(2,1)S(1)} collective-permute-done((bf16[46,16,128]{2,1,0:T(8,128)(2,1)S(1)}, bf16[46,16,128]{2,1,0:T(8,128)(2,1)S(1)}, u32[]{:S(2)}, u32[]{:S(2)}) %collective-permute-start.2) | collective-permute-done | bytes 188448 | tf_op jit(solution)/shard_map/ppermute | solution.py:322
  114.1 12.3 %collective-permute-done.4 = bf16[46,16,128]{2,1,0:T(8,128)(2,1)S(1)} collective-permute-done((bf16[46,16,128]{2,1,0:T(8,128)(2,1)S(1)}, bf16[46,16,128]{2,1,0:T(8,128)(2,1)S(1)}, u32[]{:S(2)}, u32[]{:S(2)}) %collective-permute-start.4) | collective-permute-done | bytes 188448 | tf_op jit(solution)/shard_map/ppermute | solution.py:325
  126.9 3.1 %filter.5 = bf16[8,45,16,128]{3,2,1,0:T(8,128)(2,1)} custom-call(bf16[128,128]{1,0:T(8,128)(2,1)S(1)} %copy.15.basis_ref, bf16[128,128]{1,0:T(8,128)(2,1)S(1)} %convolution_convert_fusion.basis_t_ref, f32[128,128]{1,0:T(8,128)S(1)} %copy-done.2, bf16[8,91,16,128]{3,2,1,0:T(8,128)(2,1)} %all-to-all-done.2.x_ref), custom_call_target="tpu_custom_call" | custom-call | flops 377487360 | bytes 2949120 | tf_op jit(solution)/shard_map/filter/pallas_call | solution.py:157
  130.0 6.9 %all-to-all-start.3 = ((bf16[8,45,16,128]{3,2,1,0:T(8,128)(2,1)}), bf16[8,45,16,128]{3,2,1,0:T(8,128)(2,1)S(1)}, u32[]{:S(2)}, u32[]{:S(2)}) async-start(bf16[8,45,16,128]{3,2,1,0:T(8,128)(2,1)} %filter.5), calls=%async_computation.3 | async-start | bytes 2949120 | tf_op jit(solution)/shard_map/all_to_all | solution.py:280
  136.9 2.7 %collective-permute-start.6 = (bf16[46,16,128]{2,1,0:T(8,128)(2,1)S(1)}, bf16[46,16,128]{2,1,0:T(8,128)(2,1)S(1)}, u32[]{:S(2)}, u32[]{:S(2)}) collective-permute-start(bf16[46,16,128]{2,1,0:T(8,128)(2,1)S(1)} %add_convert_fusion.2), channel_id=1, source_target_pairs={{0,96},{8,104},{16,112},{24,120},{32,0},{40,8},{48,16},{56,24},{64... | collective-permute-start | bytes 565256 | tf_op jit(solution)/shard_map/ppermute | solution.py:328
  140.7 5.1 %backward.4 = (bf16[4,46,16,128]{3,2,1,0:T(8,128)(2,1)S(1)}, bf16[4,46,16,128]{3,2,1,0:T(8,128)(2,1)S(1)}) custom-call(s32[8]{0:T(128)S(1)} %stack.80.tiles_ref, bf16[1024,1024]{1,0:T(8,128)(2,1)} %constant.68.clone.basis_ref, bf16[137,16,1024]{2,1,0:T(8,128)(2,1)} %bitcast.26, bf16[8,91,16,128]{3,2,1,0:T(8,128)(2,1)} %all-to-all-done.2.x_ref), custom_call_target="tpu_custom_call" | custom-call | flops 1543503872 | bytes 6619136 | tf_op jit(solution)/shard_map/backward/pallas_call | solution.py:191
  145.8 4.7 %collective-permute-start.5 = (bf16[4,46,16,128]{3,2,1,0:T(8,128)(2,1)S(1)}, bf16[4,46,16,128]{3,2,1,0:T(8,128)(2,1)S(1)}, u32[]{:S(2)}, u32[]{:S(2)}) collective-permute-start(bf16[4,46,16,128]{3,2,1,0:T(8,128)(2,1)S(1)} %get-tuple-element.59), channel_id=1, source_target_pairs={{0,8},{8,0},{16,24},{24,16},{32,40},{40,32},{48,56},{56,48},{64,72... | collective-permute-start | bytes 2261000 | tf_op jit(solution)/shard_map/ppermute | solution.py:319
  150.6 2.6 %collective-permute-start.9 = (bf16[4,46,16,128]{3,2,1,0:T(8,128)(2,1)S(1)}, bf16[4,46,16,128]{3,2,1,0:T(8,128)(2,1)S(1)}, u32[]{:S(2)}, u32[]{:S(2)}) collective-permute-start(bf16[4,46,16,128]{3,2,1,0:T(8,128)(2,1)S(1)} %pad_maximum_fusion.mine_ref), channel_id=1, source_target_pairs={{0,8},{8,0},{16,24},{24,16},{32,40},{40,32},{48,56},{56,48},{64,72... | collective-permute-start | bytes 2261000 | tf_op jit(solution)/shard_map/ppermute | solution.py:332
  154.2 0.9 collective-permute-done.9.theirs_ref
  155.0 5.4 %backward.5 = (bf16[4,45,16,128]{3,2,1,0:T(8,128)(2,1)S(1)}, bf16[4,45,16,128]{3,2,1,0:T(8,128)(2,1)S(1)}) custom-call(s32[8]{0:T(128)S(1)} %stack.80.tiles_ref, bf16[1024,1024]{1,0:T(8,128)(2,1)} %constant.68.clone.basis_ref, bf16[137,16,1024]{2,1,0:T(8,128)(2,1)} %bitcast.27, bf16[8,45,16,128]{3,2,1,0:T(8,128)(2,1)S(1)} %all-to-all-done.3.x_ref), custom_call_target="tpu_custom_call" | custom-call | flops 1509949440 | bytes 6520832 | tf_op jit(solution)/shard_map/backward/pallas_call | solution.py:191
  160.4 4.7 %collective-permute-start.10 = (bf16[4,45,16,128]{3,2,1,0:T(8,128)(2,1)S(1)}, bf16[4,45,16,128]{3,2,1,0:T(8,128)(2,1)S(1)}, u32[]{:S(2)}, u32[]{:S(2)}) collective-permute-start(bf16[4,45,16,128]{3,2,1,0:T(8,128)(2,1)S(1)} %get-tuple-element.67), channel_id=1, source_target_pairs={{0,8},{8,0},{16,24},{24,16},{32,40},{40,32},{48,56},{56,48},{64,72... | collective-permute-start | bytes 2211848 | tf_op jit(solution)/shard_map/ppermute | solution.py:319
  165.2 1.3 collective-permute-start.19
  166.5 2.6 %collective-permute-start.20 = (bf16[46,16,128]{2,1,0:T(8,128)(2,1)S(1)}, bf16[46,16,128]{2,1,0:T(8,128)(2,1)S(1)}, u32[]{:S(2)}, u32[]{:S(2)}) collective-permute-start(bf16[46,16,128]{2,1,0:T(8,128)(2,1)S(1)} %get-tuple-element.80), channel_id=1, source_target_pairs={{0,64},{8,72},{16,80},{24,88},{32,96},{40,104},{48,112},{56,120},{... | collective-permute-start | bytes 565256 | tf_op jit(solution)/shard_map/ppermute | solution.py:322
  169.1 1.1 collective-permute-start.21
  170.2 2.0 pair_sum.5
  173.4 1.7 collective-permute-start.13
  175.1 2.8 %collective-permute-done.20 = bf16[46,16,128]{2,1,0:T(8,128)(2,1)S(1)} collective-permute-done((bf16[46,16,128]{2,1,0:T(8,128)(2,1)S(1)}, bf16[46,16,128]{2,1,0:T(8,128)(2,1)S(1)}, u32[]{:S(2)}, u32[]{:S(2)}) %collective-permute-start.20) | collective-permute-done | bytes 188448 | tf_op jit(solution)/shard_map/ppermute | solution.py:322
  178.2 4.4 %collective-permute-done.11 = bf16[45,16,128]{2,1,0:T(8,128)(2,1)S(1)} collective-permute-done((bf16[45,16,128]{2,1,0:T(8,128)(2,1)S(1)}, bf16[45,16,128]{2,1,0:T(8,128)(2,1)S(1)}, u32[]{:S(2)}, u32[]{:S(2)}) %collective-permute-start.11) | collective-permute-done | bytes 184352 | tf_op jit(solution)/shard_map/ppermute | solution.py:322
  182.6 3.3 %collective-permute-done.12 = bf16[45,16,128]{2,1,0:T(8,128)(2,1)S(1)} collective-permute-done((bf16[45,16,128]{2,1,0:T(8,128)(2,1)S(1)}, bf16[45,16,128]{2,1,0:T(8,128)(2,1)S(1)}, u32[]{:S(2)}, u32[]{:S(2)}) %collective-permute-start.12) | collective-permute-done | bytes 184352 | tf_op jit(solution)/shard_map/ppermute | solution.py:322
  186.1 2.2 %collective-permute-start.23 = (bf16[46,16,128]{2,1,0:T(8,128)(2,1)S(1)}, bf16[46,16,128]{2,1,0:T(8,128)(2,1)S(1)}, u32[]{:S(2)}, u32[]{:S(2)}) collective-permute-start(bf16[46,16,128]{2,1,0:T(8,128)(2,1)S(1)} %add_convert_fusion), channel_id=1, source_target_pairs={{0,96},{8,104},{16,112},{24,120},{32,0},{40,8},{48,16},{56,24},{64... | collective-permute-start | bytes 565256 | tf_op jit(solution)/shard_map/ppermute | solution.py:328
  189.1 2.3 %collective-permute-done.14 = bf16[45,16,128]{2,1,0:T(8,128)(2,1)S(1)} collective-permute-done((bf16[45,16,128]{2,1,0:T(8,128)(2,1)S(1)}, bf16[45,16,128]{2,1,0:T(8,128)(2,1)S(1)}, u32[]{:S(2)}, u32[]{:S(2)}) %collective-permute-start.14) | collective-permute-done | bytes 184352 | tf_op jit(solution)/shard_map/ppermute | solution.py:325
  191.4 2.6 %collective-permute-start.15 = (bf16[45,16,128]{2,1,0:T(8,128)(2,1)S(1)}, bf16[45,16,128]{2,1,0:T(8,128)(2,1)S(1)}, u32[]{:S(2)}, u32[]{:S(2)}) collective-permute-start(bf16[45,16,128]{2,1,0:T(8,128)(2,1)S(1)} %add_convert_fusion.4), channel_id=1, source_target_pairs={{0,96},{8,104},{16,112},{24,120},{32,0},{40,8},{48,16},{56,24},{64... | collective-permute-start | bytes 552968 | tf_op jit(solution)/shard_map/ppermute | solution.py:328
  194.7 2.0 place.3.refs_0_
  196.7 4.0 %collective-permute-done.25 = bf16[46,16,128]{2,1,0:T(8,128)(2,1)S(1)} collective-permute-done((bf16[46,16,128]{2,1,0:T(8,128)(2,1)S(1)}, bf16[46,16,128]{2,1,0:T(8,128)(2,1)S(1)}, u32[]{:S(2)}, u32[]{:S(2)}) %collective-permute-start.25) | collective-permute-done | bytes 188448 | tf_op jit(solution)/shard_map/ppermute | solution.py:328
  200.8 1.8 collective-permute-start.26
  203.3 4.5 %collective-permute-done.17 = bf16[45,16,128]{2,1,0:T(8,128)(2,1)S(1)} collective-permute-done((bf16[45,16,128]{2,1,0:T(8,128)(2,1)S(1)}, bf16[45,16,128]{2,1,0:T(8,128)(2,1)S(1)}, u32[]{:S(2)}, u32[]{:S(2)}) %collective-permute-start.17) | collective-permute-done | bytes 184352 | tf_op jit(solution)/shard_map/ppermute | solution.py:328
  207.9 0.9 collective-permute-start.18
  208.9 2.0 place.4.refs_0_
  210.9 2.5 %place.5 = bf16[137,16,1024]{2,1,0:T(8,128)(2,1)} custom-call(s32[8]{0:T(128)S(1)} %stack.80.tiles_ref, bf16[4,45,16,128]{3,2,1,0:T(8,128)(2,1)S(1)} %pad_maximum_fusion.2.mine_ref, bf16[4,45,16,128]{3,2,1,0:T(8,128)(2,1)S(1)} %collective-permute-done.18.theirs_ref, bf16[137,16,1024]{2,1,0:T(8,128)(2,1)} %place.4.refs_0_), custom_call_target="tpu_custom_call", output_to_operand_aliasing={{}: (3, {})} | custom-call | bytes 2949120 | tf_op jit(solution)/shard_map/place/pallas_call | solution.py:247
  (57 shorter events, 7.9 us)
Async XLA Ops:
  0.0 0.9 copy-start.3
  11.2 8.5 %copy-start.6 = (bf16[128,128]{1,0:T(8,128)(2,1)S(1)}, bf16[128,128]{1,0:T(8,128)(2,1)}, u32[]{:S(2)}) copy-start(bf16[128,128]{1,0:T(8,128)(2,1)} %constant.70.clone) | copy-start | bytes 98308
  11.2 8.5 %copy-start.7 = (s32[128]{0:T(128)S(1)}, s32[128]{0:T(128)}, u32[]{:S(2)}) copy-start(s32[128]{0:T(128)} %param.12) | copy-start | bytes 1540
  11.2 8.8 %copy-start = (bf16[1024,1024]{1,0:T(8,128)(2,1)S(1)}, bf16[1024,1024]{1,0:T(8,128)(2,1)}, u32[]{:S(2)}) copy-start(bf16[1024,1024]{1,0:T(8,128)(2,1)} %constant.69.clone.basis_ref) | copy-start | bytes 6291460
  11.2 29.8 %all-to-all-start = ((bf16[8,46,16,128]{3,2,1,0:T(8,128)(2,1)}), bf16[8,46,16,128]{3,2,1,0:T(8,128)(2,1)}, u32[]{:S(2)}, u32[]{:S(2)}) async-start(bf16[8,46,16,128]{3,2,1,0:T(8,128)(2,1)} %get-tuple-element.44), calls=%async_computation | async-start | bytes 3014656 | tf_op jit(solution)/shard_map/all_to_all | solution.py:280
  20.0 21.0 %copy-start.2 = (f32[128,128]{1,0:T(8,128)S(1)}, f32[128,128]{1,0:T(8,128)}, u32[]{:S(2)}) copy-start(f32[128,128]{1,0:T(8,128)} %weights_ref.5) | copy-start | bytes 196612
  44.1 40.5 %all-to-all-start.1 = ((bf16[8,92,16,128]{3,2,1,0:T(8,128)(2,1)}), bf16[8,92,16,128]{3,2,1,0:T(8,128)(2,1)S(1)}, u32[]{:S(2)}, u32[]{:S(2)}) async-start(bf16[8,92,16,128]{3,2,1,0:T(8,128)(2,1)} %filter.3), calls=%async_computation.1 | async-start | bytes 6029312 | tf_op jit(solution)/shard_map/all_to_all | solution.py:280
  47.9 1.6 copy-start.1
  86.7 40.2 %all-to-all-start.2 = ((bf16[8,91,16,128]{3,2,1,0:T(8,128)(2,1)}), bf16[8,91,16,128]{3,2,1,0:T(8,128)(2,1)}, u32[]{:S(2)}, u32[]{:S(2)}) async-start(bf16[8,91,16,128]{3,2,1,0:T(8,128)(2,1)} %filter.4), calls=%async_computation.2 | async-start | bytes 5963776 | tf_op jit(solution)/shard_map/all_to_all | solution.py:280
  96.1 4.5 %collective-permute-start = (bf16[4,46,16,128]{3,2,1,0:T(8,128)(2,1)S(1)}, bf16[4,46,16,128]{3,2,1,0:T(8,128)(2,1)S(1)}, u32[]{:S(2)}, u32[]{:S(2)}) collective-permute-start(bf16[4,46,16,128]{3,2,1,0:T(8,128)(2,1)S(1)} %get-tuple-element.52), channel_id=1, source_target_pairs={{0,8},{8,0},{16,24},{24,16},{32,40},{40,32},{48,56},{56,48},{64,72... | collective-permute-start | bytes 2261000 | tf_op jit(solution)/shard_map/ppermute | solution.py:319
  101.0 7.5 %collective-permute-start.1 = (bf16[46,16,128]{2,1,0:T(8,128)(2,1)S(1)}, bf16[46,16,128]{2,1,0:T(8,128)(2,1)S(1)}, u32[]{:S(2)}, u32[]{:S(2)}) collective-permute-start(bf16[46,16,128]{2,1,0:T(8,128)(2,1)S(1)} %get-tuple-element.54), channel_id=1, source_target_pairs={{0,32},{8,40},{16,48},{24,56},{32,64},{40,72},{48,80},{56,88},{64,... | collective-permute-start | bytes 565256 | tf_op jit(solution)/shard_map/ppermute | solution.py:322
  102.4 11.2 %collective-permute-start.2 = (bf16[46,16,128]{2,1,0:T(8,128)(2,1)S(1)}, bf16[46,16,128]{2,1,0:T(8,128)(2,1)S(1)}, u32[]{:S(2)}, u32[]{:S(2)}) collective-permute-start(bf16[46,16,128]{2,1,0:T(8,128)(2,1)S(1)} %get-tuple-element.55), channel_id=1, source_target_pairs={{0,64},{8,72},{16,80},{24,88},{32,96},{40,104},{48,112},{56,120},{... | collective-permute-start | bytes 565256 | tf_op jit(solution)/shard_map/ppermute | solution.py:322
  105.0 8.6 %collective-permute-start.3 = (bf16[46,16,128]{2,1,0:T(8,128)(2,1)S(1)}, bf16[46,16,128]{2,1,0:T(8,128)(2,1)S(1)}, u32[]{:S(2)}, u32[]{:S(2)}) collective-permute-start(bf16[46,16,128]{2,1,0:T(8,128)(2,1)S(1)} %get-tuple-element.56), channel_id=1, source_target_pairs={{0,96},{8,104},{16,112},{24,120},{32,0},{40,8},{48,16},{56,24},{64... | collective-permute-start | bytes 565256 | tf_op jit(solution)/shard_map/ppermute | solution.py:322
  113.7 12.7 %collective-permute-start.4 = (bf16[46,16,128]{2,1,0:T(8,128)(2,1)S(1)}, bf16[46,16,128]{2,1,0:T(8,128)(2,1)S(1)}, u32[]{:S(2)}, u32[]{:S(2)}) collective-permute-start(bf16[46,16,128]{2,1,0:T(8,128)(2,1)S(1)} %add_convert_fusion.3), channel_id=1, source_target_pairs={{0,16},{8,24},{16,0},{24,8},{32,48},{40,56},{48,32},{56,40},{64,80... | collective-permute-start | bytes 565256 | tf_op jit(solution)/shard_map/ppermute | solution.py:325
  130.0 25.1 %all-to-all-start.3 = ((bf16[8,45,16,128]{3,2,1,0:T(8,128)(2,1)}), bf16[8,45,16,128]{3,2,1,0:T(8,128)(2,1)S(1)}, u32[]{:S(2)}, u32[]{:S(2)}) async-start(bf16[8,45,16,128]{3,2,1,0:T(8,128)(2,1)} %filter.5), calls=%async_computation.3 | async-start | bytes 2949120 | tf_op jit(solution)/shard_map/all_to_all | solution.py:280
  136.9 13.6 %collective-permute-start.6 = (bf16[46,16,128]{2,1,0:T(8,128)(2,1)S(1)}, bf16[46,16,128]{2,1,0:T(8,128)(2,1)S(1)}, u32[]{:S(2)}, u32[]{:S(2)}) collective-permute-start(bf16[46,16,128]{2,1,0:T(8,128)(2,1)S(1)} %add_convert_fusion.2), channel_id=1, source_target_pairs={{0,96},{8,104},{16,112},{24,120},{32,0},{40,8},{48,16},{56,24},{64... | collective-permute-start | bytes 565256 | tf_op jit(solution)/shard_map/ppermute | solution.py:328
  139.6 10.8 %collective-permute-start.7 = (bf16[46,16,128]{2,1,0:T(8,128)(2,1)S(1)}, bf16[46,16,128]{2,1,0:T(8,128)(2,1)S(1)}, u32[]{:S(2)}, u32[]{:S(2)}) collective-permute-start(bf16[46,16,128]{2,1,0:T(8,128)(2,1)S(1)} %add_convert_fusion.2), channel_id=1, source_target_pairs={{0,64},{8,72},{16,80},{24,88},{32,96},{40,104},{48,112},{56,120},{... | collective-permute-start | bytes 565256 | tf_op jit(solution)/shard_map/ppermute | solution.py:328
  140.0 10.5 %collective-permute-start.8 = (bf16[46,16,128]{2,1,0:T(8,128)(2,1)S(1)}, bf16[46,16,128]{2,1,0:T(8,128)(2,1)S(1)}, u32[]{:S(2)}, u32[]{:S(2)}) collective-permute-start(bf16[46,16,128]{2,1,0:T(8,128)(2,1)S(1)} %add_convert_fusion.2), channel_id=1, source_target_pairs={{0,32},{8,40},{16,48},{24,56},{32,64},{40,72},{48,80},{56,88},{64,... | collective-permute-start | bytes 565256 | tf_op jit(solution)/shard_map/ppermute | solution.py:328
  145.8 7.4 %collective-permute-start.5 = (bf16[4,46,16,128]{3,2,1,0:T(8,128)(2,1)S(1)}, bf16[4,46,16,128]{3,2,1,0:T(8,128)(2,1)S(1)}, u32[]{:S(2)}, u32[]{:S(2)}) collective-permute-start(bf16[4,46,16,128]{3,2,1,0:T(8,128)(2,1)S(1)} %get-tuple-element.59), channel_id=1, source_target_pairs={{0,8},{8,0},{16,24},{24,16},{32,40},{40,32},{48,56},{56,48},{64,72... | collective-permute-start | bytes 2261000 | tf_op jit(solution)/shard_map/ppermute | solution.py:319
  150.6 4.5 %collective-permute-start.9 = (bf16[4,46,16,128]{3,2,1,0:T(8,128)(2,1)S(1)}, bf16[4,46,16,128]{3,2,1,0:T(8,128)(2,1)S(1)}, u32[]{:S(2)}, u32[]{:S(2)}) collective-permute-start(bf16[4,46,16,128]{3,2,1,0:T(8,128)(2,1)S(1)} %pad_maximum_fusion.mine_ref), channel_id=1, source_target_pairs={{0,8},{8,0},{16,24},{24,16},{32,40},{40,32},{48,56},{56,48},{64,72... | collective-permute-start | bytes 2261000 | tf_op jit(solution)/shard_map/ppermute | solution.py:332
  153.5 0.7 copy-start.4
  155.0 10.1 %copy-start.5 = (bf16[46,16,128]{2,1,0:T(8,128)(2,1)S(1)}, bf16[46,16,128]{2,1,0:T(8,128)(2,1)}, u32[]{:S(2)}) copy-start(bf16[46,16,128]{2,1,0:T(8,128)(2,1)} %copy-done.4) | copy-start | bytes 565252
  160.4 9.7 %collective-permute-start.10 = (bf16[4,45,16,128]{3,2,1,0:T(8,128)(2,1)S(1)}, bf16[4,45,16,128]{3,2,1,0:T(8,128)(2,1)S(1)}, u32[]{:S(2)}, u32[]{:S(2)}) collective-permute-start(bf16[4,45,16,128]{3,2,1,0:T(8,128)(2,1)S(1)} %get-tuple-element.67), channel_id=1, source_target_pairs={{0,8},{8,0},{16,24},{24,16},{32,40},{40,32},{48,56},{56,48},{64,72... | collective-permute-start | bytes 2211848 | tf_op jit(solution)/shard_map/ppermute | solution.py:319
  165.2 8.3 %collective-permute-start.19 = (bf16[46,16,128]{2,1,0:T(8,128)(2,1)S(1)}, bf16[46,16,128]{2,1,0:T(8,128)(2,1)S(1)}, u32[]{:S(2)}, u32[]{:S(2)}) collective-permute-start(bf16[46,16,128]{2,1,0:T(8,128)(2,1)S(1)} %copy-done.5), channel_id=1, source_target_pairs={{0,32},{8,40},{16,48},{24,56},{32,64},{40,72},{48,80},{56,88},{64,... | collective-permute-start | bytes 565256 | tf_op jit(solution)/shard_map/ppermute | solution.py:322
  166.5 11.5 %collective-permute-start.20 = (bf16[46,16,128]{2,1,0:T(8,128)(2,1)S(1)}, bf16[46,16,128]{2,1,0:T(8,128)(2,1)S(1)}, u32[]{:S(2)}, u32[]{:S(2)}) collective-permute-start(bf16[46,16,128]{2,1,0:T(8,128)(2,1)S(1)} %get-tuple-element.80), channel_id=1, source_target_pairs={{0,64},{8,72},{16,80},{24,88},{32,96},{40,104},{48,112},{56,120},{... | collective-permute-start | bytes 565256 | tf_op jit(solution)/shard_map/ppermute | solution.py:322
  169.1 8.9 %collective-permute-start.21 = (bf16[46,16,128]{2,1,0:T(8,128)(2,1)S(1)}, bf16[46,16,128]{2,1,0:T(8,128)(2,1)S(1)}, u32[]{:S(2)}, u32[]{:S(2)}) collective-permute-start(bf16[46,16,128]{2,1,0:T(8,128)(2,1)S(1)} %get-tuple-element.81), channel_id=1, source_target_pairs={{0,96},{8,104},{16,112},{24,120},{32,0},{40,8},{48,16},{56,24},{64... | collective-permute-start | bytes 565256 | tf_op jit(solution)/shard_map/ppermute | solution.py:322
  172.2 10.4 %collective-permute-start.11 = (bf16[45,16,128]{2,1,0:T(8,128)(2,1)S(1)}, bf16[45,16,128]{2,1,0:T(8,128)(2,1)S(1)}, u32[]{:S(2)}, u32[]{:S(2)}) collective-permute-start(bf16[45,16,128]{2,1,0:T(8,128)(2,1)S(1)} %get-tuple-element.69), channel_id=1, source_target_pairs={{0,32},{8,40},{16,48},{24,56},{32,64},{40,72},{48,80},{56,88},{64,... | collective-permute-start | bytes 552968 | tf_op jit(solution)/shard_map/ppermute | solution.py:322
  172.6 13.2 %collective-permute-start.12 = (bf16[45,16,128]{2,1,0:T(8,128)(2,1)S(1)}, bf16[45,16,128]{2,1,0:T(8,128)(2,1)S(1)}, u32[]{:S(2)}, u32[]{:S(2)}) collective-permute-start(bf16[45,16,128]{2,1,0:T(8,128)(2,1)S(1)} %get-tuple-element.70), channel_id=1, source_target_pairs={{0,64},{8,72},{16,80},{24,88},{32,96},{40,104},{48,112},{56,120},{... | collective-permute-start | bytes 552968 | tf_op jit(solution)/shard_map/ppermute | solution.py:322
  173.4 12.4 %collective-permute-start.13 = (bf16[45,16,128]{2,1,0:T(8,128)(2,1)S(1)}, bf16[45,16,128]{2,1,0:T(8,128)(2,1)S(1)}, u32[]{:S(2)}, u32[]{:S(2)}) collective-permute-start(bf16[45,16,128]{2,1,0:T(8,128)(2,1)S(1)} %get-tuple-element.71), channel_id=1, source_target_pairs={{0,96},{8,104},{16,112},{24,120},{32,0},{40,8},{48,16},{56,24},{64... | collective-permute-start | bytes 552968 | tf_op jit(solution)/shard_map/ppermute | solution.py:322
  178.1 8.0 %collective-permute-start.22 = (bf16[46,16,128]{2,1,0:T(8,128)(2,1)S(1)}, bf16[46,16,128]{2,1,0:T(8,128)(2,1)S(1)}, u32[]{:S(2)}, u32[]{:S(2)}) collective-permute-start(bf16[46,16,128]{2,1,0:T(8,128)(2,1)S(1)} %add_convert_fusion.1), channel_id=1, source_target_pairs={{0,16},{8,24},{16,0},{24,8},{32,48},{40,56},{48,32},{56,40},{64,80... | collective-permute-start | bytes 565256 | tf_op jit(solution)/shard_map/ppermute | solution.py:325
  186.0 5.4 %collective-permute-start.14 = (bf16[45,16,128]{2,1,0:T(8,128)(2,1)S(1)}, bf16[45,16,128]{2,1,0:T(8,128)(2,1)S(1)}, u32[]{:S(2)}, u32[]{:S(2)}) collective-permute-start(bf16[45,16,128]{2,1,0:T(8,128)(2,1)S(1)} %add_convert_fusion.5), channel_id=1, source_target_pairs={{0,16},{8,24},{16,0},{24,8},{32,48},{40,56},{48,32},{56,40},{64,80... | collective-permute-start | bytes 552968 | tf_op jit(solution)/shard_map/ppermute | solution.py:325
  186.1 7.9 %collective-permute-start.23 = (bf16[46,16,128]{2,1,0:T(8,128)(2,1)S(1)}, bf16[46,16,128]{2,1,0:T(8,128)(2,1)S(1)}, u32[]{:S(2)}, u32[]{:S(2)}) collective-permute-start(bf16[46,16,128]{2,1,0:T(8,128)(2,1)S(1)} %add_convert_fusion), channel_id=1, source_target_pairs={{0,96},{8,104},{16,112},{24,120},{32,0},{40,8},{48,16},{56,24},{64... | collective-permute-start | bytes 565256 | tf_op jit(solution)/shard_map/ppermute | solution.py:328
  188.3 8.4 %collective-permute-start.24 = (bf16[46,16,128]{2,1,0:T(8,128)(2,1)S(1)}, bf16[46,16,128]{2,1,0:T(8,128)(2,1)S(1)}, u32[]{:S(2)}, u32[]{:S(2)}) collective-permute-start(bf16[46,16,128]{2,1,0:T(8,128)(2,1)S(1)} %add_convert_fusion), channel_id=1, source_target_pairs={{0,64},{8,72},{16,80},{24,88},{32,96},{40,104},{48,112},{56,120},{... | collective-permute-start | bytes 565256 | tf_op jit(solution)/shard_map/ppermute | solution.py:328
  188.4 12.3 %collective-permute-start.25 = (bf16[46,16,128]{2,1,0:T(8,128)(2,1)S(1)}, bf16[46,16,128]{2,1,0:T(8,128)(2,1)S(1)}, u32[]{:S(2)}, u32[]{:S(2)}) collective-permute-start(bf16[46,16,128]{2,1,0:T(8,128)(2,1)S(1)} %add_convert_fusion), channel_id=1, source_target_pairs={{0,32},{8,40},{16,48},{24,56},{32,64},{40,72},{48,80},{56,88},{64,... | collective-permute-start | bytes 565256 | tf_op jit(solution)/shard_map/ppermute | solution.py:328
  191.4 11.2 %collective-permute-start.15 = (bf16[45,16,128]{2,1,0:T(8,128)(2,1)S(1)}, bf16[45,16,128]{2,1,0:T(8,128)(2,1)S(1)}, u32[]{:S(2)}, u32[]{:S(2)}) collective-permute-start(bf16[45,16,128]{2,1,0:T(8,128)(2,1)S(1)} %add_convert_fusion.4), channel_id=1, source_target_pairs={{0,96},{8,104},{16,112},{24,120},{32,0},{40,8},{48,16},{56,24},{64... | collective-permute-start | bytes 552968 | tf_op jit(solution)/shard_map/ppermute | solution.py:328
  194.0 9.3 %collective-permute-start.16 = (bf16[45,16,128]{2,1,0:T(8,128)(2,1)S(1)}, bf16[45,16,128]{2,1,0:T(8,128)(2,1)S(1)}, u32[]{:S(2)}, u32[]{:S(2)}) collective-permute-start(bf16[45,16,128]{2,1,0:T(8,128)(2,1)S(1)} %add_convert_fusion.4), channel_id=1, source_target_pairs={{0,64},{8,72},{16,80},{24,88},{32,96},{40,104},{48,112},{56,120},{... | collective-permute-start | bytes 552968 | tf_op jit(solution)/shard_map/ppermute | solution.py:328
  194.0 13.8 %collective-permute-start.17 = (bf16[45,16,128]{2,1,0:T(8,128)(2,1)S(1)}, bf16[45,16,128]{2,1,0:T(8,128)(2,1)S(1)}, u32[]{:S(2)}, u32[]{:S(2)}) collective-permute-start(bf16[45,16,128]{2,1,0:T(8,128)(2,1)S(1)} %add_convert_fusion.4), channel_id=1, source_target_pairs={{0,32},{8,40},{16,48},{24,56},{32,64},{40,72},{48,80},{56,88},{64,... | collective-permute-start | bytes 552968 | tf_op jit(solution)/shard_map/ppermute | solution.py:328
  200.8 8.0 %collective-permute-start.26 = (bf16[4,46,16,128]{3,2,1,0:T(8,128)(2,1)S(1)}, bf16[4,46,16,128]{3,2,1,0:T(8,128)(2,1)S(1)}, u32[]{:S(2)}, u32[]{:S(2)}) collective-permute-start(bf16[4,46,16,128]{3,2,1,0:T(8,128)(2,1)S(1)} %pad_maximum_fusion.1.mine_ref), channel_id=1, source_target_pairs={{0,8},{8,0},{16,24},{24,16},{32,40},{40,32},{48,56},{56,48},{64,72... | collective-permute-start | bytes 2261000 | tf_op jit(solution)/shard_map/ppermute | solution.py:332
  207.9 2.9 %collective-permute-start.18 = (bf16[4,45,16,128]{3,2,1,0:T(8,128)(2,1)S(1)}, bf16[4,45,16,128]{3,2,1,0:T(8,128)(2,1)S(1)}, u32[]{:S(2)}, u32[]{:S(2)}) collective-permute-start(bf16[4,45,16,128]{3,2,1,0:T(8,128)(2,1)S(1)} %pad_maximum_fusion.2.mine_ref), channel_id=1, source_target_pairs={{0,8},{8,0},{16,24},{24,16},{32,40},{40,32},{48,56},{56,48},{64,72... | collective-permute-start | bytes 2211848 | tf_op jit(solution)/shard_map/ppermute | solution.py:332
